TPU v7x, 32 devices: a whole 2x2x4 slice. The times are simulated.
32 devices in a mesh: dp: 4 (over y, x), blk: 8 (over z, core).
Axes of the slice: x: 2, y: 2, z: 4, core: 2. Of those that a mesh axis runs over, the one named last changes fastest.
Arguments:
- frames: bfloat16 [8192, 1024], P(('dp', 'blk')), may hold values from -6 to 6
- skip_feats: bfloat16 [8192, 1024], P(('dp', 'blk')), may hold values from -6 to 6
- w_skip: bfloat16 [2048, 1024], replicated, may hold values from -0.125 to 0.125
- gain_attn: float32 [1024], replicated, may hold values from 0.1 to 1.9
- w_query: bfloat16 [1024, 1024], replicated, may hold values from -0.1875 to 0.1875
- w_key: bfloat16 [1024, 1024], replicated, may hold values from -0.1875 to 0.1875
- w_value: bfloat16 [1024, 1024], replicated, may hold values from -0.1875 to 0.1875
- w_output: bfloat16 [1024, 1024], replicated, may hold values from -0.75 to 0.75
- gain_ffn: float32 [1024], replicated, may hold values from 0.1 to 1.9
- w_up: bfloat16 [1024, 4096], replicated, may hold values from -0.1875 to 0.1875
- w_down: bfloat16 [4096, 1024], replicated, may hold values from -0.09375 to 0.09375
- cotangent: bfloat16 [8192, 1024], P(('dp', 'blk')), may hold values from -6 to 6
- utt_lengths: int32 [4, 4], P('dp'), may hold values from 1 to 2045, as said below
- padded_lengths: int32 [4, 4], P('dp'), may hold values from 1 to 2045, as said below
Outputs:
- mixed: bfloat16 [8192, 1024], P(('dp', 'blk'))
- grad_frames: bfloat16 [8192, 1024], P(('dp', 'blk'))
- grad_skip: bfloat16 [8192, 1024], P(('dp', 'blk'))
- grad_w_skip: float32 [2048, 1024], P(None, 'dp')
- grad_gain_attn: float32 [1024], P('dp')
- grad_w_query: float32 [1024, 1024], P(None, 'dp')
- grad_w_key: float32 [1024, 1024], P(None, 'dp')
- grad_w_value: float32 [1024, 1024], P(None, 'dp')
- grad_w_output: float32 [1024, 1024], P(None, 'dp')
- grad_gain_ffn: float32 [1024], P('dp')
- grad_w_up: float32 [1024, 4096], P(None, 'dp')
- grad_w_down: float32 [4096, 1024], P(None, 'dp')
Inputs may be any that keep to these rules, and one draw needn't show every extreme that they name: `utt_lengths`: each utterance has from 1 to its padded length of live frames; in every group one utterance, which one varies, covers the first frame block and the last one of the group. `padded_lengths`: A group's 4 padded lengths add up to 2048.
All inputs are finite; a program needn't handle non-finite values.
Results may differ from a plain program's by a relative error of at most 0.022.
Values may be sent and summed in bfloat16 or wider, within the bound.
No kernel may reach another device: no remote copies, remote signals or barrier semaphores. Data moves between devices by JAX's collectives and lax.ppermute only.
A program may use at most 192 MiB of HBM per device.

v0:
```python
from functools import partial
import math

import jax
import jax.numpy as jnp
from jax import lax
from jax.sharding import PartitionSpec as P

HEADS = 16
HEAD_DIM = 64


NEG_FILL = -1e30
NORM_EPS = 1e-05


def shifted(array, axis, by):
    size = lax.axis_size(axis)
    return lax.ppermute(array, axis, [(i, (i + by) % size) for i in range(size)])


def layer_norm(values, gain_vec):
    centred = values - jnp.mean(values, axis=-1, keepdims=True)
    variance = jnp.mean(centred * centred, axis=-1, keepdims=True)
    return centred * lax.rsqrt(variance + NORM_EPS) * gain_vec


def alibi_slopes(seq_len):
    head_rank = jnp.arange(1, HEADS + 1, dtype=jnp.float32)
    return jnp.exp2(-8.0 * head_rank / HEADS) * (256.0 / seq_len)


def utterance_tables(lengths, padded, positions):
    starts = jnp.cumsum(padded) - padded
    utt_owner = jnp.sum((positions[:, None] >= starts[None, :]).astype(jnp.int32), axis=1) - 1
    is_member = utt_owner[:, None] == jnp.arange(lengths.shape[0], dtype=jnp.int32)[None, :]
    offset_in = positions - jnp.sum(jnp.where(is_member, starts[None, :], 0), axis=1)
    is_live = offset_in < jnp.sum(jnp.where(is_member, lengths[None, :], 0), axis=1)
    return (utt_owner, is_live)


def product(form, left, right):
    return jnp.einsum(form, left, right, preferred_element_type=jnp.float32)


def on_device(
    frames,
    skip_feats,
    w_skip,
    gain_attn,
    w_query,
    w_key,
    w_value,
    w_output,
    gain_ffn,
    w_up,
    w_down,
    cotangent,
    utt_lengths,
    padded_lengths,
):
    row_count = frames.shape[0]
    blocks = lax.axis_size("blk")
    seq_len = row_count * blocks
    inv_root = 1.0 / math.sqrt(HEAD_DIM)
    lengths = utt_lengths[0]
    padded = padded_lengths[0]
    my_block = lax.axis_index("blk")
    row_pos = my_block * row_count + jnp.arange(row_count, dtype=jnp.int32)
    row_owner, row_live = utterance_tables(lengths, padded, row_pos)
    slopes = alibi_slopes(seq_len)
    joined = jnp.concatenate([frames, skip_feats], axis=1)
    hidden = product("rc,cd->rd", joined, w_skip)
    normed = layer_norm(hidden, gain_attn).astype(jnp.bfloat16)
    queries = (
        product("rd,de->re", normed, w_query)
        .astype(jnp.bfloat16)
        .reshape(row_count, HEADS, HEAD_DIM)
    )
    key_rows = (
        product("rd,de->re", normed, w_key).astype(jnp.bfloat16).reshape(row_count, HEADS, HEAD_DIM)
    )
    value_rows = (
        product("rd,de->re", normed, w_value)
        .astype(jnp.bfloat16)
        .reshape(row_count, HEADS, HEAD_DIM)
    )

    def score_block(keys_part, key_start):
        key_count = keys_part.shape[0]
        key_pos = key_start + jnp.arange(key_count, dtype=jnp.int32)
        key_owner, key_live = utterance_tables(lengths, padded, key_pos)
        allowed = (row_owner[:, None] == key_owner[None, :]) & key_live[None, :]
        distance = jnp.abs(row_pos[:, None] - key_pos[None, :]).astype(jnp.float32)
        scores = (
            product("qhd,khd->hqk", queries, keys_part) * inv_root
            - slopes[:, None, None] * distance[None]
        )
        return (scores, allowed)

    start_state = (
        jnp.full((HEADS, row_count), NEG_FILL, jnp.float32),
        jnp.zeros((HEADS, row_count), jnp.float32),
        jnp.zeros((row_count, HEADS, HEAD_DIM), jnp.float32),
    )
    pieces = (
        lax.all_gather(key_rows, "blk", axis=0, tiled=True),
        lax.all_gather(value_rows, "blk", axis=0, tiled=True),
    )
    key_count = pieces[0].shape[0]
    step_rows = math.gcd(key_count, 512)

    def one_block(block_index, state_now):
        running_max, running_sum, accumulated = state_now
        offset_rows = block_index * step_rows
        keys_part = lax.dynamic_slice_in_dim(pieces[0], offset_rows, step_rows, 0)
        vals_part = lax.dynamic_slice_in_dim(pieces[1], offset_rows, step_rows, 0)
        scores, allowed = score_block(keys_part, offset_rows)
        masked = jnp.where(allowed[None], scores, NEG_FILL)
        new_max = jnp.maximum(running_max, jnp.max(masked, axis=-1))
        exp_scores = jnp.where(allowed[None], jnp.exp(masked - new_max[:, :, None]), 0.0)
        rescale = jnp.exp(running_max - new_max)
        running_sum = running_sum * rescale + jnp.sum(exp_scores, axis=-1)
        accumulated = accumulated * rescale.T[:, :, None] + product(
            "hqk,khd->qhd", exp_scores.astype(jnp.bfloat16), vals_part
        )
        return (new_max, running_sum, accumulated)

    running_max, running_sum, accumulated = lax.fori_loop(
        0, key_count // step_rows, one_block, start_state
    )
    attn_full = accumulated / running_sum.T[:, :, None]
    log_total = running_max + jnp.log(running_sum)
    attn = attn_full.reshape(row_count, HEADS * HEAD_DIM).astype(jnp.bfloat16)
    residual = hidden + product("rd,de->re", attn, w_output)
    normed_ffn = layer_norm(residual, gain_ffn).astype(jnp.bfloat16)
    pre_act = product("rd,df->rf", normed_ffn, w_up)
    activ = jax.nn.gelu(pre_act, approximate=False).astype(jnp.bfloat16)
    mixed = (residual + product("rf,fd->rd", activ, w_down)).astype(jnp.bfloat16)
    grad_w_down = product("rf,rd->fd", activ, cotangent)
    grad_activ = product("rd,fd->rf", cotangent, w_down)
    gelu_out, gelu_pull = jax.vjp(partial(jax.nn.gelu, approximate=False), pre_act)
    grad_pre = gelu_pull(grad_activ)[0].astype(jnp.bfloat16)
    grad_w_up = product("rd,rf->df", normed_ffn, grad_pre)
    grad_normed_ffn = product("rf,df->rd", grad_pre, w_up)
    norm_out, norm_pull = jax.vjp(layer_norm, residual, gain_ffn)
    grad_resid_rows, grad_gain_ffn = norm_pull(grad_normed_ffn)
    grad_residual = cotangent.astype(jnp.float32) + grad_resid_rows
    grad_branch = grad_residual.astype(jnp.bfloat16)
    grad_w_output = product("rd,re->de", attn, grad_branch)
    grad_attn = (
        product("re,de->rd", grad_branch, w_output)
        .astype(jnp.bfloat16)
        .reshape(row_count, HEADS, HEAD_DIM)
    )
    delta = jnp.sum(grad_attn.astype(jnp.float32) * attn_full, axis=-1).T

    def back_turn(turn_index, state_now):
        keys_now, vals_now, grad_keys, grad_vals, grad_queries = state_now
        source = (my_block - turn_index) % blocks
        scores, allowed = score_block(keys_now, source * row_count)
        probs = jnp.where(allowed[None], jnp.exp(scores - log_total[:, :, None]), 0.0)
        grad_vals = grad_vals + product("hqk,qhd->khd", probs.astype(jnp.bfloat16), grad_attn)
        grad_probs = product("qhd,khd->hqk", grad_attn, vals_now)
        grad_scores = (probs * (grad_probs - delta[:, :, None])).astype(jnp.bfloat16)
        grad_queries = grad_queries + product("hqk,khd->qhd", grad_scores, keys_now) * inv_root
        grad_keys = grad_keys + product("hqk,qhd->khd", grad_scores, queries) * inv_root
        keys_now, vals_now = shifted((keys_now, vals_now), "blk", 1)
        grad_keys, grad_vals = (
            shifted(grad_keys.astype(jnp.bfloat16), "blk", 1).astype(grad_keys.dtype),
            shifted(grad_vals.astype(jnp.bfloat16), "blk", 1).astype(grad_vals.dtype),
        )
        return (keys_now, vals_now, grad_keys, grad_vals, grad_queries)

    zero_heads = jnp.zeros((row_count, HEADS, HEAD_DIM), jnp.float32)
    cycle_state = lax.fori_loop(
        0, blocks, back_turn, (key_rows, value_rows, zero_heads, zero_heads, zero_heads)
    )
    grad_keys_low = cycle_state[2].reshape(row_count, HEADS * HEAD_DIM).astype(jnp.bfloat16)
    grad_vals_low = cycle_state[3].reshape(row_count, HEADS * HEAD_DIM).astype(jnp.bfloat16)
    grad_query_low = cycle_state[4].reshape(row_count, HEADS * HEAD_DIM).astype(jnp.bfloat16)
    grad_w_query = product("rd,re->de", normed, grad_query_low)
    grad_w_key = product("rd,re->de", normed, grad_keys_low)
    grad_w_value = product("rd,re->de", normed, grad_vals_low)
    grad_normed = (
        product("re,de->rd", grad_query_low, w_query)
        + product("re,de->rd", grad_keys_low, w_key)
        + product("re,de->rd", grad_vals_low, w_value)
    )
    norm_first, first_pull = jax.vjp(layer_norm, hidden, gain_attn)
    grad_hidden_rows, grad_gain_attn = first_pull(grad_normed)
    grad_hidden = (grad_residual + grad_hidden_rows).astype(jnp.bfloat16)
    grad_w_skip = product("rc,rd->cd", joined, grad_hidden)
    grad_joined = product("rd,cd->rc", grad_hidden, w_skip)
    model_width = frames.shape[1]
    grad_frames = grad_joined[:, :model_width].astype(jnp.bfloat16)
    grad_skip = grad_joined[:, model_width:].astype(jnp.bfloat16)
    shares = (
        lax.psum_scatter(
            grad_w_skip.astype(jnp.bfloat16), "dp", scatter_dimension=1, tiled=True
        ).astype(jnp.float32),
        lax.psum_scatter(
            grad_w_query.astype(jnp.bfloat16), "dp", scatter_dimension=1, tiled=True
        ).astype(jnp.float32),
        lax.psum_scatter(
            grad_w_key.astype(jnp.bfloat16), "dp", scatter_dimension=1, tiled=True
        ).astype(jnp.float32),
        lax.psum_scatter(
            grad_w_value.astype(jnp.bfloat16), "dp", scatter_dimension=1, tiled=True
        ).astype(jnp.float32),
        lax.psum_scatter(
            grad_w_output.astype(jnp.bfloat16), "dp", scatter_dimension=1, tiled=True
        ).astype(jnp.float32),
        lax.psum_scatter(
            grad_w_up.astype(jnp.bfloat16), "dp", scatter_dimension=1, tiled=True
        ).astype(jnp.float32),
        lax.psum_scatter(
            grad_w_down.astype(jnp.bfloat16), "dp", scatter_dimension=1, tiled=True
        ).astype(jnp.float32),
        lax.psum_scatter(
            grad_gain_attn.astype(jnp.bfloat16), "dp", scatter_dimension=0, tiled=True
        ).astype(jnp.float32),
        lax.psum_scatter(
            grad_gain_ffn.astype(jnp.bfloat16), "dp", scatter_dimension=0, tiled=True
        ).astype(jnp.float32),
    )
    totals = (
        lax.psum(shares[0].astype(jnp.bfloat16), "blk").astype(jnp.float32),
        lax.psum(shares[1].astype(jnp.bfloat16), "blk").astype(jnp.float32),
        lax.psum(shares[2].astype(jnp.bfloat16), "blk").astype(jnp.float32),
        lax.psum(shares[3].astype(jnp.bfloat16), "blk").astype(jnp.float32),
        lax.psum(shares[4].astype(jnp.bfloat16), "blk").astype(jnp.float32),
        lax.psum(shares[5].astype(jnp.bfloat16), "blk").astype(jnp.float32),
        lax.psum(shares[6].astype(jnp.bfloat16), "blk").astype(jnp.float32),
        lax.psum(shares[7].astype(jnp.bfloat16), "blk").astype(jnp.float32),
        lax.psum(shares[8].astype(jnp.bfloat16), "blk").astype(jnp.float32),
    )
    return (
        mixed,
        grad_frames,
        grad_skip,
        totals[0],
        totals[7],
        totals[1],
        totals[2],
        totals[3],
        totals[4],
        totals[8],
        totals[5],
        totals[6],
    )


def solution(mesh):
    return jax.shard_map(
        on_device,
        mesh=mesh,
        in_specs=(
            P(("dp", "blk"), None),
            P(("dp", "blk"), None),
            P(),
            P(),
            P(),
            P(),
            P(),
            P(),
            P(),
            P(),
            P(),
            P(("dp", "blk"), None),
            P("dp", None),
            P("dp", None),
        ),
        out_specs=(
            P(("dp", "blk"), None),
            P(("dp", "blk"), None),
            P(("dp", "blk"), None),
            P(None, "dp"),
            P("dp"),
            P(None, "dp"),
            P(None, "dp"),
            P(None, "dp"),
            P(None, "dp"),
            P("dp"),
            P(None, "dp"),
            P(None, "dp"),
        ),
        check_vma=False,
    )
```

profile of v0, /device:TPU:0, one launch (start us, length us, event | category | flops | bytes accessed | tf_op | source)
XLA Modules:
  0.0 1088.4 jit_solution(14260799592365389874)
XLA Ops:
  9.6 3.9 fusion.66
  22.4 45.3 %all-gather.3.cloned.1.call-done = bf16[2048,16,64]{0,2,1:T(8,128)(2,1)} async-done(((bf16[256,16,64]{0,2,1:T(8,128)(2,1)}), bf16[2048,16,64]{0,2,1:T(8,128)(2,1)}) %all-gather.3.cloned.1.call-update) | async-done | bytes 4194320 | tf_op jit(solution)/shard_map/all_gather | solution.py:107
  67.8 47.7 %all-gather.5.cloned.1.call-done = bf16[2048,16,64]{0,2,1:T(8,128)(2,1)} async-done(((bf16[256,16,64]{0,2,1:T(8,128)(2,1)}), bf16[2048,16,64]{0,2,1:T(8,128)(2,1)}) %all-gather.5.cloned.1.call-update) | async-done | bytes 4194320 | tf_op jit(solution)/shard_map/all_gather | solution.py:108
  115.4 76.0 %while.44 = (s32[]{:T(128)}, f32[16,256]{1,0:T(8,128)S(1)}, f32[16,256]{1,0:T(8,128)S(1)}, f32[256,16,64]{0,2,1:T(8,128)}, s32[256]{0:T(256)S(1)}, /*index=5*/s3...) while((s32[]{:T(128)}, f32[16,256]{1,0:T(8,128)S(1)}, ...), condition=%wide.region_10.11_spmd.clone, body=%wide.region_4.10_spmd.clone.sunk | while | flops 578200896 | bytes 66351660 | solution.py:129
  116.0 6.9 fusion.145
  123.0 5.0 fusion.147
  128.8 5.5 fusion.149
  134.9 6.9 fusion.145
  141.9 5.0 fusion.147
  147.7 5.7 fusion.149
  154.0 6.9 fusion.145
  160.9 5.0 fusion.147
  166.7 5.7 fusion.149
  173.0 6.9 fusion.145
  179.9 5.0 fusion.147
  185.8 5.7 fusion.149
  196.0 6.0 fusion.61
  202.0 16.9 %add_convert_fusion = (bf16[256,4096]{1,0:T(8,128)(2,1)S(1)}, f32[256,4096]{1,0:T(8,128)}) fusion(f32[256,4096]{1,0:T(8,128)S(1)} %fusion.61, bf16[256,1024]{1,0:T(8,128)(2,1)S(1)} %copy-done.17, bf16[4096,1024]{1,0:T(8,128)(2,1)} %param.28), kind=kOutput, calls=%fused_computation.70 | convolution fusion | flops 2222981120 | bytes 19398656 | tf_op jit(solution)/shard_map/rd,fd->rf/dot_general | solution.py:43
  227.3 291.2 %while.45 = (s32[]{:T(128)}, bf16[256,16,64]{0,2,1:T(8,128)(2,1)}, bf16[256,16,64]{0,2,1:T(8,128)(2,1)}, f32[256,16,64]{0,2,1:T(8,128)}, f32[256,16,64]{0,2,1:T(...) while((s32[]{:T(128)}, bf16[256,16,64]{0,2,1:T(8,128)(2,1)}, ...), condition=%wide.region_20.21_spmd.clone, body=%wide.region_16.20_spmd.clone.sunk | while | flops 689251136 | bytes 59244848 | solution.py:176
  249.2 3.5 collective-permute-done.3
  254.9 3.5 collective-permute-done
  258.3 5.6 collective-permute-done.1
  276.7 3.6 fusion.163
  285.6 3.5 collective-permute-done.3
  291.2 3.5 collective-permute-done
  294.7 5.6 collective-permute-done.1
  313.0 3.6 fusion.163
  322.0 3.5 collective-permute-done.3
  327.6 3.5 collective-permute-done
  331.1 5.6 collective-permute-done.1
  349.4 3.6 fusion.163
  358.3 3.5 collective-permute-done.3
  364.0 3.5 collective-permute-done
  367.5 5.6 collective-permute-done.1
  385.8 3.6 fusion.163
  394.7 3.5 collective-permute-done.3
  400.3 3.5 collective-permute-done
  403.8 5.6 collective-permute-done.1
  422.2 3.6 fusion.163
  431.1 3.5 collective-permute-done.3
  436.7 3.5 collective-permute-done
  440.2 5.6 collective-permute-done.1
  458.5 3.6 fusion.163
  467.5 3.5 collective-permute-done.3
  473.1 3.5 collective-permute-done
  476.6 5.6 collective-permute-done.1
  494.9 3.6 fusion.163
  503.8 3.5 collective-permute-done.3
  509.4 3.5 collective-permute-done
  512.9 5.6 collective-permute-done.1
  547.8 7.6 convolution_convert_fusion.1
  555.5 4.3 multiply_convert_fusion.1
  561.2 5.6 convolution_convert_fusion
  566.9 28.9 %reduce-scatter.12.cloned.1.call-done = bf16[1024,256]{1,0:T(8,128)(2,1)} async-done(((bf16[1024,1024]{1,0:T(8,128)(2,1)}), bf16[1024,256]{1,0:T(8,128)(2,1)}) %reduce-scatter.12.cloned.1.call-update) | async-done | bytes 524304 | tf_op jit(solution)/shard_map/reduce_scatter | solution.py:205
  595.8 38.0 %reduce-scatter.14.cloned.1.call-done = bf16[1024,256]{1,0:T(8,128)(2,1)} async-done(((bf16[1024,1024]{1,0:T(8,128)(2,1)}), bf16[1024,256]{1,0:T(8,128)(2,1)}) %reduce-scatter.14.cloned.1.call-update) | async-done | bytes 524304 | tf_op jit(solution)/shard_map/reduce_scatter | solution.py:208
  633.8 38.3 %reduce-scatter.16.cloned.1.call-done = bf16[1024,256]{1,0:T(8,128)(2,1)} async-done(((bf16[1024,1024]{1,0:T(8,128)(2,1)}), bf16[1024,256]{1,0:T(8,128)(2,1)}) %reduce-scatter.16.cloned.1.call-update) | async-done | bytes 524304 | tf_op jit(solution)/shard_map/reduce_scatter | solution.py:211
  672.1 55.6 %reduce-scatter.8.cloned.1.call-done = bf16[2048,256]{1,0:T(8,128)(2,1)} async-done(((bf16[2048,1024]{1,0:T(8,128)(2,1)}), bf16[2048,256]{1,0:T(8,128)(2,1)}) %reduce-scatter.8.cloned.1.call-update) | async-done | bytes 1048592 | tf_op jit(solution)/shard_map/reduce_scatter | solution.py:199
  727.8 89.8 %reduce-scatter.18.cloned.1.call-done = bf16[1024,1024]{1,0:T(8,128)(2,1)} async-done(((bf16[1024,4096]{1,0:T(8,128)(2,1)}), bf16[1024,1024]{1,0:T(8,128)(2,1)}) %reduce-scatter.18.cloned.1.call-update) | async-done | bytes 2097168 | tf_op jit(solution)/shard_map/reduce_scatter | solution.py:214
  817.5 89.5 %reduce-scatter.20.cloned.1.call-done = bf16[4096,256]{1,0:T(8,128)(2,1)} async-done(((bf16[4096,1024]{1,0:T(8,128)(2,1)}), bf16[4096,256]{1,0:T(8,128)(2,1)}) %reduce-scatter.20.cloned.1.call-update) | async-done | bytes 2097168 | tf_op jit(solution)/shard_map/reduce_scatter | solution.py:217
  908.3 8.9 all-reduce.4
  917.4 15.3 %all-reduce.2 = (bf16[256]{0:T(256)(128)(2,1)S(1)}, bf16[256]{0:T(256)(128)(2,1)S(1)}) all-reduce(bf16[256]{0:T(256)(128)(2,1)S(1)} %dynamic-slice.1, bf16[256]{0:T(256)(128)(2,1)S(1)} %dynamic-slice.3), channel_id=1, replica_groups=mesh['dp'=4,'blk'=8] {'blk'}, use_global_device_ids=true, to_apply=%region_27.28 | all-reduce | flops 512 | bytes 2048 | tf_op jit(solution)/shard_map/psum | solution.py:235
  933.8 3.8 convolution_convert_fusion.3
  938.7 6.6 fusion.56
  945.3 123.1 %all-reduce.7.cloned.1.call-done = (bf16[2048,256]{1,0:T(8,128)(2,1)}, bf16[1024,256]{1,0:T(8,128)(2,1)}, bf16[1024,256]{1,0:T(8,128)(2,1)}, bf16[1024,256]{1,0:...) async-done(((bf16[2048,256]{1,0:T(8,128)(2,1)}, bf16[1024,256]{1,0:T(8,128)(2,1)}, bf16[1024,256]{1,0:T(8,128)(2,1)}, ...) | async-done | bytes 7340048 | tf_op jit(solution)/shard_map/psum | solution.py:228
  (466 shorter events, 239.8 us)
Async XLA Ops:
  7.2 10.0 copy-start
  7.2 60.6 %all-gather.3.cloned.1.call-start = ((), (), s32[]{:S(2)}) async-start(), calls=%async_computation.7 | async-start | bytes 4718592 | tf_op jit(solution)/shard_map/all_gather | solution.py:107
  9.6 5.5 copy-start.41
  9.6 5.7 copy-start.31
  17.1 98.3 %copy-start.40 = (s32[1,4]{1,0:T(1,128)S(1)}, s32[1,4]{1,0:T(1,128)}, u32[]{:S(2)}) copy-start(s32[1,4]{1,0:T(1,128)} %param.30) | copy-start | bytes 52
  17.1 98.3 %all-gather.5.cloned.1.call-start = ((), (), s32[]{:S(2)}) async-start(), calls=%async_computation.8 | async-start | bytes 4718592 | tf_op jit(solution)/shard_map/all_gather | solution.py:108
  18.9 548.0 %reduce-scatter.10.cloned.1.call-start = ((), (), s32[]{:S(2)}) async-start(), calls=%async_computation.10 | async-start | bytes 2621440 | tf_op jit(solution)/shard_map/reduce_scatter | solution.py:202
  122.9 5.8 copy-start.1
  141.8 5.8 copy-start.1
  160.9 5.8 copy-start.1
  179.9 5.8 copy-start.1
  192.8 9.2 copy-start.20
  195.7 25.9 %copy-start.7 = (f32[256,1024]{1,0:T(8,128)}, f32[256,1024]{1,0:T(8,128)S(1)}, u32[]{:S(2)}) copy-start(f32[256,1024]{1,0:T(8,128)S(1)} %get-tuple-element.896) | copy-start | bytes 3145732
  196.0 6.0 copy-start.17
  196.0 23.0 %slice-start = ((s8[8388608]{0:T(1024)(128)(4,1)}), s8[4194304]{0:T(1024)(128)(4,1)S(1)}, s32[]{:S(2)}) async-start(s8[8388608]{0:T(1024)(128)(4,1)} %bitcast.167), calls=%async_computation.17 | async-start | bytes 8388608
  202.0 17.0 %copy-start.26 = (f32[256,4096]{1,0:T(8,128)}, f32[256,4096]{1,0:T(8,128)S(1)}, u32[]{:S(2)}) copy-start(f32[256,4096]{1,0:T(8,128)S(1)} %fusion.61) | copy-start | bytes 12582916
  202.0 17.0 %slice-start.1 = ((s8[8388608]{0:T(1024)(128)(4,1)}), s8[4194304]{0:T(1024)(128)(4,1)S(1)}, s32[]{:S(2)}) async-start(s8[8388608]{0:T(1024)(128)(4,1)} %bitcast.167), calls=%async_computation.18 | async-start | bytes 8388608
  236.4 10.7 collective-permute-start.2
  240.2 12.5 %collective-permute-start.3 = (bf16[256,16,64]{0,2,1:T(8,128)(2,1)}, bf16[256,16,64]{0,2,1:T(8,128)(2,1)}, u32[]{:S(2)}, u32[]{:S(2)}) collective-permute-start(bf16[256,16,64]{0,2,1:T(8,128)(2,1)} %fusion.162), channel_id=1, source_target_pairs={{0,1},{1,2},{2,3},{3,4},{4,5},{5,6},{6,7},{7,0},{8,9},{9,10},{10,1... | collective-permute-start | bytes 1572872 | tf_op jit(solution)/shard_map/while/body/eval_jaxpr/ppermute | solution.py:19
  240.5 17.9 %collective-permute-start = (bf16[256,16,64]{0,2,1:T(8,128)(2,1)S(1)}, bf16[256,16,64]{0,2,1:T(8,128)(2,1)}, u32[]{:S(2)}, u32[]{:S(2)}) collective-permute-start(bf16[256,16,64]{0,2,1:T(8,128)(2,1)S(1)} %copy.71), channel_id=1, source_target_pairs={{0,1},{1,2},{2,3},{3,4},{4,5},{5,6},{6,7},{7,0},{8,9},{9,10},{10,1... | collective-permute-start | bytes 1572872 | tf_op jit(solution)/shard_map/while/body/eval_jaxpr/ppermute | solution.py:19
  240.5 23.4 %collective-permute-start.1 = (bf16[256,16,64]{0,2,1:T(8,128)(2,1)}, bf16[256,16,64]{0,2,1:T(8,128)(2,1)}, u32[]{:S(2)}, u32[]{:S(2)}) collective-permute-start(bf16[256,16,64]{0,2,1:T(8,128)(2,1)} %copy.72), channel_id=1, source_target_pairs={{0,1},{1,2},{2,3},{3,4},{4,5},{5,6},{6,7},{7,0},{8,9},{9,10},{10,1... | collective-permute-start | bytes 1572872 | tf_op jit(solution)/shard_map/while/body/eval_jaxpr/ppermute | solution.py:19
  271.5 5.1 copy-start.2
  272.8 10.7 collective-permute-start.2
  276.6 12.5 %collective-permute-start.3 = (bf16[256,16,64]{0,2,1:T(8,128)(2,1)}, bf16[256,16,64]{0,2,1:T(8,128)(2,1)}, u32[]{:S(2)}, u32[]{:S(2)}) collective-permute-start(bf16[256,16,64]{0,2,1:T(8,128)(2,1)} %fusion.162), channel_id=1, source_target_pairs={{0,1},{1,2},{2,3},{3,4},{4,5},{5,6},{6,7},{7,0},{8,9},{9,10},{10,1... | collective-permute-start | bytes 1572872 | tf_op jit(solution)/shard_map/while/body/eval_jaxpr/ppermute | solution.py:19
  276.6 18.1 %collective-permute-start = (bf16[256,16,64]{0,2,1:T(8,128)(2,1)S(1)}, bf16[256,16,64]{0,2,1:T(8,128)(2,1)}, u32[]{:S(2)}, u32[]{:S(2)}) collective-permute-start(bf16[256,16,64]{0,2,1:T(8,128)(2,1)S(1)} %copy.71), channel_id=1, source_target_pairs={{0,1},{1,2},{2,3},{3,4},{4,5},{5,6},{6,7},{7,0},{8,9},{9,10},{10,1... | collective-permute-start | bytes 1572872 | tf_op jit(solution)/shard_map/while/body/eval_jaxpr/ppermute | solution.py:19
  276.6 23.7 %collective-permute-start.1 = (bf16[256,16,64]{0,2,1:T(8,128)(2,1)}, bf16[256,16,64]{0,2,1:T(8,128)(2,1)}, u32[]{:S(2)}, u32[]{:S(2)}) collective-permute-start(bf16[256,16,64]{0,2,1:T(8,128)(2,1)} %copy.72), channel_id=1, source_target_pairs={{0,1},{1,2},{2,3},{3,4},{4,5},{5,6},{6,7},{7,0},{8,9},{9,10},{10,1... | collective-permute-start | bytes 1572872 | tf_op jit(solution)/shard_map/while/body/eval_jaxpr/ppermute | solution.py:19
  309.1 10.7 collective-permute-start.2
  313.0 12.5 %collective-permute-start.3 = (bf16[256,16,64]{0,2,1:T(8,128)(2,1)}, bf16[256,16,64]{0,2,1:T(8,128)(2,1)}, u32[]{:S(2)}, u32[]{:S(2)}) collective-permute-start(bf16[256,16,64]{0,2,1:T(8,128)(2,1)} %fusion.162), channel_id=1, source_target_pairs={{0,1},{1,2},{2,3},{3,4},{4,5},{5,6},{6,7},{7,0},{8,9},{9,10},{10,1... | collective-permute-start | bytes 1572872 | tf_op jit(solution)/shard_map/while/body/eval_jaxpr/ppermute | solution.py:19
  313.0 18.1 %collective-permute-start = (bf16[256,16,64]{0,2,1:T(8,128)(2,1)S(1)}, bf16[256,16,64]{0,2,1:T(8,128)(2,1)}, u32[]{:S(2)}, u32[]{:S(2)}) collective-permute-start(bf16[256,16,64]{0,2,1:T(8,128)(2,1)S(1)} %copy.71), channel_id=1, source_target_pairs={{0,1},{1,2},{2,3},{3,4},{4,5},{5,6},{6,7},{7,0},{8,9},{9,10},{10,1... | collective-permute-start | bytes 1572872 | tf_op jit(solution)/shard_map/while/body/eval_jaxpr/ppermute | solution.py:19
  313.0 23.7 %collective-permute-start.1 = (bf16[256,16,64]{0,2,1:T(8,128)(2,1)}, bf16[256,16,64]{0,2,1:T(8,128)(2,1)}, u32[]{:S(2)}, u32[]{:S(2)}) collective-permute-start(bf16[256,16,64]{0,2,1:T(8,128)(2,1)} %copy.72), channel_id=1, source_target_pairs={{0,1},{1,2},{2,3},{3,4},{4,5},{5,6},{6,7},{7,0},{8,9},{9,10},{10,1... | collective-permute-start | bytes 1572872 | tf_op jit(solution)/shard_map/while/body/eval_jaxpr/ppermute | solution.py:19
  345.5 10.7 collective-permute-start.2
  349.3 12.5 %collective-permute-start.3 = (bf16[256,16,64]{0,2,1:T(8,128)(2,1)}, bf16[256,16,64]{0,2,1:T(8,128)(2,1)}, u32[]{:S(2)}, u32[]{:S(2)}) collective-permute-start(bf16[256,16,64]{0,2,1:T(8,128)(2,1)} %fusion.162), channel_id=1, source_target_pairs={{0,1},{1,2},{2,3},{3,4},{4,5},{5,6},{6,7},{7,0},{8,9},{9,10},{10,1... | collective-permute-start | bytes 1572872 | tf_op jit(solution)/shard_map/while/body/eval_jaxpr/ppermute | solution.py:19
  349.3 18.1 %collective-permute-start = (bf16[256,16,64]{0,2,1:T(8,128)(2,1)S(1)}, bf16[256,16,64]{0,2,1:T(8,128)(2,1)}, u32[]{:S(2)}, u32[]{:S(2)}) collective-permute-start(bf16[256,16,64]{0,2,1:T(8,128)(2,1)S(1)} %copy.71), channel_id=1, source_target_pairs={{0,1},{1,2},{2,3},{3,4},{4,5},{5,6},{6,7},{7,0},{8,9},{9,10},{10,1... | collective-permute-start | bytes 1572872 | tf_op jit(solution)/shard_map/while/body/eval_jaxpr/ppermute | solution.py:19
  349.3 23.7 %collective-permute-start.1 = (bf16[256,16,64]{0,2,1:T(8,128)(2,1)}, bf16[256,16,64]{0,2,1:T(8,128)(2,1)}, u32[]{:S(2)}, u32[]{:S(2)}) collective-permute-start(bf16[256,16,64]{0,2,1:T(8,128)(2,1)} %copy.72), channel_id=1, source_target_pairs={{0,1},{1,2},{2,3},{3,4},{4,5},{5,6},{6,7},{7,0},{8,9},{9,10},{10,1... | collective-permute-start | bytes 1572872 | tf_op jit(solution)/shard_map/while/body/eval_jaxpr/ppermute | solution.py:19
  381.9 10.7 collective-permute-start.2
  385.7 12.5 %collective-permute-start.3 = (bf16[256,16,64]{0,2,1:T(8,128)(2,1)}, bf16[256,16,64]{0,2,1:T(8,128)(2,1)}, u32[]{:S(2)}, u32[]{:S(2)}) collective-permute-start(bf16[256,16,64]{0,2,1:T(8,128)(2,1)} %fusion.162), channel_id=1, source_target_pairs={{0,1},{1,2},{2,3},{3,4},{4,5},{5,6},{6,7},{7,0},{8,9},{9,10},{10,1... | collective-permute-start | bytes 1572872 | tf_op jit(solution)/shard_map/while/body/eval_jaxpr/ppermute | solution.py:19
  385.7 18.1 %collective-permute-start = (bf16[256,16,64]{0,2,1:T(8,128)(2,1)S(1)}, bf16[256,16,64]{0,2,1:T(8,128)(2,1)}, u32[]{:S(2)}, u32[]{:S(2)}) collective-permute-start(bf16[256,16,64]{0,2,1:T(8,128)(2,1)S(1)} %copy.71), channel_id=1, source_target_pairs={{0,1},{1,2},{2,3},{3,4},{4,5},{5,6},{6,7},{7,0},{8,9},{9,10},{10,1... | collective-permute-start | bytes 1572872 | tf_op jit(solution)/shard_map/while/body/eval_jaxpr/ppermute | solution.py:19
  385.7 23.7 %collective-permute-start.1 = (bf16[256,16,64]{0,2,1:T(8,128)(2,1)}, bf16[256,16,64]{0,2,1:T(8,128)(2,1)}, u32[]{:S(2)}, u32[]{:S(2)}) collective-permute-start(bf16[256,16,64]{0,2,1:T(8,128)(2,1)} %copy.72), channel_id=1, source_target_pairs={{0,1},{1,2},{2,3},{3,4},{4,5},{5,6},{6,7},{7,0},{8,9},{9,10},{10,1... | collective-permute-start | bytes 1572872 | tf_op jit(solution)/shard_map/while/body/eval_jaxpr/ppermute | solution.py:19
  418.2 10.7 collective-permute-start.2
  422.1 12.5 %collective-permute-start.3 = (bf16[256,16,64]{0,2,1:T(8,128)(2,1)}, bf16[256,16,64]{0,2,1:T(8,128)(2,1)}, u32[]{:S(2)}, u32[]{:S(2)}) collective-permute-start(bf16[256,16,64]{0,2,1:T(8,128)(2,1)} %fusion.162), channel_id=1, source_target_pairs={{0,1},{1,2},{2,3},{3,4},{4,5},{5,6},{6,7},{7,0},{8,9},{9,10},{10,1... | collective-permute-start | bytes 1572872 | tf_op jit(solution)/shard_map/while/body/eval_jaxpr/ppermute | solution.py:19
  422.1 18.1 %collective-permute-start = (bf16[256,16,64]{0,2,1:T(8,128)(2,1)S(1)}, bf16[256,16,64]{0,2,1:T(8,128)(2,1)}, u32[]{:S(2)}, u32[]{:S(2)}) collective-permute-start(bf16[256,16,64]{0,2,1:T(8,128)(2,1)S(1)} %copy.71), channel_id=1, source_target_pairs={{0,1},{1,2},{2,3},{3,4},{4,5},{5,6},{6,7},{7,0},{8,9},{9,10},{10,1... | collective-permute-start | bytes 1572872 | tf_op jit(solution)/shard_map/while/body/eval_jaxpr/ppermute | solution.py:19
  422.1 23.7 %collective-permute-start.1 = (bf16[256,16,64]{0,2,1:T(8,128)(2,1)}, bf16[256,16,64]{0,2,1:T(8,128)(2,1)}, u32[]{:S(2)}, u32[]{:S(2)}) collective-permute-start(bf16[256,16,64]{0,2,1:T(8,128)(2,1)} %copy.72), channel_id=1, source_target_pairs={{0,1},{1,2},{2,3},{3,4},{4,5},{5,6},{6,7},{7,0},{8,9},{9,10},{10,1... | collective-permute-start | bytes 1572872 | tf_op jit(solution)/shard_map/while/body/eval_jaxpr/ppermute | solution.py:19
  454.6 10.7 collective-permute-start.2
  458.4 12.5 %collective-permute-start.3 = (bf16[256,16,64]{0,2,1:T(8,128)(2,1)}, bf16[256,16,64]{0,2,1:T(8,128)(2,1)}, u32[]{:S(2)}, u32[]{:S(2)}) collective-permute-start(bf16[256,16,64]{0,2,1:T(8,128)(2,1)} %fusion.162), channel_id=1, source_target_pairs={{0,1},{1,2},{2,3},{3,4},{4,5},{5,6},{6,7},{7,0},{8,9},{9,10},{10,1... | collective-permute-start | bytes 1572872 | tf_op jit(solution)/shard_map/while/body/eval_jaxpr/ppermute | solution.py:19
  458.4 18.1 %collective-permute-start = (bf16[256,16,64]{0,2,1:T(8,128)(2,1)S(1)}, bf16[256,16,64]{0,2,1:T(8,128)(2,1)}, u32[]{:S(2)}, u32[]{:S(2)}) collective-permute-start(bf16[256,16,64]{0,2,1:T(8,128)(2,1)S(1)} %copy.71), channel_id=1, source_target_pairs={{0,1},{1,2},{2,3},{3,4},{4,5},{5,6},{6,7},{7,0},{8,9},{9,10},{10,1... | collective-permute-start | bytes 1572872 | tf_op jit(solution)/shard_map/while/body/eval_jaxpr/ppermute | solution.py:19
  458.5 23.7 %collective-permute-start.1 = (bf16[256,16,64]{0,2,1:T(8,128)(2,1)}, bf16[256,16,64]{0,2,1:T(8,128)(2,1)}, u32[]{:S(2)}, u32[]{:S(2)}) collective-permute-start(bf16[256,16,64]{0,2,1:T(8,128)(2,1)} %copy.72), channel_id=1, source_target_pairs={{0,1},{1,2},{2,3},{3,4},{4,5},{5,6},{6,7},{7,0},{8,9},{9,10},{10,1... | collective-permute-start | bytes 1572872 | tf_op jit(solution)/shard_map/while/body/eval_jaxpr/ppermute | solution.py:19
  491.0 10.7 collective-permute-start.2
  494.8 12.5 %collective-permute-start.3 = (bf16[256,16,64]{0,2,1:T(8,128)(2,1)}, bf16[256,16,64]{0,2,1:T(8,128)(2,1)}, u32[]{:S(2)}, u32[]{:S(2)}) collective-permute-start(bf16[256,16,64]{0,2,1:T(8,128)(2,1)} %fusion.162), channel_id=1, source_target_pairs={{0,1},{1,2},{2,3},{3,4},{4,5},{5,6},{6,7},{7,0},{8,9},{9,10},{10,1... | collective-permute-start | bytes 1572872 | tf_op jit(solution)/shard_map/while/body/eval_jaxpr/ppermute | solution.py:19
  494.8 18.1 %collective-permute-start = (bf16[256,16,64]{0,2,1:T(8,128)(2,1)S(1)}, bf16[256,16,64]{0,2,1:T(8,128)(2,1)}, u32[]{:S(2)}, u32[]{:S(2)}) collective-permute-start(bf16[256,16,64]{0,2,1:T(8,128)(2,1)S(1)} %copy.71), channel_id=1, source_target_pairs={{0,1},{1,2},{2,3},{3,4},{4,5},{5,6},{6,7},{7,0},{8,9},{9,10},{10,1... | collective-permute-start | bytes 1572872 | tf_op jit(solution)/shard_map/while/body/eval_jaxpr/ppermute | solution.py:19
  494.8 23.7 %collective-permute-start.1 = (bf16[256,16,64]{0,2,1:T(8,128)(2,1)}, bf16[256,16,64]{0,2,1:T(8,128)(2,1)}, u32[]{:S(2)}, u32[]{:S(2)}) collective-permute-start(bf16[256,16,64]{0,2,1:T(8,128)(2,1)} %copy.72), channel_id=1, source_target_pairs={{0,1},{1,2},{2,3},{3,4},{4,5},{5,6},{6,7},{7,0},{8,9},{9,10},{10,1... | collective-permute-start | bytes 1572872 | tf_op jit(solution)/shard_map/while/body/eval_jaxpr/ppermute | solution.py:19
  518.6 5.4 copy-start.4
  523.9 71.9 %reduce-scatter.12.cloned.1.call-start = ((), (), s32[]{:S(2)}) async-start(), calls=%async_computation.11 | async-start | bytes 2621440 | tf_op jit(solution)/shard_map/reduce_scatter | solution.py:205
  524.1 6.4 copy-start.14
  528.0 105.8 %reduce-scatter.14.cloned.1.call-start = ((), (), s32[]{:S(2)}) async-start(), calls=%async_computation.12 | async-start | bytes 2621440 | tf_op jit(solution)/shard_map/reduce_scatter | solution.py:208
  532.6 139.5 %reduce-scatter.16.cloned.1.call-start = ((), (), s32[]{:S(2)}) async-start(), calls=%async_computation.13 | async-start | bytes 2621440 | tf_op jit(solution)/shard_map/reduce_scatter | solution.py:211
  535.7 192.0 %reduce-scatter.8.cloned.1.call-start = ((), (), s32[]{:S(2)}) async-start(), calls=%async_computation.9 | async-start | bytes 5242880 | tf_op jit(solution)/shard_map/reduce_scatter | solution.py:199
  546.6 270.9 %reduce-scatter.18.cloned.1.call-start = ((), (), s32[]{:S(2)}) async-start(), calls=%async_computation.14 | async-start | bytes 10485760 | tf_op jit(solution)/shard_map/reduce_scatter | solution.py:214
  555.5 351.5 %reduce-scatter.20.cloned.1.call-start = ((), (), s32[]{:S(2)}) async-start(), calls=%async_computation.15 | async-start | bytes 10485760 | tf_op jit(solution)/shard_map/reduce_scatter | solution.py:217
  555.5 5.7 copy-start.19
  566.8 340.2 %copy-start.50 = (u32[32]{0:T(128)S(1)}, u32[32]{0:T(128)}, u32[]{:S(2)}) copy-start(u32[32]{0:T(128)} %constant.267) | copy-start | bytes 388
  566.8 501.5 %all-reduce.7.cloned.1.call-start = ((), (), s32[]{:S(2)}) async-start(), calls=%async_computation.16 | async-start | bytes 14680064 | tf_op jit(solution)/shard_map/psum | solution.py:228
  1068.4 6.0 copy-start.37
  1068.4 7.0 copy-start.36
  1068.4 8.1 copy-start.29
  (55 other events, 163.6 us)
Sparse Core Ops, SparseCore 0:
  17.2 50.4 all-gather.2
  69.3 46.0 all-gather.4
  524.0 33.3 reduce-scatter.9
  560.5 35.1 reduce-scatter.11
  598.6 35.1 reduce-scatter.13
  636.9 35.1 reduce-scatter.15
  675.1 52.6 reduce-scatter.7
  731.1 86.3 reduce-scatter.17
  820.6 86.3 reduce-scatter.19
  910.0 158.2 all-reduce.6
where the time goes:
time: 1100 us; the launch traced here: 1090 us
  waiting for transfers between devices  682 us (62%)
  matrix products  227 us (21%)
  other arithmetic  86.4 us (8%)
  local copies, waits for them, and re-layouts  48.3 us (4%)
  blocking collectives  24.2 us (2%)
  between operations  15.9 us (1%)
    dot_general x69, matrix products, product(): return jnp.einsum(form, left, right, preferred_element_type=jnp.float32)  227 us
    ppermute x32, waiting for transfers between devices, shifted(): lax.ppermute(array, axis, [(i, (i + by) % size) for i in range(size)])  126 us
    psum x1, waiting for transfers between devices, on_device(): lax.psum(shares[0].astype(jnp.bfloat16), 'blk').astype(jnp.float32)  123 us
    reduce_scatter x1, waiting for transfers between devices, on_device(): lax.psum_scatter(grad_w_up.astype(jnp.bfloat16), 'dp', scatter_dimension=...  89.8 us
    reduce_scatter x1, waiting for transfers between devices, on_device(): lax.psum_scatter(grad_w_down.astype(jnp.bfloat16), 'dp', scatter_dimensio...  89.5 us
    reduce_scatter x1, waiting for transfers between devices, on_device(): lax.psum_scatter(grad_w_skip.astype(jnp.bfloat16), 'dp', scatter_dimensio...  55.6 us
    all_gather x1, waiting for transfers between devices, on_device(): lax.all_gather(value_rows, 'blk', axis=0, tiled=True)  47.7 us
    all_gather x1, waiting for transfers between devices, on_device(): lax.all_gather(key_rows, 'blk', axis=0, tiled=True)  45.3 us
  transfers between devices with their start and end apart: 42, of which 41 were waited for; matrix products, arithmetic and copies ran while one was open for 13% of the time, Pallas kernels for 0%

commit v1 on v0

--- a/solution.py
+++ b/solution.py
@@ -4,6 +4,8 @@
 import jax
 import jax.numpy as jnp
 from jax import lax
+from jax.experimental import pallas as pl
+from jax.experimental.pallas import tpu as pltpu
 from jax.sharding import PartitionSpec as P
 
 HEADS = 16
@@ -43,7 +45,7 @@
     return jnp.einsum(form, left, right, preferred_element_type=jnp.float32)
 
 
-def on_device(
+def on_device_general(
     frames,
     skip_feats,
     w_skip,
@@ -251,9 +253,580 @@
     )
 
 
+BF = jnp.bfloat16
+F32 = jnp.float32
+NT = (((1,), (1,)), ((), ()))
+NN = (((1,), (0,)), ((), ()))
+TN = (((0,), (0,)), ((), ()))
+TILE = 512
+LANES = 128
+VMEM_SPEC = pl.BlockSpec(memory_space=pltpu.VMEM)
+SMEM_SPEC = pl.BlockSpec(memory_space=pltpu.SMEM)
+
+
+def mm(left, right, form):
+    return lax.dot_general(left, right, form, preferred_element_type=F32)
+
+
+def split3(value):
+    first = value.astype(BF)
+    rest = value - first.astype(F32)
+    second = rest.astype(BF)
+    return first, second, (rest - second.astype(F32)).astype(BF)
+
+
+def tables_kernel(seg_ref, slope_ref, qx_ref, kx_ref):
+    heads = qx_ref.shape[0]
+    seq_len = kx_ref.shape[0]
+    n_utt = seg_ref.shape[1]
+
+    def one(b, carry):
+        rows = pl.ds(pl.multiple_of(b * TILE, TILE), TILE)
+        lane = lax.broadcasted_iota(jnp.int32, (TILE, LANES), 1) - HEAD_DIM
+        pos = lax.broadcasted_iota(jnp.int32, (TILE, LANES), 0) + b * TILE
+        coarse = (pos >> 8).astype(F32)
+        fine = (pos & 255).astype(F32)
+        first = jnp.zeros_like(lane)
+        last = jnp.zeros_like(lane)
+        last_live = jnp.zeros_like(lane)
+        for u in range(n_utt):
+            here = lane == 9 + u
+            first = jnp.where(here, seg_ref[0, u], first)
+            last = jnp.where(here, seg_ref[1, u], last)
+            last_live = jnp.where(here, seg_ref[2, u], last_live)
+        member = jnp.where((pos >= first) & (pos < last), 1.0, 0.0)
+        is_utt = (lane >= 9) & (lane < 9 + n_utt)
+        closed = jnp.where((pos >= first) & (pos < last_live), 0.0, NEG_FILL)
+        digits = jnp.where((lane & 1) == 0, coarse, fine)
+        keys = jnp.where(is_utt, closed, jnp.where(lane < 6, digits, 1.0))
+        keys = jnp.where((lane >= 0) & (lane < 9 + n_utt), keys, 0.0)
+        kx_ref[rows, :] = keys.astype(BF)
+        for h in range(heads):
+            for s in range(2):
+                sign = 1.0 if s == 0 else -1.0
+                out = jnp.where(is_utt, member, 0.0)
+                for e in range(6):
+                    out = jnp.where(lane == e, slope_ref[h, e] * sign, out)
+                for p, piece in enumerate(split3(pos.astype(F32) * (slope_ref[h, 6] * -sign))):
+                    out = jnp.where(lane == 6 + p, piece.astype(F32), out)
+                qx_ref[h, s, rows, :] = out.astype(BF)
+        return carry
+
+    lax.fori_loop(0, seq_len // TILE, one, 0)
+
+
+def attn_tables(lengths, padded, slopes, seq_len):
+    starts = jnp.cumsum(padded) - padded
+    segments = jnp.stack([starts, starts + padded, starts + lengths]).astype(jnp.int32)
+    heads = slopes.shape[0]
+    cols = []
+    rest = slopes
+    for _ in range(3):
+        piece = lax.reduce_precision(rest, 8, 7)
+        rest = rest - piece
+        cols += [piece * 256.0, piece]
+    coefs = jnp.stack(cols + [slopes], axis=1)
+    qx, kx = pl.pallas_call(
+        tables_kernel,
+        out_shape=(
+            jax.ShapeDtypeStruct((heads, 2, seq_len, LANES), BF),
+            jax.ShapeDtypeStruct((seq_len, LANES), BF),
+        ),
+        in_specs=[SMEM_SPEC, SMEM_SPEC],
+        out_specs=(VMEM_SPEC, VMEM_SPEC),
+        compiler_params=pltpu.CompilerParams(vmem_limit_bytes=24 * 2**20),
+        name="attn_tables",
+    )(segments, coefs)
+    return coefs, qx, kx
+
+
+def head_first(tile, h):
+    wide = tile.astype(F32)
+    return pltpu.roll(wide, HEAD_DIM, 1) if h else wide
+
+
+def ahead_of(rows, cols, axis):
+    return jnp.maximum(
+        lax.broadcasted_iota(jnp.int32, (rows, cols), axis)
+        - lax.broadcasted_iota(jnp.int32, (rows, cols), 1 - axis),
+        0,
+    ).astype(F32)
+
+
+def fwd_kernel(coef_ref, qkv_ref, qx_ref, kx_ref, o_ref, olow_ref, qb_ref, ka_ref, va_ref, s_ref):
+    seq_len = qkv_ref.shape[0]
+    blocks = seq_len // TILE
+    heads = qx_ref.shape[0]
+    for h in range(heads):
+        lo = h * HEAD_DIM
+
+        def prepare(b, carry, h=h):
+            rows = pl.ds(pl.multiple_of(b * TILE, TILE), TILE)
+            low_lane = lax.broadcasted_iota(jnp.int32, (TILE, LANES), 1) < HEAD_DIM
+            q = head_first(qkv_ref[rows, :LANES], h) * 0.125
+            k = head_first(qkv_ref[rows, LANES : 2 * LANES], h)
+            v = head_first(qkv_ref[rows, 2 * LANES :], h)
+            lane = lax.broadcasted_iota(jnp.int32, (TILE, LANES), 1)
+            ka_ref[h, rows, :] = jnp.where(low_lane, k, kx_ref[rows, :].astype(F32)).astype(BF)
+            va_ref[h, rows, :] = jnp.where(
+                low_lane, v, jnp.where(lane < HEAD_DIM + 3, 1.0, 0.0)
+            ).astype(BF)
+            for s in range(2):
+                qb_ref[h, s, rows, :] = jnp.where(
+                    low_lane, q, qx_ref[h, s, rows, :].astype(F32)
+                ).astype(BF)
+            return carry
+
+        lax.fori_loop(0, blocks, prepare, 0)
+
+        def one(qb, carry, h=h, lo=lo):
+            rows = pl.ds(pl.multiple_of(qb * TILE, TILE), TILE)
+            slope = coef_ref[h, 6]
+            top = None
+            for t in range(blocks):
+                kb = lax.rem(qb + t, blocks)
+                krows = pl.ds(pl.multiple_of(kb * TILE, TILE), TILE)
+                side = (kb > qb).astype(jnp.int32)
+                scores = mm(qb_ref[h, side, rows, :], ka_ref[h, krows, :], NT)
+                if t == 0:
+                    scores = scores - ahead_of(TILE, TILE, 1) * (2.0 * slope)
+                s_ref[:, t * TILE : (t + 1) * TILE] = scores
+                part = jnp.max(scores, axis=1, keepdims=True)
+                top = part if top is None else jnp.maximum(top, part)
+            acc = jnp.zeros((TILE, LANES), F32)
+            for t in range(blocks):
+                kb = lax.rem(qb + t, blocks)
+                krows = pl.ds(pl.multiple_of(kb * TILE, TILE), TILE)
+                probs = jnp.exp(s_ref[:, t * TILE : (t + 1) * TILE] - top).astype(BF)
+                acc = acc + mm(probs, va_ref[h, krows, :], NN)
+            total = acc[:, HEAD_DIM : HEAD_DIM + 1]
+            out = acc[:, :HEAD_DIM] / total
+            o_ref[rows, lo : lo + HEAD_DIM] = out
+            olow_ref[rows, lo : lo + HEAD_DIM] = out.astype(BF)
+            log_total = top + jnp.log(total)
+            lane = lax.broadcasted_iota(jnp.int32, (TILE, LANES), 1)
+            row_pos = (qb * TILE + lax.broadcasted_iota(jnp.int32, (TILE, 1), 0)).astype(F32)
+            for s in range(2):
+                base = row_pos * (slope * (1.0 if s else -1.0)) - log_total
+                full = qb_ref[h, s, rows, :].astype(F32)
+                for p, piece in enumerate(split3(base)):
+                    full = jnp.where(lane == HEAD_DIM + 6 + p, piece.astype(F32), full)
+                qb_ref[h, s, rows, :] = full.astype(BF)
+            return carry
+
+        lax.fori_loop(0, blocks, one, 0)
+
+
+def attn_fwd(coefs, qkv, qx, kx):
+    seq_len = qkv.shape[0]
+    heads = coefs.shape[0]
+    width = heads * HEAD_DIM
+    return pl.pallas_call(
+        fwd_kernel,
+        out_shape=(
+            jax.ShapeDtypeStruct((seq_len, width), F32),
+            jax.ShapeDtypeStruct((seq_len, width), BF),
+            jax.ShapeDtypeStruct((heads, 2, seq_len, LANES), BF),
+            jax.ShapeDtypeStruct((heads, seq_len, LANES), BF),
+            jax.ShapeDtypeStruct((heads, seq_len, LANES), BF),
+        ),
+        in_specs=[SMEM_SPEC, VMEM_SPEC, VMEM_SPEC, VMEM_SPEC],
+        out_specs=(VMEM_SPEC,) * 5,
+        scratch_shapes=[pltpu.VMEM((TILE, seq_len), F32)],
+        compiler_params=pltpu.CompilerParams(vmem_limit_bytes=36 * 2**20),
+        cost_estimate=pl.CostEstimate(
+            flops=16 * seq_len * seq_len * width,
+            bytes_accessed=10 * 2**20,
+            transcendentals=heads * seq_len * seq_len,
+        ),
+        name="attn_fwd",
+    )(coefs, qkv, qx, kx)
+
+
+def bwd_kernel(coef_ref, go_ref, o_ref, qb_ref, ka_ref, va_ref, dqkv_ref, ga_ref, dq_ref, kt_ref):
+    seq_len = go_ref.shape[0]
+    blocks = seq_len // TILE
+    heads = ka_ref.shape[0]
+    width = heads * HEAD_DIM
+    for h in range(heads):
+        lo = h * HEAD_DIM
+
+        def prepare(b, carry, h=h, lo=lo):
+            rows = pl.ds(pl.multiple_of(b * TILE, TILE), TILE)
+            go = go_ref[rows, lo : lo + HEAD_DIM].astype(F32)
+            delta = jnp.sum(go * o_ref[rows, lo : lo + HEAD_DIM], axis=1, keepdims=True)
+            lane = lax.broadcasted_iota(jnp.int32, (TILE, LANES), 1)
+            full = jnp.where(lane < HEAD_DIM, head_first(go_ref[rows, :], h), 0.0)
+            for p, piece in enumerate(split3(-delta)):
+                full = jnp.where(lane == HEAD_DIM + p, piece.astype(F32), full)
+            ga_ref[h, rows, :] = full.astype(BF)
+            kt_ref[h, :, rows] = ka_ref[h, rows, :].astype(F32).T.astype(BF)
+            return carry
+
+        lax.fori_loop(0, blocks, prepare, 0)
+        dq_ref[...] = jnp.zeros_like(dq_ref)
+
+        def one(kb, carry, h=h, lo=lo):
+            krows = pl.ds(pl.multiple_of(kb * TILE, TILE), TILE)
+            slope = coef_ref[h, 6]
+            ka = ka_ref[h, krows, :]
+            va = va_ref[h, krows, :]
+            kt = kt_ref[h, :HEAD_DIM, krows]
+            dv = jnp.zeros((TILE, LANES), F32)
+            dk = jnp.zeros((TILE, LANES), F32)
+            for t in range(blocks):
+                qb = lax.rem(kb + t, blocks)
+                rows = pl.ds(pl.multiple_of(qb * TILE, TILE), TILE)
+                ga = ga_ref[h, rows, :]
+                qa = qb_ref[h, (kb > qb).astype(jnp.int32), rows, :]
+                scores = mm(ka, qa, NT)
+                if t == 0:
+                    scores = scores - ahead_of(TILE, TILE, 0) * (2.0 * slope)
+                probs = jnp.exp(scores)
+                ds = (probs * mm(va, ga, NT)).astype(BF)
+                dv = dv + mm(probs.astype(BF), ga, NN)
+                dk = dk + mm(ds, qa, NN)
+                dq_ref[:, rows] += mm(kt, ds, NN)
+            dqkv_ref[krows, width + lo : width + lo + HEAD_DIM] = dk[:, :HEAD_DIM].astype(BF)
+            dqkv_ref[krows, 2 * width + lo : 2 * width + lo + HEAD_DIM] = dv[
+                :, :HEAD_DIM
+            ].astype(BF)
+            return carry
+
+        lax.fori_loop(0, blocks, one, 0)
+
+        def finish(b, carry, lo=lo):
+            rows = pl.ds(pl.multiple_of(b * TILE, TILE), TILE)
+            dqkv_ref[rows, lo : lo + HEAD_DIM] = (dq_ref[:, rows].T * 0.125).astype(BF)
+            return carry
+
+        lax.fori_loop(0, blocks, finish, 0)
+
+
+def attn_bwd(coefs, go, o, qb, ka, va):
+    seq_len = go.shape[0]
+    heads = coefs.shape[0]
+    width = heads * HEAD_DIM
+    return pl.pallas_call(
+        bwd_kernel,
+        out_shape=jax.ShapeDtypeStruct((seq_len, 3 * width), BF),
+        in_specs=[SMEM_SPEC] + [VMEM_SPEC] * 5,
+        out_specs=VMEM_SPEC,
+        scratch_shapes=[
+            pltpu.VMEM((heads, seq_len, LANES), BF),
+            pltpu.VMEM((HEAD_DIM, seq_len), F32),
+            pltpu.VMEM((heads, LANES, seq_len), BF),
+        ],
+        compiler_params=pltpu.CompilerParams(vmem_limit_bytes=36 * 2**20),
+        cost_estimate=pl.CostEstimate(
+            flops=40 * seq_len * seq_len * width,
+            bytes_accessed=10 * 2**20,
+            transcendentals=heads * seq_len * seq_len,
+        ),
+        name="attn_bwd",
+    )(coefs, go, o, qb, ka, va)
+
+
+def ffn_kernel(nf_ref, cot_ref, up_ref, down_ref, mix_in, gnf_in, mix_ref, gnf_ref, gwd_ref, gwu_ref):
+    @pl.when(pl.program_id(0) == 0)
+    def _():
+        mix_ref[...] = mix_in[...]
+        gnf_ref[...] = gnf_in[...]
+
+    nf = nf_ref[...]
+    cot = cot_ref[...]
+    up = up_ref[...]
+    down = down_ref[...]
+    pre = mm(nf, up, NN)
+    phi = 0.5 + 0.5 * lax.erf(pre * math.sqrt(0.5))
+    activ = (pre * phi).astype(BF)
+    slope = phi + pre * (jnp.exp(-0.5 * pre * pre) * (1.0 / math.sqrt(2.0 * math.pi)))
+    grad_pre = (slope * mm(cot, down, NT)).astype(BF)
+    mix_ref[...] += mm(activ, down, NN)
+    gnf_ref[...] += mm(grad_pre, up, NT)
+    shards, _, cols = gwd_ref.shape
+    gwd = mm(activ, cot, TN).astype(BF)
+    for s in range(shards):
+        gwd_ref[s] = gwd[:, s * cols : (s + 1) * cols]
+    gwu = mm(nf, grad_pre, TN).astype(BF)
+    for j in range(gwu_ref.shape[1]):
+        gwu_ref[0, j] = gwu[:, j * cols : (j + 1) * cols]
+
+
+def ffn_part(nf, cot, w_up, w_down, mix, gnf, shards, parts, part):
+    rows, width = nf.shape
+    ff = w_up.shape[1]
+    tile = ff // (shards * parts)
+    cols = width // shards
+    whole = pl.BlockSpec((rows, width), lambda d: (0, 0))
+    return pl.pallas_call(
+        ffn_kernel,
+        grid=(shards,),
+        out_shape=(
+            jax.ShapeDtypeStruct((rows, width), F32),
+            jax.ShapeDtypeStruct((rows, width), F32),
+            jax.ShapeDtypeStruct((shards, shards * tile, cols), BF),
+            jax.ShapeDtypeStruct((shards, tile // cols, width, cols), BF),
+        ),
+        in_specs=[
+            whole,
+            whole,
+            pl.BlockSpec((width, tile), lambda d: (0, d * parts + part)),
+            pl.BlockSpec((tile, width), lambda d: (d * parts + part, 0)),
+            whole,
+            whole,
+        ],
+        out_specs=(
+            whole,
+            whole,
+            pl.BlockSpec((shards, tile, cols), lambda d: (0, d, 0)),
+            pl.BlockSpec((1, tile // cols, width, cols), lambda d: (d, 0, 0, 0)),
+        ),
+        compiler_params=pltpu.CompilerParams(vmem_limit_bytes=40 * 2**20),
+        cost_estimate=pl.CostEstimate(
+            flops=12 * rows * width * tile * shards,
+            bytes_accessed=8 * width * tile * shards,
+            transcendentals=2 * rows * tile * shards,
+        ),
+        name="ffn",
+    )(nf, cot, w_up, w_down, mix, gnf)
+
+
+def add_low(left, right):
+    return (left.astype(F32) + right.astype(F32)).astype(BF)
+
+
+def pick(array, index, axis):
+    return lax.dynamic_index_in_dim(array, index, axis, keepdims=False)
+
+
+BOTH = ("dp", "blk")
+CORE_SWAP = [(i, i ^ 1) for i in range(8)]
+X_SWAP = [(i, i ^ 1) for i in range(4)]
+Y_SWAP = [(i, i ^ 2) for i in range(4)]
+Z_STEPS = [[(i, (i + 2 * k) % 8) for i in range(8)] for k in (1, 2, 3)]
+
+
+def scatter_grad(share):
+    shards, rows, cols = share.shape
+    part = rows // 16
+    blk = lax.axis_index("blk")
+    core, level = blk % 2, blk // 2
+    dp = lax.axis_index("dp")
+    at_x, at_y = dp % 2, dp // 2
+    share = share.reshape(2, 2, 4, 2, 2, part, cols)
+    came = lax.ppermute(pick(share, 1 - core, 3), "blk", CORE_SWAP)
+    share = add_low(pick(share, core, 3), came)
+    x_first, y_first = share[:, :, :, 0], share[:, :, :, 1]
+    came_x = lax.ppermute(pick(x_first, 1 - at_x, 1), "dp", X_SWAP)
+    came_y = lax.ppermute(pick(y_first, 1 - at_y, 0), "dp", Y_SWAP)
+    x_first = add_low(pick(x_first, at_x, 1), came_x)
+    y_first = add_low(pick(y_first, at_y, 0), came_y)
+    came_y = lax.ppermute(pick(x_first, 1 - at_y, 0), "dp", Y_SWAP)
+    came_x = lax.ppermute(pick(y_first, 1 - at_x, 0), "dp", X_SWAP)
+    x_first = add_low(pick(x_first, at_y, 0), came_y)
+    y_first = add_low(pick(y_first, at_x, 0), came_x)
+    both = jnp.stack([x_first, y_first], axis=1)
+    total = pick(both, level, 0).astype(F32)
+    for k in (1, 2, 3):
+        total = total + lax.ppermute(
+            pick(both, (level + k) % 4, 0), "blk", Z_STEPS[k - 1]
+        ).astype(F32)
+    return total.astype(BF).reshape(2 * part, cols)
+
+
+def gather_grads(pieces):
+    sizes = [piece.shape[0] for piece in pieces]
+    joined = jnp.concatenate(pieces, axis=0) if len(pieces) > 1 else pieces[0]
+    whole = lax.all_gather(joined, "blk", axis=0, tiled=False)
+    out, at = [], 0
+    for size in sizes:
+        out.append(whole[:, at : at + size].reshape(8 * size, -1).astype(F32))
+        at += size
+    return out
+
+
+def sum_everywhere(values):
+    for axis, perm in (("blk", CORE_SWAP), ("dp", X_SWAP), ("dp", Y_SWAP)):
+        values = values + lax.ppermute(values, axis, perm)
+    parts = [lax.ppermute(values, "blk", perm) for perm in Z_STEPS]
+    return values + parts[0] + parts[1] + parts[2]
+
+
+def heads_to_columns(slab):
+    blk = lax.axis_index("blk")
+    core, level = blk % 2, blk // 2
+    dp = lax.axis_index("dp")
+    rows = slab.shape[0] // 2
+    halves = [slab[:rows], slab[rows:]]
+    for first, half in ((0, 0), (1, 1)):
+        mask = 1
+        value = halves[half]
+        done = 0
+        for bit in ((1, 2) if first == 0 else (2, 1)):
+            pairs = [
+                (p * 8 + b, (p ^ bit) * 8 + b)
+                for p in range(4)
+                for b in range(8)
+                if ((p ^ (b // 2)) & bit) and not ((p ^ (b // 2)) & done)
+            ]
+            value = add_low(value, lax.ppermute(value, BOTH, pairs))
+            done |= bit
+        halves[half] = value
+    total = jnp.concatenate(halves, axis=0)
+    mine = jnp.where(dp == level, total, jnp.zeros_like(total))
+    for k in (1, 2, 3):
+        pairs = [
+            (d * 8 + d * 2 + c, d * 8 + ((d + k) % 4) * 2 + c) for d in range(4) for c in range(2)
+        ]
+        mine = mine + lax.ppermute(total, BOTH, pairs)
+    other = lax.ppermute(mine, "blk", CORE_SWAP)
+    return jnp.where(core == 0, mine, other), jnp.where(core == 0, other, mine)
+
+
+def norm_stats(values):
+    centred = values - jnp.mean(values, axis=-1, keepdims=True)
+    scale = lax.rsqrt(jnp.mean(centred * centred, axis=-1, keepdims=True) + NORM_EPS)
+    return centred * scale, scale
+
+
+def norm_back(grad, xhat, scale, gain):
+    scaled = grad * gain
+    inner = jnp.mean(scaled * xhat, axis=-1, keepdims=True)
+    rows = scale * (scaled - jnp.mean(scaled, axis=-1, keepdims=True) - xhat * inner)
+    return rows, jnp.sum(grad * xhat, axis=0)
+
+
+def on_device_grid(
+    frames,
+    skip_feats,
+    w_skip,
+    gain_attn,
+    w_query,
+    w_key,
+    w_value,
+    w_output,
+    gain_ffn,
+    w_up,
+    w_down,
+    cotangent,
+    utt_lengths,
+    padded_lengths,
+):
+    row_count, width = frames.shape
+    blocks = lax.axis_size("blk")
+    shards = lax.axis_size("dp")
+    seq_len = row_count * blocks
+    pair = width // blocks
+    blk = lax.axis_index("blk")
+    dp = lax.axis_index("dp")
+
+    joined = jnp.concatenate([frames, skip_feats], axis=1)
+    hidden = product("rc,cd->rd", joined, w_skip)
+    xhat_attn, scale_attn = norm_stats(hidden)
+    normed = (xhat_attn * gain_attn).astype(BF)
+    normed_all = lax.all_gather(normed, "blk", axis=0, tiled=True)
+
+    slopes = lax.dynamic_slice_in_dim(alibi_slopes(seq_len), blk * 2, 2, 0)
+    coefs, qx, kx = attn_tables(utt_lengths[0], padded_lengths[0], slopes, seq_len)
+    w_mine = jnp.concatenate(
+        [lax.dynamic_slice_in_dim(w, blk * pair, pair, 1) for w in (w_query, w_key, w_value)],
+        axis=1,
+    )
+    qkv = product("rd,de->re", normed_all, w_mine).astype(BF)
+    attn_wide, attn_low, qb, ka, va = attn_fwd(coefs, qkv, qx, kx)
+
+    def to_rows(values):
+        k = values.shape[1]
+        came = lax.all_to_all(values.reshape(blocks, row_count, k), "blk", 0, 0, tiled=True)
+        return came
+
+    attn = to_rows(attn_low).transpose(1, 0, 2).reshape(row_count, width)
+    residual = hidden + product("rd,de->re", attn, w_output)
+    xhat_ffn, scale_ffn = norm_stats(residual)
+    normed_ffn = (xhat_ffn * gain_ffn).astype(BF)
+
+    mix, gnf = residual, jnp.zeros_like(residual)
+    parts = 2
+    scattered = []
+    for part in range(parts):
+        mix, gnf, gwd, gwu = ffn_part(
+            normed_ffn, cotangent, w_up, w_down, mix, gnf, shards, parts, part
+        )
+        scattered.append(scatter_grad(gwd))
+        scattered.append(scatter_grad(gwu.reshape(shards, -1, gwu.shape[-1])))
+    mixed = mix.astype(BF)
+
+    rows_ffn, grad_gain_ffn = norm_back(gnf, xhat_ffn, scale_ffn, gain_ffn)
+    grad_residual = cotangent.astype(F32) + rows_ffn
+    grad_branch = grad_residual.astype(BF)
+    grad_attn = product("re,de->rd", grad_branch, w_output).astype(BF)
+    grad_attn = lax.all_to_all(
+        grad_attn.reshape(row_count, blocks, pair).transpose(1, 0, 2), "blk", 0, 0, tiled=True
+    ).reshape(seq_len, pair)
+    grad_w_output = product("rd,rse->sde", attn, grad_branch.reshape(row_count, shards, -1))
+    scattered.append(scatter_grad(grad_w_output.astype(BF)))
+
+    dqkv = attn_bwd(coefs, grad_attn, attn_wide, qb, ka, va)
+    slab = product("rd,re->de", normed_all, dqkv).astype(BF)
+    came = to_rows(dqkv)
+    grad_normed = jnp.zeros_like(hidden)
+    for i, w in enumerate((w_query, w_key, w_value)):
+        part = came[:, :, i * pair : (i + 1) * pair].transpose(1, 0, 2).reshape(row_count, width)
+        grad_normed = grad_normed + product("re,de->rd", part, w)
+    first, second = heads_to_columns(slab)
+
+    rows_attn, grad_gain_attn = norm_back(grad_normed, xhat_attn, scale_attn, gain_attn)
+    grad_hidden = (grad_residual + rows_attn).astype(BF)
+    grad_w_skip = product("rc,rse->sce", joined, grad_hidden.reshape(row_count, shards, -1))
+    skip_piece = scatter_grad(grad_w_skip.astype(BF))
+    gains = jnp.concatenate([grad_gain_attn, grad_gain_ffn]).reshape(16, -1)
+    gains = sum_everywhere(gains).reshape(2, shards, -1)
+    gains = pick(gains, dp, 1)
+
+    grad_joined = product("rd,cd->rc", grad_hidden, w_skip)
+    grad_frames = grad_joined[:, :width].astype(BF)
+    grad_skip = grad_joined[:, width:].astype(BF)
+
+    early = gather_grads(scattered[:2])
+    late = gather_grads(scattered[2:])
+    (g_skip,) = gather_grads([skip_piece])
+    downs = [early[0], late[0]]
+    ups = [early[1], late[1]]
+    cols = width // shards
+    g_down = jnp.stack([d.reshape(shards, -1, cols) for d in downs], axis=1).reshape(-1, cols)
+    g_up = jnp.concatenate(
+        [u.reshape(-1, width, cols)[j] for u in ups for j in range(u.shape[0] // width)], axis=1
+    )
+    g_output = late[2]
+    g_heads = [
+        jnp.concatenate(
+            [piece[:, i * pair : (i + 1) * pair] for piece in (first, second)], axis=1
+        ).astype(F32)
+        for i in range(3)
+    ]
+    return (
+        mixed,
+        grad_frames,
+        grad_skip,
+        g_skip,
+        gains[0],
+        g_heads[0],
+        g_heads[1],
+        g_heads[2],
+        g_output,
+        gains[1],
+        g_up,
+        g_down,
+    )
+
+
 def solution(mesh):
+    shape = dict(mesh.shape)
+    grid = (shape["dp"], shape["blk"])
+    body = on_device_grid if grid == (4, 8) else on_device_general
     return jax.shard_map(
-        on_device,
+        body,
         mesh=mesh,
         in_specs=(
             P(("dp", "blk"), None),

time: 1100 us -> 562 us (0.51)
  waiting for transfers between devices: 682 us -> 198 us
  matrix products: 227 us -> 28.1 us
  starting transfers between devices: 2.68 us -> 102 us
  Pallas kernels: 0 us -> 73.3 us
  local copies, waits for them, and re-layouts: 48.3 us -> 87.7 us
  other arithmetic: 86.4 us -> 48 us
  blocking collectives: 24.2 us -> 0 us
    reduce_scatter x7 -> x0, waiting for transfers between devices: 340 us -> none  [the longest x1 89.8 us: on_device(): lax.psum_scatter(grad_w_up.astype(jnp.bfloat16), 'dp', scatter_dimension=...]
    dot_general x69 -> x11, matrix products: 227 us -> 28.1 us  [product(): return jnp.einsum(form, left, right, preferred_element_type=jnp.float32)]
    psum x1 -> x0, waiting for transfers between devices: 123 us -> none  [on_device(): lax.psum(shares[0].astype(jnp.bfloat16), 'blk').astype(jnp.float32)]
    ppermute x32 -> x62, starting transfers between devices: 1.43 us -> 89.3 us  [the longest x18 47.8 us: scatter_grad(): lax.ppermute(pick(both, (level + k) % 4, 0), 'blk', Z_STEPS[k - 1])]
    pallas_call x0 -> x5, Pallas kernels: none -> 73.3 us  [the longest x1 26.6 us: attn_bwd(): pl.pallas_call(bwd_kernel, out_shape=jax.ShapeDtypeStruct((seq_len, 3 * w...]
    all_gather x2 -> x4, waiting for transfers between devices: 93 us -> 54 us  [the longest x1 42.1 us: on_device_grid(): normed_all = lax.all_gather(normed, 'blk', axis=0, tiled=True)]
    while x76 -> x0, local copies, waits for them, and re-layouts: 32.1 us -> none
    convert_element_type x45 -> x37, other arithmetic: 58.9 us -> 30.4 us  [the longest x21 13.7 us: add_low(): return (left.astype(F32) + right.astype(F32)).astype(BF)]
  transfers between devices with their start and end apart: 42 -> 69, of which waited for: 41 -> 28; matrix products, arithmetic and copies ran while one was open for 13% -> 20% of each run, Pallas kernels for 0% -> 5%
where the time goes in v1:
time: 562 us; the launch traced here: 552 us
  waiting for transfers between devices  198 us (35%)
  starting transfers between devices  102 us (18%)
  local copies, waits for them, and re-layouts  87.7 us (16%)
  Pallas kernels  73.3 us (13%)
  other arithmetic  48 us (9%)
  matrix products  28.1 us (5%)
  between operations  15.8 us (3%)
    ppermute x18, starting transfers between devices, scatter_grad(): lax.ppermute(pick(both, (level + k) % 4, 0), 'blk', Z_STEPS[k - 1])  47.8 us
    ppermute x3, waiting for transfers between devices, heads_to_columns(): mine = mine + lax.ppermute(total, BOTH, pairs)  47.5 us
    all_gather x1, waiting for transfers between devices, on_device_grid(): normed_all = lax.all_gather(normed, 'blk', axis=0, tiled=True)  42.1 us
    unnamed x114, local copies, waits for them, and re-layouts  33 us
    ppermute x6, waiting for transfers between devices, scatter_grad(): came_x = lax.ppermute(pick(x_first, 1 - at_x, 1), 'dp', X_SWAP)  31.8 us
    dot_general x11, matrix products, product(): return jnp.einsum(form, left, right, preferred_element_type=jnp.float32)  28.1 us
    pallas_call x1, Pallas kernels, attn_bwd(): pl.pallas_call(bwd_kernel, out_shape=jax.ShapeDtypeStruct((seq_len, 3 * w...  26.6 us
    pallas_call x1, Pallas kernels, attn_fwd(): pl.pallas_call(fwd_kernel, out_shape=(jax.ShapeDtypeStruct((seq_len, widt...  24.2 us
  transfers between devices with their start and end apart: 69, of which 28 were waited for; matrix products, arithmetic and copies ran while one was open for 20% of the time, Pallas kernels for 5%

profile of v1, /device:TPU:0, one launch (start us, length us, event | category | flops | bytes accessed | tf_op | source)
XLA Modules:
  0.0 552.3 jit_solution(13902862763189917938)
XLA Ops:
  9.6 3.9 fusion.137
  16.6 3.4 attn_tables.1
  23.4 42.1 %all-gather.7.cloned.1.call-done = bf16[2048,1024]{1,0:T(8,128)(2,1)} async-done(((bf16[256,1024]{1,0:T(8,128)(2,1)}), bf16[2048,1024]{1,0:T(8,128)(2,1)}) %all-gather.7.cloned.1.call-update) | async-done | bytes 4194320 | tf_op jit(solution)/shard_map/all_gather | solution.py:728
  65.5 4.7 convolution_convert_fusion.qkv_ref
  70.2 24.2 %attn_fwd.1 = (f32[2048,128]{1,0:T(8,128)S(1)}, bf16[2048,128]{1,0:T(8,128)(2,1)}, bf16[2,2,2048,128]{3,2,1,0:T(8,128)(2,1)S(1)}, bf16[2,2048,128]{2,1,0:T(8,128)(2,1)S(1)}, bf16[2,2048,128]{2,1,0:T(8,128)(2,1)S(1)}) custom-call(f32[2,7]{1,0:T(2,128)S(1)} %stack.95.slope_ref.coef_ref, bf16[2048,384]{1,0:T(8,128)(2,1)S(1)} %convolution_convert_fusion.qkv_ref, ...), custom_call_target="tpu_custom_call" | custom-call | flops 8589934592 | bytes 10485760 | tf_op jit(solution)/shard_map/attn_fwd/pallas_call | solution.py:424
  98.7 3.7 all-to-all-start
  102.6 15.1 %all-to-all-done = bf16[8,256,128]{2,1,0:T(8,128)(2,1)S(1)} async-done(((bf16[8,256,128]{2,1,0:T(8,128)(2,1)}), bf16[8,256,128]{2,1,0:T(8,128)(2,1)S(1)}, u32[]{:S(2)}, u32[]{:S(2)}) %all-to-all-start) | async-done | bytes 524320 | tf_op jit(solution)/shard_map/all_to_all | solution.py:741
  117.7 2.2 fusion.138
  121.0 9.5 %ffn.2 = (f32[256,1024]{1,0:T(8,128)S(1)}, f32[256,1024]{1,0:T(8,128)S(1)}, bf16[4,2048,256]{2,1,0:T(8,128)(2,1)S(1)}, bf16[4,2,1024,256]{3,2,1,0:T(8,128)(2,1)S(1)}) custom-call(bf16[256,1024]{1,0:T(8,128)(2,1)S(1)} %multiply_convert_fusion.nf_ref, bf16[256,1024]{1,0:T(8,128)(2,1)S(1)} %copy-done.16, bf16[1024,4096]{1,0:T(8,128)(2,1)} %up_ref.3, ...), custom_call_target="tpu_custom_call" | custom-call | flops 6442450944 | bytes 16777216 | tf_op jit(solution)/shard_map/ffn/pallas_call | solution.py:562
  134.5 9.6 %ffn.3 = (f32[256,1024]{1,0:T(8,128)S(1)}, f32[256,1024]{1,0:T(8,128)S(1)}, bf16[4,2048,256]{2,1,0:T(8,128)(2,1)S(1)}, bf16[4,2,1024,256]{3,2,1,0:T(8,128)(2,1)S(1)}) custom-call(bf16[256,1024]{1,0:T(8,128)(2,1)S(1)} %multiply_convert_fusion.nf_ref, bf16[256,1024]{1,0:T(8,128)(2,1)S(1)} %copy-done.16, bf16[1024,4096]{1,0:T(8,128)(2,1)} %up_ref.3, ...), custom_call_target="tpu_custom_call" | custom-call | flops 6442450944 | bytes 16777216 | tf_op jit(solution)/shard_map/ffn/pallas_call | solution.py:562
  150.7 2.6 fusion.6
  155.2 3.9 all-to-all-start.1
  159.1 3.3 dynamic-slice_bitcast_fusion
  166.5 3.9 copy.79
  170.4 2.3 dynamic-slice_bitcast_fusion.4
  173.2 3.2 dynamic-slice_bitcast_fusion.3
  183.4 26.6 %attn_bwd.1 = bf16[2048,384]{1,0:T(8,128)(2,1)S(1)} custom-call(f32[2,7]{1,0:T(2,128)S(1)} %stack.95.slope_ref.coef_ref, bf16[2048,128]{1,0:T(8,128)(2,1)S(1)} %bitcast.373, f32[2048,128]{1,0:T(8,128)S(1)} %copy-done.22, bf16[2,2,2048,128]{3,2,1,0:T(8,128)(2,1)S(1)} %copy-done.20, bf16[2,2048,128]{2,1,0:T(8,128)(2,1)S(1)} %copy-done.24, ...), custom_call_target="tpu_custom_call" | custom-call | flops 21474836480 | bytes 10485760 | tf_op jit(solution)/shard_map/attn_bwd/pallas_call | solution.py:510
  210.1 2.4 convolution_convert_fusion.2
  218.4 5.0 collective-permute-done.39
  225.0 10.4 %collective-permute-done.41 = bf16[2,4,64,256]{3,2,1,0:T(8,128)(2,1)S(1)} collective-permute-done((bf16[2,4,64,256]{3,2,1,0:T(8,128)(2,1)S(1)}, bf16[2,4,64,256]{3,2,1,0:T(8,128)(2,1)S(1)}, u32[]{:S(2)}, u32[]{:S(2)}) %collective-permute-start.41) | collective-permute-done | bytes 262176 | tf_op jit(solution)/shard_map/ppermute | solution.py:622
  235.5 4.9 collective-permute-done.40
  240.4 2.4 collective-permute-start.42
  242.8 2.9 collective-permute-done.42
  246.4 2.5 collective-permute-start.43
  250.5 5.2 collective-permute-start.44
  260.4 4.4 all-to-all-start.2
  269.7 8.6 %collective-permute-done.17 = bf16[512,384]{1,0:T(8,128)(2,1)S(1)} collective-permute-done((bf16[512,384]{1,0:T(8,128)(2,1)S(1)}, bf16[512,384]{1,0:T(8,128)(2,1)S(1)}, u32[]{:S(2)}, u32[]{:S(2)}) %collective-permute-start.17) | collective-permute-done | bytes 393248 | tf_op jit(solution)/shard_map/ppermute | solution.py:673
  281.3 2.3 fusion
  285.8 2.3 fusion.1
  294.2 14.0 %collective-permute-done.19 = bf16[1024,384]{1,0:T(8,128)(2,1)S(1)} collective-permute-done((bf16[1024,384]{1,0:T(8,128)(2,1)S(1)}, bf16[1024,384]{1,0:T(8,128)(2,1)S(1)}, u32[]{:S(2)}, u32[]{:S(2)}) %collective-permute-start.19) | collective-permute-done | bytes 786464 | tf_op jit(solution)/shard_map/ppermute | solution.py:682
  308.2 16.8 %collective-permute-done.18 = bf16[1024,384]{1,0:T(8,128)(2,1)S(1)} collective-permute-done((bf16[1024,384]{1,0:T(8,128)(2,1)S(1)}, bf16[1024,384]{1,0:T(8,128)(2,1)S(1)}, u32[]{:S(2)}, u32[]{:S(2)}) %collective-permute-start.18) | collective-permute-done | bytes 786464 | tf_op jit(solution)/shard_map/ppermute | solution.py:682
  325.1 16.6 %collective-permute-done.20 = bf16[1024,384]{1,0:T(8,128)(2,1)S(1)} collective-permute-done((bf16[1024,384]{1,0:T(8,128)(2,1)S(1)}, bf16[1024,384]{1,0:T(8,128)(2,1)S(1)}, u32[]{:S(2)}, u32[]{:S(2)}) %collective-permute-start.20) | collective-permute-done | bytes 786464 | tf_op jit(solution)/shard_map/ppermute | solution.py:682
  342.4 2.1 collective-permute-start.23
  344.7 2.1 collective-permute-start.25
  347.1 9.4 %collective-permute-done.31 = bf16[2,4,128,256]{3,2,1,0:T(8,128)(2,1)S(1)} collective-permute-done((bf16[2,4,128,256]{3,2,1,0:T(8,128)(2,1)S(1)}, bf16[2,4,128,256]{3,2,1,0:T(8,128)(2,1)S(1)}, u32[]{:S(2)}, u32[]{:S(2)}) %collective-permute-start.31) | collective-permute-done | bytes 524320 | tf_op jit(solution)/shard_map/ppermute | solution.py:621
  359.2 8.5 %collective-permute-done.23 = bf16[2,4,128,256]{3,2,1,0:T(8,128)(2,1)S(1)} collective-permute-done((bf16[2,4,128,256]{3,2,1,0:T(8,128)(2,1)S(1)}, bf16[2,4,128,256]{3,2,1,0:T(8,128)(2,1)S(1)}, u32[]{:S(2)}, u32[]{:S(2)}) %collective-permute-start.23) | collective-permute-done | bytes 524320 | tf_op jit(solution)/shard_map/ppermute | solution.py:621
  368.3 2.1 collective-permute-start.50
  371.3 2.6 collective-permute-done.56
  374.0 2.1 collective-permute-start.34
  376.2 3.3 collective-permute-done.48
  379.6 2.1 collective-permute-start.26
  381.9 3.3 collective-permute-done.32
  385.2 4.9 collective-permute-start.60
  390.2 3.7 collective-permute-start.61
  398.9 9.1 %collective-permute-start.53 = (bf16[2,128,256]{2,1,0:T(8,128)(2,1)S(1)}, bf16[2,128,256]{2,1,0:T(8,128)(2,1)S(1)}, u32[]{:S(2)}, u32[]{:S(2)}) collective-permute-start(bf16[2,128,256]{2,1,0:T(8,128)(2,1)S(1)} %get-tuple-element.95), channel_id=1, source_target_pairs={{0,6},{1,7},{2,0},{3,1},{4,2},{5,3},{6,4},{7,5},{8,14},{9,15},{10,... | collective-permute-start | bytes 393224 | tf_op jit(solution)/shard_map/ppermute | solution.py:632
  410.3 2.4 collective-permute-done.53
  412.7 7.4 %collective-permute-start.37 = (bf16[2,128,256]{2,1,0:T(8,128)(2,1)S(1)}, bf16[2,128,256]{2,1,0:T(8,128)(2,1)}, u32[]{:S(2)}, u32[]{:S(2)}) collective-permute-start(bf16[2,128,256]{2,1,0:T(8,128)(2,1)S(1)} %get-tuple-element.104), channel_id=1, source_target_pairs={{0,6},{1,7},{2,0},{3,1},{4,2},{5,3},{6,4},{7,5},{8,14},{9,15},{10,... | collective-permute-start | bytes 393224 | tf_op jit(solution)/shard_map/ppermute | solution.py:632
  425.1 2.6 fusion.139
  433.2 4.5 convert_bitcast_fusion
  437.7 7.7 %reshape.328 = bf16[2,2,4,2,2,128,256]{5,4,3,2,6,1,0:T(2,128)(2,1)} reshape(bf16[4,2048,256]{1,2,0:T(8,128)(2,1)} %convert_bitcast_fusion) | data formatting | bytes 8388608 | tf_op jit(solution)/shard_map/reshape | solution.py:617
  445.5 6.4 %constant_dynamic-slice_fusion.3 = (bf16[2,2,4,1,2,128,256]{5,4,3,2,6,1,0:T(2,128)(2,1)S(1)}, bf16[2,2,4,1,2,128,256]{5,4,3,2,6,1,0:T(2,128)(2,1)}) fusion(bf16[2,2,4,2,2,128,256]{5,4,3,2,6,1,0:T(2,128)(2,1)} %reshape.328, s32[]{:T(128)S(6)} %select_n.240, s32[]{:T(128)S(6)} %select_n.241), kind=kLoop, calls=%fused_computation.277 | loop fusion | bytes 8388616 | tf_op jit(solution)/shard_map/jit(dynamic_index_in_dim)/dynamic_slice | solution.py:600
  451.9 6.1 %copy.75 = bf16[2,2,4,1,2,128,256]{6,5,2,0,4,1,3:T(8,128)(2,1)} copy(bf16[2,2,4,1,2,128,256]{5,4,3,2,6,1,0:T(2,128)(2,1)} %get-tuple-element.55) | data formatting | bytes 4194304 | tf_op jit(solution)/shard_map/jit(dynamic_index_in_dim)/dynamic_slice | solution.py:600
  459.6 2.8 collective-permute-start.29
  472.3 4.1 copy.85
  476.5 3.0 fusion.4
  479.7 2.1 collective-permute-start.1
  485.3 8.8 %collective-permute-done.1 = bf16[2,4,128,256]{3,2,1,0:T(8,128)(2,1)S(1)} collective-permute-done((bf16[2,4,128,256]{3,2,1,0:T(8,128)(2,1)S(1)}, bf16[2,4,128,256]{3,2,1,0:T(8,128)(2,1)S(1)}, u32[]{:S(2)}, u32[]{:S(2)}) %collective-permute-start.1) | collective-permute-done | bytes 524320 | tf_op jit(solution)/shard_map/ppermute | solution.py:621
  498.9 3.8 collective-permute-start.13
  503.8 2.7 collective-permute-start.5
  512.3 3.6 collective-permute-done.6
  524.6 2.7 pad_maximum_fusion
  528.3 2.5 bitcast_convert_fusion
  530.8 11.8 %all-gather.9.cloned.1.call-done = bf16[8,256,256]{2,1,0:T(8,128)(2,1)} async-done(((bf16[1,256,256]{2,1,0:T(8,128)(2,1)}), bf16[8,256,256]{2,1,0:T(8,128)(2,1)}) %all-gather.9.cloned.1.call-update) | async-done | bytes 1048592 | tf_op jit(solution)/shard_map/all_gather | solution.py:641
  542.6 2.7 bitcast_convert_fusion.1
  (362 shorter events, 128.3 us)
Async XLA Ops:
  7.2 58.3 %all-gather.7.cloned.1.call-start = ((), (), s32[]{:S(2)}) async-start(), calls=%async_computation.3 | async-start | bytes 4718592 | tf_op jit(solution)/shard_map/all_gather | solution.py:728
  98.7 19.0 %all-to-all-start = ((bf16[8,256,128]{2,1,0:T(8,128)(2,1)}), bf16[8,256,128]{2,1,0:T(8,128)(2,1)S(1)}, u32[]{:S(2)}, u32[]{:S(2)}) async-start(bf16[8,256,128]{2,1,0:T(8,128)(2,1)} %bitcast.7), calls=%async_computation | async-start | bytes 1048576 | tf_op jit(solution)/shard_map/all_to_all | solution.py:741
  155.2 21.1 %all-to-all-start.1 = ((bf16[8,256,128]{2,1,0:T(8,128)(2,1)}), bf16[8,256,128]{2,1,0:T(8,128)(2,1)S(1)}, u32[]{:S(2)}, u32[]{:S(2)}) async-start(bf16[8,256,128]{2,1,0:T(8,128)(2,1)} %bitcast.363), calls=%async_computation.1 | async-start | bytes 1048576 | tf_op jit(solution)/shard_map/all_to_all | solution.py:764
  162.4 117.4 %collective-permute-start.54 = (bf16[2,2,4,2,128,256]{5,4,3,2,1,0:T(8,128)(2,1)}, bf16[2,2,4,2,128,256]{5,4,3,2,1,0:T(8,128)(2,1)}, u32[]{:S(2)}, u32[]{:S(2)}) collective-permute-start(bf16[2,2,4,2,128,256]{5,4,3,2,1,0:T(8,128)(2,1)} %dynamic-slice_bitcast_fusion), channel_id=1, source_target_pairs={{0,1},{1,0},{2,3},{3,2},{4,5},{5,4},{6,7},{7,6},{8,9},{9,8},{10,11... | collective-permute-start | bytes 6291464 | tf_op jit(solution)/shard_map/ppermute | solution.py:618
  164.3 119.5 %collective-permute-start.46 = (bf16[2,2,4,2,128,256]{5,4,3,2,1,0:T(8,128)(2,1)}, bf16[2,2,4,2,128,256]{5,4,3,2,1,0:T(8,128)(2,1)}, u32[]{:S(2)}, u32[]{:S(2)}) collective-permute-start(bf16[2,2,4,2,128,256]{5,4,3,2,1,0:T(8,128)(2,1)} %dynamic-slice_bitcast_fusion.1), channel_id=1, source_target_pairs={{0,1},{1,0},{2,3},{3,2},{4,5},{5,4},{6,7},{7,6},{8,9},{9,8},{10,11... | collective-permute-start | bytes 6291464 | tf_op jit(solution)/shard_map/ppermute | solution.py:618
  172.7 39.7 %collective-permute-start.38 = (bf16[2,2,4,2,64,256]{5,4,3,2,1,0:T(8,128)(2,1)}, bf16[2,2,4,2,64,256]{5,4,3,2,1,0:T(8,128)(2,1)}, u32[]{:S(2)}, u32[]{:S(2)}) collective-permute-start(bf16[2,2,4,2,64,256]{5,4,3,2,1,0:T(8,128)(2,1)} %dynamic-slice_bitcast_fusion.4), channel_id=1, source_target_pairs={{0,1},{1,0},{2,3},{3,2},{4,5},{5,4},{6,7},{7,6},{8,9},{9,8},{10,11... | collective-permute-start | bytes 3145736 | tf_op jit(solution)/shard_map/ppermute | solution.py:618
  214.2 9.2 %collective-permute-start.39 = (bf16[2,4,64,256]{3,2,1,0:T(8,128)(2,1)S(1)}, bf16[2,4,64,256]{3,2,1,0:T(8,128)(2,1)S(1)}, u32[]{:S(2)}, u32[]{:S(2)}) collective-permute-start(bf16[2,4,64,256]{3,2,1,0:T(8,128)(2,1)S(1)} %dynamic-slice_bitcast_fusion.20), channel_id=1, source_target_pairs={{0,8},{8,0},{16,24},{24,16},{1,9},{9,1},{17,25},{25,17},{2,10},{10... | collective-permute-start | bytes 786440 | tf_op jit(solution)/shard_map/ppermute | solution.py:621
  215.8 33.2 %collective-permute-start.14 = (bf16[512,384]{1,0:T(8,128)(2,1)S(1)}, bf16[512,384]{1,0:T(8,128)(2,1)S(1)}, u32[]{:S(2)}, u32[]{:S(2)}) collective-permute-start(bf16[512,384]{1,0:T(8,128)(2,1)S(1)} %get-tuple-element.91), channel_id=1, source_target_pairs={{2,10},{3,11},{6,14},{7,15},{8,0},{9,1},{12,4},{13,5},{18,26},{19,... | collective-permute-start | bytes 1179656 | tf_op jit(solution)/shard_map/ppermute | solution.py:673
  217.1 31.9 %collective-permute-start.16 = (bf16[512,384]{1,0:T(8,128)(2,1)S(1)}, bf16[512,384]{1,0:T(8,128)(2,1)S(1)}, u32[]{:S(2)}, u32[]{:S(2)}) collective-permute-start(bf16[512,384]{1,0:T(8,128)(2,1)S(1)} %get-tuple-element.92), channel_id=1, source_target_pairs={{4,20},{5,21},{6,22},{7,23},{12,28},{13,29},{14,30},{15,31},{16,0}... | collective-permute-start | bytes 1179656 | tf_op jit(solution)/shard_map/ppermute | solution.py:673
  223.4 12.0 %collective-permute-start.41 = (bf16[2,4,64,256]{3,2,1,0:T(8,128)(2,1)S(1)}, bf16[2,4,64,256]{3,2,1,0:T(8,128)(2,1)S(1)}, u32[]{:S(2)}, u32[]{:S(2)}) collective-permute-start(bf16[2,4,64,256]{3,2,1,0:T(8,128)(2,1)S(1)} %dynamic-slice_bitcast_fusion.19), channel_id=1, source_target_pairs={{0,16},{8,24},{16,0},{24,8},{1,17},{9,25},{17,1},{25,9},{2,18},{10... | collective-permute-start | bytes 786440 | tf_op jit(solution)/shard_map/ppermute | solution.py:622
  246.4 9.3 %collective-permute-start.43 = (bf16[2,64,256]{2,1,0:T(8,128)(2,1)S(1)}, bf16[2,64,256]{2,1,0:T(8,128)(2,1)S(1)}, u32[]{:S(2)}, u32[]{:S(2)}) collective-permute-start(bf16[2,64,256]{2,1,0:T(8,128)(2,1)S(1)} %get-tuple-element.108), channel_id=1, source_target_pairs={{0,2},{1,3},{2,4},{3,5},{4,6},{5,7},{6,0},{7,1},{8,10},{9,11},{10,... | collective-permute-start | bytes 196616 | tf_op jit(solution)/shard_map/ppermute | solution.py:632
  249.2 19.3 %collective-permute-start.15 = (bf16[512,384]{1,0:T(8,128)(2,1)S(1)}, bf16[512,384]{1,0:T(8,128)(2,1)}, u32[]{:S(2)}, u32[]{:S(2)}) collective-permute-start(bf16[512,384]{1,0:T(8,128)(2,1)S(1)} %get-tuple-element.89), channel_id=1, source_target_pairs={{4,20},{5,21},{14,30},{15,31},{16,0},{17,1},{26,10},{27,11}} | collective-permute-start | bytes 1179656 | tf_op jit(solution)/shard_map/ppermute | solution.py:673
  250.5 14.4 %collective-permute-start.44 = (bf16[2,64,256]{2,1,0:T(8,128)(2,1)}, bf16[2,64,256]{2,1,0:T(8,128)(2,1)}, u32[]{:S(2)}, u32[]{:S(2)}) collective-permute-start(bf16[2,64,256]{2,1,0:T(8,128)(2,1)} %get-tuple-element.109), channel_id=1, source_target_pairs={{0,4},{1,5},{2,6},{3,7},{4,0},{5,1},{6,2},{7,3},{8,12},{9,13},{10,... | collective-permute-start | bytes 196616 | tf_op jit(solution)/shard_map/ppermute | solution.py:632
  255.7 9.5 %collective-permute-start.45 = (bf16[2,64,256]{2,1,0:T(8,128)(2,1)}, bf16[2,64,256]{2,1,0:T(8,128)(2,1)}, u32[]{:S(2)}, u32[]{:S(2)}) collective-permute-start(bf16[2,64,256]{2,1,0:T(8,128)(2,1)} %get-tuple-element.110), channel_id=1, source_target_pairs={{0,6},{1,7},{2,0},{3,1},{4,2},{5,3},{6,4},{7,5},{8,14},{9,15},{10,... | collective-permute-start | bytes 196616 | tf_op jit(solution)/shard_map/ppermute | solution.py:632
  260.4 163.2 %all-to-all-start.2 = ((bf16[8,256,384]{1,2,0:T(8,128)(2,1)}), bf16[8,256,384]{1,2,0:T(8,128)(2,1)}, u32[]{:S(2)}, u32[]{:S(2)}) async-start(bf16[8,256,384]{1,2,0:T(8,128)(2,1)} %copy.72), calls=%async_computation.2 | async-start | bytes 3145728 | tf_op jit(solution)/shard_map/all_to_all | solution.py:741
  264.8 251.8 %all-gather.13.cloned.1.call-start = ((), (), s32[]{:S(2)}) async-start(), calls=%async_computation.6 | async-start | bytes 2359296 | tf_op jit(solution)/shard_map/all_gather | solution.py:641
  264.9 23.5 %collective-permute-start.30 = (bf16[2,2,4,2,128,256]{5,4,3,2,1,0:T(8,128)(2,1)}, bf16[2,2,4,2,128,256]{5,4,3,2,1,0:T(8,128)(2,1)S(1)}, u32[]{:S(2)}, u32[]{:S(2)}) collective-permute-start(bf16[2,2,4,2,128,256]{5,4,3,2,1,0:T(8,128)(2,1)} %dynamic-slice_bitcast_fusion.2), channel_id=1, source_target_pairs={{0,1},{1,0},{2,3},{3,2},{4,5},{5,4},{6,7},{7,6},{8,9},{9,8},{10,11... | collective-permute-start | bytes 6291464 | tf_op jit(solution)/shard_map/ppermute | solution.py:618
  265.3 13.1 %collective-permute-start.17 = (bf16[512,384]{1,0:T(8,128)(2,1)S(1)}, bf16[512,384]{1,0:T(8,128)(2,1)S(1)}, u32[]{:S(2)}, u32[]{:S(2)}) collective-permute-start(bf16[512,384]{1,0:T(8,128)(2,1)S(1)} %get-tuple-element.90), channel_id=1, source_target_pairs={{2,10},{3,11},{8,0},{9,1},{22,30},{23,31},{28,20},{29,21}} | collective-permute-start | bytes 1179656 | tf_op jit(solution)/shard_map/ppermute | solution.py:673
  268.4 22.9 %collective-permute-start.22 = (bf16[2,2,4,2,128,256]{5,4,3,2,1,0:T(8,128)(2,1)}, bf16[2,2,4,2,128,256]{5,4,3,2,1,0:T(8,128)(2,1)S(1)}, u32[]{:S(2)}, u32[]{:S(2)}) collective-permute-start(bf16[2,2,4,2,128,256]{5,4,3,2,1,0:T(8,128)(2,1)} %dynamic-slice_bitcast_fusion.3), channel_id=1, source_target_pairs={{0,1},{1,0},{2,3},{3,2},{4,5},{5,4},{6,7},{7,6},{8,9},{9,8},{10,11... | collective-permute-start | bytes 6291464 | tf_op jit(solution)/shard_map/ppermute | solution.py:618
  278.5 29.7 %collective-permute-start.19 = (bf16[1024,384]{1,0:T(8,128)(2,1)S(1)}, bf16[1024,384]{1,0:T(8,128)(2,1)S(1)}, u32[]{:S(2)}, u32[]{:S(2)}) collective-permute-start(bf16[1024,384]{1,0:T(8,128)(2,1)S(1)} %pad_maximum_fusion.2), channel_id=1, source_target_pairs={{0,4},{1,5},{10,14},{11,15},{20,16},{21,17},{30,26},{31,27}} | collective-permute-start | bytes 2359304 | tf_op jit(solution)/shard_map/ppermute | solution.py:682
  279.9 45.2 %collective-permute-start.18 = (bf16[1024,384]{1,0:T(8,128)(2,1)S(1)}, bf16[1024,384]{1,0:T(8,128)(2,1)S(1)}, u32[]{:S(2)}, u32[]{:S(2)}) collective-permute-start(bf16[1024,384]{1,0:T(8,128)(2,1)S(1)} %pad_maximum_fusion.2), channel_id=1, source_target_pairs={{0,2},{1,3},{10,12},{11,13},{20,22},{21,23},{30,24},{31,25}} | collective-permute-start | bytes 2359304 | tf_op jit(solution)/shard_map/ppermute | solution.py:682
  283.8 57.9 %collective-permute-start.20 = (bf16[1024,384]{1,0:T(8,128)(2,1)S(1)}, bf16[1024,384]{1,0:T(8,128)(2,1)S(1)}, u32[]{:S(2)}, u32[]{:S(2)}) collective-permute-start(bf16[1024,384]{1,0:T(8,128)(2,1)S(1)} %pad_maximum_fusion.2), channel_id=1, source_target_pairs={{0,6},{1,7},{10,8},{11,9},{20,18},{21,19},{30,28},{31,29}} | collective-permute-start | bytes 2359304 | tf_op jit(solution)/shard_map/ppermute | solution.py:682
  288.3 53.8 %collective-permute-start.55 = (bf16[2,4,128,256]{3,2,1,0:T(8,128)(2,1)S(1)}, bf16[2,4,128,256]{3,2,1,0:T(8,128)(2,1)S(1)}, u32[]{:S(2)}, u32[]{:S(2)}) collective-permute-start(bf16[2,4,128,256]{3,2,1,0:T(8,128)(2,1)S(1)} %dynamic-slice_bitcast_fusion.6), channel_id=1, source_target_pairs={{0,8},{8,0},{16,24},{24,16},{1,9},{9,1},{17,25},{25,17},{2,10},{10... | collective-permute-start | bytes 1572872 | tf_op jit(solution)/shard_map/ppermute | solution.py:621
  291.3 51.1 %collective-permute-start.57 = (bf16[2,4,128,256]{3,2,1,0:T(8,128)(2,1)S(1)}, bf16[2,4,128,256]{3,2,1,0:T(8,128)(2,1)S(1)}, u32[]{:S(2)}, u32[]{:S(2)}) collective-permute-start(bf16[2,4,128,256]{3,2,1,0:T(8,128)(2,1)S(1)} %dynamic-slice_bitcast_fusion.5), channel_id=1, source_target_pairs={{0,16},{8,24},{16,0},{24,8},{1,17},{9,25},{17,1},{25,9},{2,18},{10... | collective-permute-start | bytes 1572872 | tf_op jit(solution)/shard_map/ppermute | solution.py:622
  308.2 36.4 %collective-permute-start.47 = (bf16[2,4,128,256]{3,2,1,0:T(8,128)(2,1)S(1)}, bf16[2,4,128,256]{3,2,1,0:T(8,128)(2,1)S(1)}, u32[]{:S(2)}, u32[]{:S(2)}) collective-permute-start(bf16[2,4,128,256]{3,2,1,0:T(8,128)(2,1)S(1)} %dynamic-slice_bitcast_fusion.8), channel_id=1, source_target_pairs={{0,8},{8,0},{16,24},{24,16},{1,9},{9,1},{17,25},{25,17},{2,10},{10... | collective-permute-start | bytes 1572872 | tf_op jit(solution)/shard_map/ppermute | solution.py:621
  325.1 21.8 %collective-permute-start.49 = (bf16[2,4,128,256]{3,2,1,0:T(8,128)(2,1)S(1)}, bf16[2,4,128,256]{3,2,1,0:T(8,128)(2,1)S(1)}, u32[]{:S(2)}, u32[]{:S(2)}) collective-permute-start(bf16[2,4,128,256]{3,2,1,0:T(8,128)(2,1)S(1)} %dynamic-slice_bitcast_fusion.7), channel_id=1, source_target_pairs={{0,16},{8,24},{16,0},{24,8},{1,17},{9,25},{17,1},{25,9},{2,18},{10... | collective-permute-start | bytes 1572872 | tf_op jit(solution)/shard_map/ppermute | solution.py:622
  341.7 14.8 %collective-permute-start.31 = (bf16[2,4,128,256]{3,2,1,0:T(8,128)(2,1)S(1)}, bf16[2,4,128,256]{3,2,1,0:T(8,128)(2,1)S(1)}, u32[]{:S(2)}, u32[]{:S(2)}) collective-permute-start(bf16[2,4,128,256]{3,2,1,0:T(8,128)(2,1)S(1)} %dynamic-slice_bitcast_fusion.10), channel_id=1, source_target_pairs={{0,8},{8,0},{16,24},{24,16},{1,9},{9,1},{17,25},{25,17},{2,10},{10... | collective-permute-start | bytes 1572872 | tf_op jit(solution)/shard_map/ppermute | solution.py:621
  342.2 14.9 %collective-permute-start.33 = (bf16[2,4,128,256]{3,2,1,0:T(8,128)(2,1)S(1)}, bf16[2,4,128,256]{3,2,1,0:T(8,128)(2,1)S(1)}, u32[]{:S(2)}, u32[]{:S(2)}) collective-permute-start(bf16[2,4,128,256]{3,2,1,0:T(8,128)(2,1)S(1)} %dynamic-slice_bitcast_fusion.9), channel_id=1, source_target_pairs={{0,16},{8,24},{16,0},{24,8},{1,17},{9,25},{17,1},{25,9},{2,18},{10... | collective-permute-start | bytes 1572872 | tf_op jit(solution)/shard_map/ppermute | solution.py:622
  342.4 25.4 %collective-permute-start.23 = (bf16[2,4,128,256]{3,2,1,0:T(8,128)(2,1)S(1)}, bf16[2,4,128,256]{3,2,1,0:T(8,128)(2,1)S(1)}, u32[]{:S(2)}, u32[]{:S(2)}) collective-permute-start(bf16[2,4,128,256]{3,2,1,0:T(8,128)(2,1)S(1)} %dynamic-slice_bitcast_fusion.12), channel_id=1, source_target_pairs={{0,8},{8,0},{16,24},{24,16},{1,9},{9,1},{17,25},{25,17},{2,10},{10... | collective-permute-start | bytes 1572872 | tf_op jit(solution)/shard_map/ppermute | solution.py:621
  344.7 23.6 %collective-permute-start.25 = (bf16[2,4,128,256]{3,2,1,0:T(8,128)(2,1)S(1)}, bf16[2,4,128,256]{3,2,1,0:T(8,128)(2,1)S(1)}, u32[]{:S(2)}, u32[]{:S(2)}) collective-permute-start(bf16[2,4,128,256]{3,2,1,0:T(8,128)(2,1)S(1)} %dynamic-slice_bitcast_fusion.11), channel_id=1, source_target_pairs={{0,16},{8,24},{16,0},{24,8},{1,17},{9,25},{17,1},{25,9},{2,18},{10... | collective-permute-start | bytes 1572872 | tf_op jit(solution)/shard_map/ppermute | solution.py:622
  346.9 120.7 %collective-permute-start.21 = (bf16[1024,384]{1,0:T(8,128)(2,1)S(1)}, bf16[1024,384]{1,0:T(8,128)(2,1)}, u32[]{:S(2)}, u32[]{:S(2)}) collective-permute-start(bf16[1024,384]{1,0:T(8,128)(2,1)S(1)} %add_add_fusion), channel_id=1, source_target_pairs={{0,1},{1,0},{2,3},{3,2},{4,5},{5,4},{6,7},{7,6},{8,9},{9,8},{10,11... | collective-permute-start | bytes 2359304 | tf_op jit(solution)/shard_map/ppermute | solution.py:683
  356.5 17.4 %collective-permute-start.56 = (bf16[4,128,256]{2,1,0:T(8,128)(2,1)S(1)}, bf16[4,128,256]{2,1,0:T(8,128)(2,1)S(1)}, u32[]{:S(2)}, u32[]{:S(2)}) collective-permute-start(bf16[4,128,256]{2,1,0:T(8,128)(2,1)S(1)} %dynamic-slice_bitcast_fusion.16), channel_id=1, source_target_pairs={{0,16},{8,24},{16,0},{24,8},{1,17},{9,25},{17,1},{25,9},{2,18},{10... | collective-permute-start | bytes 786440 | tf_op jit(solution)/shard_map/ppermute | solution.py:625
  357.0 16.9 %collective-permute-start.58 = (bf16[4,128,256]{2,1,0:T(8,128)(2,1)S(1)}, bf16[4,128,256]{2,1,0:T(8,128)(2,1)S(1)}, u32[]{:S(2)}, u32[]{:S(2)}) collective-permute-start(bf16[4,128,256]{2,1,0:T(8,128)(2,1)S(1)} %dynamic-slice_bitcast_fusion.15), channel_id=1, source_target_pairs={{0,8},{8,0},{16,24},{24,16},{1,9},{9,1},{17,25},{25,17},{2,10},{10... | collective-permute-start | bytes 786440 | tf_op jit(solution)/shard_map/ppermute | solution.py:626
  367.8 11.8 %collective-permute-start.48 = (bf16[4,128,256]{2,1,0:T(8,128)(2,1)S(1)}, bf16[4,128,256]{2,1,0:T(8,128)(2,1)S(1)}, u32[]{:S(2)}, u32[]{:S(2)}) collective-permute-start(bf16[4,128,256]{2,1,0:T(8,128)(2,1)S(1)} %dynamic-slice_bitcast_fusion.18), channel_id=1, source_target_pairs={{0,16},{8,24},{16,0},{24,8},{1,17},{9,25},{17,1},{25,9},{2,18},{10... | collective-permute-start | bytes 786440 | tf_op jit(solution)/shard_map/ppermute | solution.py:625
  368.3 11.3 %collective-permute-start.50 = (bf16[4,128,256]{2,1,0:T(8,128)(2,1)S(1)}, bf16[4,128,256]{2,1,0:T(8,128)(2,1)S(1)}, u32[]{:S(2)}, u32[]{:S(2)}) collective-permute-start(bf16[4,128,256]{2,1,0:T(8,128)(2,1)S(1)} %dynamic-slice_bitcast_fusion.17), channel_id=1, source_target_pairs={{0,8},{8,0},{16,24},{24,16},{1,9},{9,1},{17,25},{25,17},{2,10},{10... | collective-permute-start | bytes 786440 | tf_op jit(solution)/shard_map/ppermute | solution.py:626
  373.9 11.2 %collective-permute-start.32 = (bf16[4,128,256]{2,1,0:T(8,128)(2,1)S(1)}, bf16[4,128,256]{2,1,0:T(8,128)(2,1)S(1)}, u32[]{:S(2)}, u32[]{:S(2)}) collective-permute-start(bf16[4,128,256]{2,1,0:T(8,128)(2,1)S(1)} %dynamic-slice_bitcast_fusion.22), channel_id=1, source_target_pairs={{0,16},{8,24},{16,0},{24,8},{1,17},{9,25},{17,1},{25,9},{2,18},{10... | collective-permute-start | bytes 786440 | tf_op jit(solution)/shard_map/ppermute | solution.py:625
  374.0 11.2 %collective-permute-start.34 = (bf16[4,128,256]{2,1,0:T(8,128)(2,1)S(1)}, bf16[4,128,256]{2,1,0:T(8,128)(2,1)S(1)}, u32[]{:S(2)}, u32[]{:S(2)}) collective-permute-start(bf16[4,128,256]{2,1,0:T(8,128)(2,1)S(1)} %dynamic-slice_bitcast_fusion.21), channel_id=1, source_target_pairs={{0,8},{8,0},{16,24},{24,16},{1,9},{9,1},{17,25},{25,17},{2,10},{10... | collective-permute-start | bytes 786440 | tf_op jit(solution)/shard_map/ppermute | solution.py:626
  379.5 10.7 %collective-permute-start.24 = (bf16[4,128,256]{2,1,0:T(8,128)(2,1)S(1)}, bf16[4,128,256]{2,1,0:T(8,128)(2,1)S(1)}, u32[]{:S(2)}, u32[]{:S(2)}) collective-permute-start(bf16[4,128,256]{2,1,0:T(8,128)(2,1)S(1)} %dynamic-slice_bitcast_fusion.24), channel_id=1, source_target_pairs={{0,16},{8,24},{16,0},{24,8},{1,17},{9,25},{17,1},{25,9},{2,18},{10... | collective-permute-start | bytes 786440 | tf_op jit(solution)/shard_map/ppermute | solution.py:625
  379.6 41.4 %collective-permute-start.26 = (bf16[4,128,256]{2,1,0:T(8,128)(2,1)}, bf16[4,128,256]{2,1,0:T(8,128)(2,1)}, u32[]{:S(2)}, u32[]{:S(2)}) collective-permute-start(bf16[4,128,256]{2,1,0:T(8,128)(2,1)} %dynamic-slice_bitcast_fusion.23), channel_id=1, source_target_pairs={{0,8},{8,0},{16,24},{24,16},{1,9},{9,1},{17,25},{25,17},{2,10},{10... | collective-permute-start | bytes 786440 | tf_op jit(solution)/shard_map/ppermute | solution.py:626
  385.1 9.6 %collective-permute-start.59 = (bf16[2,128,256]{2,1,0:T(8,128)(2,1)S(1)}, bf16[2,128,256]{2,1,0:T(8,128)(2,1)S(1)}, u32[]{:S(2)}, u32[]{:S(2)}) collective-permute-start(bf16[2,128,256]{2,1,0:T(8,128)(2,1)S(1)} %get-tuple-element.96), channel_id=1, source_target_pairs={{0,2},{1,3},{2,4},{3,5},{4,6},{5,7},{6,0},{7,1},{8,10},{9,11},{10,... | collective-permute-start | bytes 393224 | tf_op jit(solution)/shard_map/ppermute | solution.py:632
  385.2 12.6 %collective-permute-start.60 = (bf16[2,128,256]{2,1,0:T(8,128)(2,1)S(1)}, bf16[2,128,256]{2,1,0:T(8,128)(2,1)S(1)}, u32[]{:S(2)}, u32[]{:S(2)}) collective-permute-start(bf16[2,128,256]{2,1,0:T(8,128)(2,1)S(1)} %get-tuple-element.97), channel_id=1, source_target_pairs={{0,4},{1,5},{2,6},{3,7},{4,0},{5,1},{6,2},{7,3},{8,12},{9,13},{10,... | collective-permute-start | bytes 393224 | tf_op jit(solution)/shard_map/ppermute | solution.py:632
  390.2 8.6 %collective-permute-start.61 = (bf16[2,128,256]{2,1,0:T(8,128)(2,1)S(1)}, bf16[2,128,256]{2,1,0:T(8,128)(2,1)S(1)}, u32[]{:S(2)}, u32[]{:S(2)}) collective-permute-start(bf16[2,128,256]{2,1,0:T(8,128)(2,1)S(1)} %get-tuple-element.98), channel_id=1, source_target_pairs={{0,6},{1,7},{2,0},{3,1},{4,2},{5,3},{6,4},{7,5},{8,14},{9,15},{10,... | collective-permute-start | bytes 393224 | tf_op jit(solution)/shard_map/ppermute | solution.py:632
  394.8 13.3 %collective-permute-start.51 = (bf16[2,128,256]{2,1,0:T(8,128)(2,1)S(1)}, bf16[2,128,256]{2,1,0:T(8,128)(2,1)S(1)}, u32[]{:S(2)}, u32[]{:S(2)}) collective-permute-start(bf16[2,128,256]{2,1,0:T(8,128)(2,1)S(1)} %get-tuple-element.93), channel_id=1, source_target_pairs={{0,2},{1,3},{2,4},{3,5},{4,6},{5,7},{6,0},{7,1},{8,10},{9,11},{10,... | collective-permute-start | bytes 393224 | tf_op jit(solution)/shard_map/ppermute | solution.py:632
  397.8 11.2 %collective-permute-start.52 = (bf16[2,128,256]{2,1,0:T(8,128)(2,1)S(1)}, bf16[2,128,256]{2,1,0:T(8,128)(2,1)S(1)}, u32[]{:S(2)}, u32[]{:S(2)}) collective-permute-start(bf16[2,128,256]{2,1,0:T(8,128)(2,1)S(1)} %get-tuple-element.94), channel_id=1, source_target_pairs={{0,4},{1,5},{2,6},{3,7},{4,0},{5,1},{6,2},{7,3},{8,12},{9,13},{10,... | collective-permute-start | bytes 393224 | tf_op jit(solution)/shard_map/ppermute | solution.py:632
  398.9 13.8 %collective-permute-start.53 = (bf16[2,128,256]{2,1,0:T(8,128)(2,1)S(1)}, bf16[2,128,256]{2,1,0:T(8,128)(2,1)S(1)}, u32[]{:S(2)}, u32[]{:S(2)}) collective-permute-start(bf16[2,128,256]{2,1,0:T(8,128)(2,1)S(1)} %get-tuple-element.95), channel_id=1, source_target_pairs={{0,6},{1,7},{2,0},{3,1},{4,2},{5,3},{6,4},{7,5},{8,14},{9,15},{10,... | collective-permute-start | bytes 393224 | tf_op jit(solution)/shard_map/ppermute | solution.py:632
  408.1 49.9 %collective-permute-start.35 = (bf16[2,128,256]{2,1,0:T(8,128)(2,1)}, bf16[2,128,256]{2,1,0:T(8,128)(2,1)}, u32[]{:S(2)}, u32[]{:S(2)}) collective-permute-start(bf16[2,128,256]{2,1,0:T(8,128)(2,1)} %get-tuple-element.102), channel_id=1, source_target_pairs={{0,2},{1,3},{2,4},{3,5},{4,6},{5,7},{6,0},{7,1},{8,10},{9,11},{10,... | collective-permute-start | bytes 393224 | tf_op jit(solution)/shard_map/ppermute | solution.py:632
  409.0 50.6 %collective-permute-start.36 = (bf16[2,128,256]{2,1,0:T(8,128)(2,1)}, bf16[2,128,256]{2,1,0:T(8,128)(2,1)}, u32[]{:S(2)}, u32[]{:S(2)}) collective-permute-start(bf16[2,128,256]{2,1,0:T(8,128)(2,1)} %get-tuple-element.103), channel_id=1, source_target_pairs={{0,4},{1,5},{2,6},{3,7},{4,0},{5,1},{6,2},{7,3},{8,12},{9,13},{10,... | collective-permute-start | bytes 393224 | tf_op jit(solution)/shard_map/ppermute | solution.py:632
  412.7 49.7 %collective-permute-start.37 = (bf16[2,128,256]{2,1,0:T(8,128)(2,1)S(1)}, bf16[2,128,256]{2,1,0:T(8,128)(2,1)}, u32[]{:S(2)}, u32[]{:S(2)}) collective-permute-start(bf16[2,128,256]{2,1,0:T(8,128)(2,1)S(1)} %get-tuple-element.104), channel_id=1, source_target_pairs={{0,6},{1,7},{2,0},{3,1},{4,2},{5,3},{6,4},{7,5},{8,14},{9,15},{10,... | collective-permute-start | bytes 393224 | tf_op jit(solution)/shard_map/ppermute | solution.py:632
  420.9 99.0 %all-gather.11.cloned.1.call-start = ((), (), s32[]{:S(2)}) async-start(), calls=%async_computation.5 | async-start | bytes 2949120 | tf_op jit(solution)/shard_map/all_gather | solution.py:641
  422.8 40.7 %collective-permute-start.27 = (bf16[2,128,256]{2,1,0:T(8,128)(2,1)}, bf16[2,128,256]{2,1,0:T(8,128)(2,1)}, u32[]{:S(2)}, u32[]{:S(2)}) collective-permute-start(bf16[2,128,256]{2,1,0:T(8,128)(2,1)} %get-tuple-element.99), channel_id=1, source_target_pairs={{0,2},{1,3},{2,4},{3,5},{4,6},{5,7},{6,0},{7,1},{8,10},{9,11},{10,... | collective-permute-start | bytes 393224 | tf_op jit(solution)/shard_map/ppermute | solution.py:632
  462.4 14.0 %collective-permute-start = (bf16[2,2,4,2,128,256]{5,4,2,0,3,1:T(8,128)(2,1)}, bf16[2,2,4,2,128,256]{5,4,2,0,3,1:T(8,128)(2,1)}, u32[]{:S(2)}, u32[]{:S(2)}) collective-permute-start(bf16[2,2,4,2,128,256]{5,4,2,0,3,1:T(8,128)(2,1)} %bitcast.386), channel_id=1, source_target_pairs={{0,1},{1,0},{2,3},{3,2},{4,5},{5,4},{6,7},{7,6},{8,9},{9,8},{10,11... | collective-permute-start | bytes 6291464 | tf_op jit(solution)/shard_map/ppermute | solution.py:618
  467.3 75.3 %all-gather.9.cloned.1.call-start = ((), (), s32[]{:S(2)}) async-start(), calls=%async_computation.4 | async-start | bytes 1179648 | tf_op jit(solution)/shard_map/all_gather | solution.py:641
  476.4 8.4 %collective-permute-start.9 = (f32[16,128]{1,0:T(8,128)S(1)}, f32[16,128]{1,0:T(8,128)S(1)}, u32[]{:S(2)}, u32[]{:S(2)}) collective-permute-start(f32[16,128]{1,0:T(8,128)S(1)} %fusion.119), channel_id=1, source_target_pairs={{0,8},{8,0},{16,24},{24,16},{1,9},{9,1},{17,25},{25,17},{2,10},{10... | collective-permute-start | bytes 24584 | tf_op jit(solution)/shard_map/ppermute | solution.py:651
  479.7 14.4 %collective-permute-start.1 = (bf16[2,4,128,256]{3,2,1,0:T(8,128)(2,1)S(1)}, bf16[2,4,128,256]{3,2,1,0:T(8,128)(2,1)S(1)}, u32[]{:S(2)}, u32[]{:S(2)}) collective-permute-start(bf16[2,4,128,256]{3,2,1,0:T(8,128)(2,1)S(1)} %dynamic-slice_bitcast_fusion.14), channel_id=1, source_target_pairs={{0,8},{8,0},{16,24},{24,16},{1,9},{9,1},{17,25},{25,17},{2,10},{10... | collective-permute-start | bytes 1572872 | tf_op jit(solution)/shard_map/ppermute | solution.py:621
  481.8 14.2 %collective-permute-start.3 = (bf16[2,4,128,256]{3,2,1,0:T(8,128)(2,1)S(1)}, bf16[2,4,128,256]{3,2,1,0:T(8,128)(2,1)S(1)}, u32[]{:S(2)}, u32[]{:S(2)}) collective-permute-start(bf16[2,4,128,256]{3,2,1,0:T(8,128)(2,1)S(1)} %dynamic-slice_bitcast_fusion.13), channel_id=1, source_target_pairs={{0,16},{8,24},{16,0},{24,8},{1,17},{9,25},{17,1},{25,9},{2,18},{10... | collective-permute-start | bytes 1572872 | tf_op jit(solution)/shard_map/ppermute | solution.py:622
  484.8 14.2 %collective-permute-start.10 = (f32[16,128]{1,0:T(8,128)S(1)}, f32[16,128]{1,0:T(8,128)S(1)}, u32[]{:S(2)}, u32[]{:S(2)}) collective-permute-start(f32[16,128]{1,0:T(8,128)S(1)} %add.457), channel_id=1, source_target_pairs={{0,16},{8,24},{16,0},{24,8},{1,17},{9,25},{17,1},{25,9},{2,18},{10... | collective-permute-start | bytes 24584 | tf_op jit(solution)/shard_map/ppermute | solution.py:651
  494.3 9.1 %collective-permute-start.2 = (bf16[4,128,256]{2,1,0:T(8,128)(2,1)S(1)}, bf16[4,128,256]{2,1,0:T(8,128)(2,1)S(1)}, u32[]{:S(2)}, u32[]{:S(2)}) collective-permute-start(bf16[4,128,256]{2,1,0:T(8,128)(2,1)S(1)} %dynamic-slice_bitcast_fusion.26), channel_id=1, source_target_pairs={{0,16},{8,24},{16,0},{24,8},{1,17},{9,25},{17,1},{25,9},{2,18},{10... | collective-permute-start | bytes 786440 | tf_op jit(solution)/shard_map/ppermute | solution.py:625
  496.2 7.5 %collective-permute-start.4 = (bf16[4,128,256]{2,1,0:T(8,128)(2,1)S(1)}, bf16[4,128,256]{2,1,0:T(8,128)(2,1)S(1)}, u32[]{:S(2)}, u32[]{:S(2)}) collective-permute-start(bf16[4,128,256]{2,1,0:T(8,128)(2,1)S(1)} %dynamic-slice_bitcast_fusion.25), channel_id=1, source_target_pairs={{0,8},{8,0},{16,24},{24,16},{1,9},{9,1},{17,25},{25,17},{2,10},{10... | collective-permute-start | bytes 786440 | tf_op jit(solution)/shard_map/ppermute | solution.py:626
  498.9 9.5 %collective-permute-start.13 = (f32[16,128]{1,0:T(8,128)S(1)}, f32[16,128]{1,0:T(8,128)S(1)}, u32[]{:S(2)}, u32[]{:S(2)}) collective-permute-start(f32[16,128]{1,0:T(8,128)S(1)} %add.458), channel_id=1, source_target_pairs={{0,6},{1,7},{2,0},{3,1},{4,2},{5,3},{6,4},{7,5},{8,14},{9,15},{10,... | collective-permute-start | bytes 24584 | tf_op jit(solution)/shard_map/ppermute | solution.py:652
  502.7 8.0 %collective-permute-start.12 = (f32[16,128]{1,0:T(8,128)S(1)}, f32[16,128]{1,0:T(8,128)S(1)}, u32[]{:S(2)}, u32[]{:S(2)}) collective-permute-start(f32[16,128]{1,0:T(8,128)S(1)} %add.458), channel_id=1, source_target_pairs={{0,4},{1,5},{2,6},{3,7},{4,0},{5,1},{6,2},{7,3},{8,12},{9,13},{10,... | collective-permute-start | bytes 24584 | tf_op jit(solution)/shard_map/ppermute | solution.py:652
  502.7 8.0 %collective-permute-start.11 = (f32[16,128]{1,0:T(8,128)S(1)}, f32[16,128]{1,0:T(8,128)S(1)}, u32[]{:S(2)}, u32[]{:S(2)}) collective-permute-start(f32[16,128]{1,0:T(8,128)S(1)} %add.458), channel_id=1, source_target_pairs={{0,2},{1,3},{2,4},{3,5},{4,6},{5,7},{6,0},{7,1},{8,10},{9,11},{10,... | collective-permute-start | bytes 24584 | tf_op jit(solution)/shard_map/ppermute | solution.py:652
  503.8 8.5 %collective-permute-start.5 = (bf16[2,128,256]{2,1,0:T(8,128)(2,1)S(1)}, bf16[2,128,256]{2,1,0:T(8,128)(2,1)S(1)}, u32[]{:S(2)}, u32[]{:S(2)}) collective-permute-start(bf16[2,128,256]{2,1,0:T(8,128)(2,1)S(1)} %get-tuple-element.105), channel_id=1, source_target_pairs={{0,2},{1,3},{2,4},{3,5},{4,6},{5,7},{6,0},{7,1},{8,10},{9,11},{10,... | collective-permute-start | bytes 393224 | tf_op jit(solution)/shard_map/ppermute | solution.py:632
  506.5 9.4 %collective-permute-start.6 = (bf16[2,128,256]{2,1,0:T(8,128)(2,1)S(1)}, bf16[2,128,256]{2,1,0:T(8,128)(2,1)S(1)}, u32[]{:S(2)}, u32[]{:S(2)}) collective-permute-start(bf16[2,128,256]{2,1,0:T(8,128)(2,1)S(1)} %get-tuple-element.106), channel_id=1, source_target_pairs={{0,4},{1,5},{2,6},{3,7},{4,0},{5,1},{6,2},{7,3},{8,12},{9,13},{10,... | collective-permute-start | bytes 393224 | tf_op jit(solution)/shard_map/ppermute | solution.py:632
  508.4 7.5 %collective-permute-start.7 = (bf16[2,128,256]{2,1,0:T(8,128)(2,1)S(1)}, bf16[2,128,256]{2,1,0:T(8,128)(2,1)S(1)}, u32[]{:S(2)}, u32[]{:S(2)}) collective-permute-start(bf16[2,128,256]{2,1,0:T(8,128)(2,1)S(1)} %get-tuple-element.107), channel_id=1, source_target_pairs={{0,6},{1,7},{2,0},{3,1},{4,2},{5,3},{6,4},{7,5},{8,14},{9,15},{10,... | collective-permute-start | bytes 393224 | tf_op jit(solution)/shard_map/ppermute | solution.py:632
  (61 other events, 443.9 us)
Sparse Core Ops, SparseCore 0:
  15.6 49.8 all-gather.6
  421.0 27.7 all-gather.12
  467.4 34.3 all-gather.10
  520.0 22.5 all-gather.8

commit v2 on v0

--- a/solution.py
+++ b/solution.py
@@ -4,6 +4,8 @@
 import jax
 import jax.numpy as jnp
 from jax import lax
+from jax.experimental import pallas as pl
+from jax.experimental.pallas import tpu as pltpu
 from jax.sharding import PartitionSpec as P
 
 HEADS = 16
@@ -43,7 +45,7 @@
     return jnp.einsum(form, left, right, preferred_element_type=jnp.float32)
 
 
-def on_device(
+def on_device_general(
     frames,
     skip_feats,
     w_skip,
@@ -251,9 +253,824 @@
     )
 
 
+BF = jnp.bfloat16
+F32 = jnp.float32
+NT = (((1,), (1,)), ((), ()))
+NN = (((1,), (0,)), ((), ()))
+TN = (((0,), (0,)), ((), ()))
+TILE = 512
+LANES = 128
+SMALL_COST = pl.CostEstimate(flops=1, bytes_accessed=1, transcendentals=0)
+SMEM_SPEC = pl.BlockSpec(memory_space=pltpu.SMEM)
+
+
+def shape_of(shape, dtype):
+    return jax.ShapeDtypeStruct(shape, dtype)
+
+
+def whole_spec(array):
+    return pl.BlockSpec(array.shape, lambda *at: (0,) * len(array.shape))
+
+
+def in_hbm(shapes):
+    return [pltpu.HBM(s.shape, s.dtype) for s in shapes]
+
+
+def from_hbm(arrays):
+    return [pltpu.with_memory_space_constraint(a, pltpu.HBM) for a in arrays]
+
+
+def mm(left, right, form):
+    return lax.dot_general(left, right, form, preferred_element_type=F32)
+
+
+def split3(value):
+    first = value.astype(BF)
+    rest = value - first.astype(F32)
+    second = rest.astype(BF)
+    return first, second, (rest - second.astype(F32)).astype(BF)
+
+
+def tables_kernel(seg_ref, slope_ref, qx_ref, kx_ref):
+    heads = qx_ref.shape[0]
+    seq_len = kx_ref.shape[0]
+    n_utt = seg_ref.shape[1]
+
+    def one(b, carry):
+        rows = pl.ds(pl.multiple_of(b * TILE, TILE), TILE)
+        lane = lax.broadcasted_iota(jnp.int32, (TILE, LANES), 1) - HEAD_DIM
+        pos = lax.broadcasted_iota(jnp.int32, (TILE, LANES), 0) + b * TILE
+        coarse = (pos >> 8).astype(F32)
+        fine = (pos & 255).astype(F32)
+        first = jnp.zeros_like(lane)
+        last = jnp.zeros_like(lane)
+        last_live = jnp.zeros_like(lane)
+        for u in range(n_utt):
+            here = lane == 9 + u
+            first = jnp.where(here, seg_ref[0, u], first)
+            last = jnp.where(here, seg_ref[1, u], last)
+            last_live = jnp.where(here, seg_ref[2, u], last_live)
+        member = jnp.where((pos >= first) & (pos < last), 1.0, 0.0)
+        is_utt = (lane >= 9) & (lane < 9 + n_utt)
+        closed = jnp.where((pos >= first) & (pos < last_live), 0.0, NEG_FILL)
+        digits = jnp.where((lane & 1) == 0, coarse, fine)
+        keys = jnp.where(is_utt, closed, jnp.where(lane < 6, digits, 1.0))
+        keys = jnp.where((lane >= 0) & (lane < 9 + n_utt), keys, 0.0)
+        kx_ref[rows, :] = keys.astype(BF)
+        for h in range(heads):
+            for s in range(2):
+                sign = 1.0 if s == 0 else -1.0
+                out = jnp.where(is_utt, member, 0.0)
+                for e in range(6):
+                    out = jnp.where(lane == e, slope_ref[h, e] * sign, out)
+                for p, piece in enumerate(split3(pos.astype(F32) * (slope_ref[h, 6] * -sign))):
+                    out = jnp.where(lane == 6 + p, piece.astype(F32), out)
+                qx_ref[h, s, rows, :] = out.astype(BF)
+        return carry
+
+    lax.fori_loop(0, seq_len // TILE, one, 0)
+
+
+def attn_tables(lengths, padded, slopes, seq_len):
+    starts = jnp.cumsum(padded) - padded
+    segments = jnp.stack([starts, starts + padded, starts + lengths]).astype(jnp.int32)
+    heads = slopes.shape[0]
+    cols = []
+    rest = slopes
+    for _ in range(3):
+        piece = lax.reduce_precision(rest, 8, 7)
+        rest = rest - piece
+        cols += [piece * 256.0, piece]
+    coefs = jnp.stack(cols + [slopes], axis=1)
+    outs = [shape_of((heads, 2, seq_len, LANES), BF), shape_of((seq_len, LANES), BF)]
+    qx, kx = pl.pallas_call(
+        tables_kernel,
+        grid=(1,),
+        out_shape=in_hbm(outs),
+        in_specs=[SMEM_SPEC, SMEM_SPEC],
+        out_specs=[whole_spec(a) for a in outs],
+        compiler_params=pltpu.CompilerParams(vmem_limit_bytes=24 * 2**20),
+        name="attn_tables",
+    )(segments, coefs)
+    return coefs, qx, kx
+
+
+def head_first(tile, h):
+    wide = tile.astype(F32)
+    return pltpu.roll(wide, HEAD_DIM, 1) if h else wide
+
+
+def ahead_of(rows, cols, axis):
+    return jnp.maximum(
+        lax.broadcasted_iota(jnp.int32, (rows, cols), axis)
+        - lax.broadcasted_iota(jnp.int32, (rows, cols), 1 - axis),
+        0,
+    ).astype(F32)
+
+
+def fwd_kernel(coef_ref, qkv_ref, qx_ref, kx_ref, o_ref, olow_ref, qb_ref, ka_ref, va_ref, s_ref):
+    seq_len = qkv_ref.shape[0]
+    blocks = seq_len // TILE
+    heads = qx_ref.shape[0]
+    for h in range(heads):
+        lo = h * HEAD_DIM
+
+        def prepare(b, carry, h=h):
+            rows = pl.ds(pl.multiple_of(b * TILE, TILE), TILE)
+            low_lane = lax.broadcasted_iota(jnp.int32, (TILE, LANES), 1) < HEAD_DIM
+            q = head_first(qkv_ref[rows, :LANES], h) * 0.125
+            k = head_first(qkv_ref[rows, LANES : 2 * LANES], h)
+            v = head_first(qkv_ref[rows, 2 * LANES :], h)
+            lane = lax.broadcasted_iota(jnp.int32, (TILE, LANES), 1)
+            ka_ref[h, rows, :] = jnp.where(low_lane, k, kx_ref[rows, :].astype(F32)).astype(BF)
+            va_ref[h, rows, :] = jnp.where(
+                low_lane, v, jnp.where(lane < HEAD_DIM + 3, 1.0, 0.0)
+            ).astype(BF)
+            for s in range(2):
+                qb_ref[h, s, rows, :] = jnp.where(
+                    low_lane, q, qx_ref[h, s, rows, :].astype(F32)
+                ).astype(BF)
+            return carry
+
+        lax.fori_loop(0, blocks, prepare, 0)
+
+        def one(qb, carry, h=h, lo=lo):
+            rows = pl.ds(pl.multiple_of(qb * TILE, TILE), TILE)
+            slope = coef_ref[h, 6]
+            top = None
+            for t in range(blocks):
+                kb = lax.rem(qb + t, blocks)
+                krows = pl.ds(pl.multiple_of(kb * TILE, TILE), TILE)
+                side = (kb > qb).astype(jnp.int32)
+                scores = mm(qb_ref[h, side, rows, :], ka_ref[h, krows, :], NT)
+                if t == 0:
+                    scores = scores - ahead_of(TILE, TILE, 1) * (2.0 * slope)
+                s_ref[:, t * TILE : (t + 1) * TILE] = scores
+                part = jnp.max(scores, axis=1, keepdims=True)
+                top = part if top is None else jnp.maximum(top, part)
+            acc = jnp.zeros((TILE, LANES), F32)
+            for t in range(blocks):
+                kb = lax.rem(qb + t, blocks)
+                krows = pl.ds(pl.multiple_of(kb * TILE, TILE), TILE)
+                probs = jnp.exp(s_ref[:, t * TILE : (t + 1) * TILE] - top).astype(BF)
+                acc = acc + mm(probs, va_ref[h, krows, :], NN)
+            total = acc[:, HEAD_DIM : HEAD_DIM + 1]
+            out = acc[:, :HEAD_DIM] / total
+            o_ref[rows, lo : lo + HEAD_DIM] = out
+            low = out.astype(BF)
+            per = olow_ref.shape[1]
+            for p in range(TILE // per):
+                olow_ref[qb * (TILE // per) + p, :, lo : lo + HEAD_DIM] = low[p * per : (p + 1) * per]
+            log_total = top + jnp.log(total)
+            lane = lax.broadcasted_iota(jnp.int32, (TILE, LANES), 1)
+            row_pos = (qb * TILE + lax.broadcasted_iota(jnp.int32, (TILE, 1), 0)).astype(F32)
+            for s in range(2):
+                base = row_pos * (slope * (1.0 if s else -1.0)) - log_total
+                full = qb_ref[h, s, rows, :].astype(F32)
+                for p, piece in enumerate(split3(base)):
+                    full = jnp.where(lane == HEAD_DIM + 6 + p, piece.astype(F32), full)
+                qb_ref[h, s, rows, :] = full.astype(BF)
+            return carry
+
+        lax.fori_loop(0, blocks, one, 0)
+
+
+def attn_fwd(coefs, qkv, qx, kx, blocks):
+    seq_len = qkv.shape[0]
+    heads = coefs.shape[0]
+    width = heads * HEAD_DIM
+    outs = [
+        shape_of((seq_len, width), F32),
+        shape_of((blocks, seq_len // blocks, width), BF),
+        shape_of((heads, 2, seq_len, LANES), BF),
+        shape_of((heads, seq_len, LANES), BF),
+        shape_of((heads, seq_len, LANES), BF),
+    ]
+    return pl.pallas_call(
+        fwd_kernel,
+        grid=(1,),
+        out_shape=in_hbm(outs),
+        in_specs=[SMEM_SPEC, *[whole_spec(a) for a in (qkv, qx, kx)]],
+        out_specs=[whole_spec(a) for a in outs],
+        scratch_shapes=[pltpu.VMEM((TILE, seq_len), F32)],
+        compiler_params=pltpu.CompilerParams(vmem_limit_bytes=48 * 2**20),
+        cost_estimate=SMALL_COST,
+        name="attn_fwd",
+    )(coefs, *from_hbm([qkv, qx, kx]))
+
+
+def pack_rows(ref, b, part, values):
+    half = ref.shape[1]
+    for p in range(TILE // half):
+        lane = part * LANES + (p % 2) * HEAD_DIM
+        ref[b * (TILE // (2 * half)) + p // 2, :, lane : lane + HEAD_DIM] = values[
+            p * half : (p + 1) * half
+        ]
+
+
+def unpack_pair(first, second):
+    low_lane = lax.broadcasted_iota(jnp.int32, first.shape, 1) < HEAD_DIM
+    first, second = first.astype(F32), second.astype(F32)
+    upper = jnp.where(low_lane, first, pltpu.roll(second, HEAD_DIM, 1))
+    lower = jnp.where(low_lane, pltpu.roll(first, HEAD_DIM, 1), second)
+    return upper.astype(BF), lower.astype(BF)
+
+
+def bwd_kernel(h, coef_ref, go_ref, o_ref, qb_ref, ka_ref, va_ref, out_ref, ga_ref, dq_ref, kt_ref):
+    seq_len = go_ref.shape[0]
+    blocks = seq_len // TILE
+    lo = h * HEAD_DIM
+    slope = coef_ref[h, 6]
+
+    def prepare(b, carry):
+        rows = pl.ds(pl.multiple_of(b * TILE, TILE), TILE)
+        go = go_ref[rows, lo : lo + HEAD_DIM].astype(F32)
+        delta = jnp.sum(go * o_ref[rows, lo : lo + HEAD_DIM], axis=1, keepdims=True)
+        lane = lax.broadcasted_iota(jnp.int32, (TILE, LANES), 1)
+        full = jnp.where(lane < HEAD_DIM, head_first(go_ref[rows, :], h), 0.0)
+        for p, piece in enumerate(split3(-delta)):
+            full = jnp.where(lane == HEAD_DIM + p, piece.astype(F32), full)
+        ga_ref[rows, :] = full.astype(BF)
+        kt_ref[:, rows] = ka_ref[0, rows, :].astype(F32).T.astype(BF)
+        dq_ref[:, rows] = jnp.zeros((HEAD_DIM, TILE), F32)
+        return carry
+
+    lax.fori_loop(0, blocks, prepare, 0)
+
+    def one(kb, carry):
+        krows = pl.ds(pl.multiple_of(kb * TILE, TILE), TILE)
+        ka = ka_ref[0, krows, :]
+        va = va_ref[0, krows, :]
+        kt = kt_ref[:HEAD_DIM, krows]
+        dv = jnp.zeros((TILE, LANES), F32)
+        dk = jnp.zeros((TILE, LANES), F32)
+        for t in range(blocks):
+            qb = lax.rem(kb + t, blocks)
+            rows = pl.ds(pl.multiple_of(qb * TILE, TILE), TILE)
+            ga = ga_ref[rows, :]
+            qa = qb_ref[0, (kb > qb).astype(jnp.int32), rows, :]
+            scores = mm(ka, qa, NT)
+            if t == 0:
+                scores = scores - ahead_of(TILE, TILE, 0) * (2.0 * slope)
+            probs = jnp.exp(scores)
+            ds = (probs * mm(va, ga, NT)).astype(BF)
+            dv = dv + mm(probs.astype(BF), ga, NN)
+            dk = dk + mm(ds, qa, NN)
+            dq_ref[:, rows] += mm(kt, ds, NN)
+        pack_rows(out_ref, kb, 1, dk[:, :HEAD_DIM].astype(BF))
+        pack_rows(out_ref, kb, 2, dv[:, :HEAD_DIM].astype(BF))
+        return carry
+
+    lax.fori_loop(0, blocks, one, 0)
+
+    def finish(b, carry):
+        rows = pl.ds(pl.multiple_of(b * TILE, TILE), TILE)
+        pack_rows(out_ref, b, 0, (dq_ref[:, rows].T * 0.125).astype(BF))
+        return carry
+
+    lax.fori_loop(0, blocks, finish, 0)
+
+
+def attn_bwd(h, coefs, go, o, qb, ka, va, blocks):
+    seq_len = go.shape[0]
+    half = seq_len // (2 * blocks)
+
+    def of_head(array):
+        zeros = (0,) * (len(array.shape) - 1)
+        return pl.BlockSpec((1, *array.shape[1:]), lambda i: (h, *zeros))
+
+    return pl.pallas_call(
+        partial(bwd_kernel, h),
+        grid=(1,),
+        out_shape=pltpu.HBM((blocks, half, 3 * LANES), BF),
+        in_specs=[SMEM_SPEC, whole_spec(go), whole_spec(o), of_head(qb), of_head(ka), of_head(va)],
+        out_specs=pl.BlockSpec((blocks, half, 3 * LANES), lambda i: (0, 0, 0)),
+        scratch_shapes=[
+            pltpu.VMEM((seq_len, LANES), BF),
+            pltpu.VMEM((HEAD_DIM, seq_len), F32),
+            pltpu.VMEM((LANES, seq_len), BF),
+        ],
+        compiler_params=pltpu.CompilerParams(vmem_limit_bytes=36 * 2**20),
+        cost_estimate=SMALL_COST,
+        name="attn_bwd",
+    )(coefs, *from_hbm([go, o, qb, ka, va]))
+
+
+def slab_kernel(left_ref, first_ref, second_ref, out_ref, right_ref):
+    @pl.when(pl.program_id(0) == 0)
+    def _():
+        half = first_ref.shape[1]
+        for b in range(first_ref.shape[0]):
+            for i in range(3):
+                lanes = slice(i * LANES, (i + 1) * LANES)
+                upper, lower = unpack_pair(first_ref[b, :, lanes], second_ref[b, :, lanes])
+                right_ref[2 * b * half : (2 * b + 1) * half, lanes] = upper
+                right_ref[(2 * b + 1) * half : (2 * b + 2) * half, lanes] = lower
+
+    grad = mm(left_ref[...], right_ref[...], TN).astype(BF)
+    block = grad.shape[0]
+    for i in range(3):
+        out_ref[0, i * block : (i + 1) * block] = grad[:, i * LANES : (i + 1) * LANES]
+
+
+def slab_call(left, first, second):
+    seq_len, width = left.shape
+    blocks = first.shape[0]
+    block = width // blocks
+    packed = pl.BlockSpec(first.shape, lambda b: (0, 0, 0))
+    return pl.pallas_call(
+        slab_kernel,
+        grid=(blocks,),
+        out_shape=pltpu.HBM((blocks, 3 * block, LANES), BF),
+        in_specs=[pl.BlockSpec((seq_len, block), lambda b: (0, b)), packed, packed],
+        out_specs=pl.BlockSpec((1, 3 * block, LANES), lambda b: (b, 0, 0)),
+        scratch_shapes=[pltpu.VMEM((seq_len, 3 * LANES), BF)],
+        compiler_params=pltpu.CompilerParams(vmem_limit_bytes=24 * 2**20),
+        cost_estimate=SMALL_COST,
+        name="slab",
+    )(*from_hbm([left, first, second]))
+
+
+def norm_stats(values):
+    centred = values - jnp.mean(values, axis=-1, keepdims=True)
+    scale = lax.rsqrt(jnp.mean(centred * centred, axis=-1, keepdims=True) + NORM_EPS)
+    return centred * scale, scale
+
+
+def norm_back(grad, xhat, scale, gain):
+    scaled = grad * gain
+    inner = jnp.mean(scaled * xhat, axis=-1, keepdims=True)
+    rows = scale * (scaled - jnp.mean(scaled, axis=-1, keepdims=True) - xhat * inner)
+    return rows, jnp.sum(grad * xhat, axis=0, keepdims=True)
+
+
+def put_columns(outs, dp, level, first, wide_ref):
+    rows = wide_ref.shape[0]
+    cols = outs[0].shape[-1]
+    if len(outs) == 1:
+        for s in range(outs[0].shape[0]):
+            outs[0][s, level, first : first + rows, :] = wide_ref[:, s * cols : (s + 1) * cols]
+        return
+    for k, out in enumerate(outs):
+        at = pl.multiple_of(jnp.bitwise_xor(dp, k) * cols, cols)
+        out[level, first : first + rows, :] = wide_ref[:, pl.ds(at, cols)]
+
+
+def row_kernel(came_ref, hidden_ref, wo_ref, gain_ref, attn_ref, xhat_ref, scale_ref, nf_ref, res_ref):
+    for s in range(came_ref.shape[0]):
+        attn_ref[:, s * LANES : (s + 1) * LANES] = came_ref[s]
+    residual = hidden_ref[...] + mm(attn_ref[...], wo_ref[...], NN)
+    xhat, scale = norm_stats(residual)
+    xhat_ref[...] = xhat
+    scale_ref[...] = scale
+    nf_ref[...] = (xhat * gain_ref[...]).astype(BF)
+    res_ref[...] = residual
+
+
+def row_call(came, hidden, w_output, gain):
+    rows, width = hidden.shape
+    wide, low = shape_of((rows, width), F32), shape_of((rows, width), BF)
+    inputs = [came, hidden, w_output, gain]
+    outs = [low, wide, shape_of((rows, 1), F32), low, wide]
+    return pl.pallas_call(
+        row_kernel,
+        grid=(1,),
+        out_shape=in_hbm(outs),
+        in_specs=[whole_spec(a) for a in inputs],
+        out_specs=[whole_spec(a) for a in outs],
+        compiler_params=pltpu.CompilerParams(vmem_limit_bytes=16 * 2**20),
+        cost_estimate=SMALL_COST,
+        name="attn_rows",
+    )(*from_hbm(inputs))
+
+
+def ffn_kernel(
+    ids_ref, nf_a, nf_b, cot_a, cot_b, up_ref, down_ref, *refs
+):
+    sums, out, (nf_ref, cot_ref) = refs[:4], refs[4], refs[5:]
+    step = pl.program_id(0)
+    rows = nf_a.shape[0]
+
+    @pl.when(step == 0)
+    def _():
+        nf_ref[:rows] = nf_a[...]
+        nf_ref[rows:] = nf_b[...]
+        cot_ref[:rows] = cot_a[...]
+        cot_ref[rows:] = cot_b[...]
+        for ref in sums:
+            ref[...] = jnp.zeros(ref.shape, F32)
+
+    nf = nf_ref[...]
+    cot = cot_ref[...]
+    up = up_ref[...]
+    down = down_ref[...]
+    pre = mm(nf, up, NN)
+    phi = 0.5 + 0.5 * lax.erf(pre * math.sqrt(0.5))
+    activ = (pre * phi).astype(BF)
+    slope = phi + pre * (jnp.exp(-0.5 * pre * pre) * (1.0 / math.sqrt(2.0 * math.pi)))
+    grad_pre = (slope * mm(cot, down, NT)).astype(BF)
+    mix = mm(activ, down, NN)
+    gnf = mm(grad_pre, up, NT)
+    for i, part in enumerate((mix[:rows], mix[rows:], gnf[:rows], gnf[rows:])):
+        sums[i][...] += part
+    gwd = mm(activ, cot, TN).astype(BF)
+    gwu = mm(nf, grad_pre, TN).astype(BF)
+    shards, levels, _, cols = out.shape
+    tile = gwd.shape[0]
+    block = gwu.shape[0] // levels
+    for s in range(shards):
+        out[s, step, :tile, :] = gwd[:, s * cols : (s + 1) * cols]
+    for level in range(levels):
+        out[step, level, tile:, :] = gwu[level * block : (level + 1) * block]
+
+
+def ffn_call(ids, nf, cot, w_up, w_down, shards, part):
+    rows, width = nf[0].shape
+    ff = w_up.shape[1]
+    tile = ff // (shards * 4)
+    inputs = [*nf, *cot]
+    out_sum = shape_of((rows, width), F32)
+    out_grad = shape_of((shards, shards, 2 * tile, width // shards), BF)
+
+    def tile_at(d, ids):
+        return d * 4 + part * 2 + ids[1]
+
+    return pl.pallas_call(
+        ffn_kernel,
+        grid_spec=pltpu.PrefetchScalarGridSpec(
+            num_scalar_prefetch=1,
+            grid=(shards,),
+            in_specs=[
+                *[whole_spec(array) for array in inputs],
+                pl.BlockSpec((width, tile), lambda d, ids: (0, tile_at(d, ids))),
+                pl.BlockSpec((tile, width), lambda d, ids: (tile_at(d, ids), 0)),
+            ],
+            out_specs=[whole_spec(out_sum)] * 4 + [whole_spec(out_grad)],
+            scratch_shapes=[
+                pltpu.VMEM((2 * rows, width), BF),
+                pltpu.VMEM((2 * rows, width), BF),
+            ],
+        ),
+        out_shape=in_hbm([out_sum] * 4 + [out_grad]),
+        compiler_params=pltpu.CompilerParams(vmem_limit_bytes=44 * 2**20),
+        cost_estimate=SMALL_COST,
+        name="ffn",
+    )(ids, *from_hbm([*inputs, w_up, w_down]))
+
+
+def branch_kernel(
+    gnf_a, came_a, gnf_b, came_b, xhat_ref, scale_ref, gain_ref, cot_ref, wo_ref,
+    resid_ref, branch_ref, gattn_ref, ggain_ref,
+):
+    gnf = gnf_a[...] + came_a[...] + gnf_b[...] + came_b[...]
+    rows, ggain = norm_back(gnf, xhat_ref[...], scale_ref[...], gain_ref[...])
+    ggain_ref[...] = ggain
+    resid = cot_ref[...].astype(F32) + rows
+    resid_ref[...] = resid
+    branch = resid.astype(BF)
+    branch_ref[...] = branch
+    gattn = mm(branch, wo_ref[...], NT).astype(BF)
+    for s in range(gattn_ref.shape[0]):
+        gattn_ref[s] = gattn[:, s * LANES : (s + 1) * LANES]
+
+
+def branch_call(gnf, xhat, scale, gain, cot, w_output, blocks):
+    rows, width = xhat.shape
+    wide, low = shape_of((rows, width), F32), shape_of((rows, width), BF)
+    inputs = [*gnf, xhat, scale, gain, cot, w_output]
+    outs = [wide, low, shape_of((blocks, rows, width // blocks), BF), shape_of((1, width), F32)]
+    return pl.pallas_call(
+        branch_kernel,
+        grid=(1,),
+        out_shape=in_hbm(outs),
+        in_specs=[whole_spec(a) for a in inputs],
+        out_specs=[whole_spec(a) for a in outs],
+        compiler_params=pltpu.CompilerParams(vmem_limit_bytes=20 * 2**20),
+        cost_estimate=SMALL_COST,
+        name="branch",
+    )(*from_hbm(inputs))
+
+
+GAIN_ROWS = 16
+
+
+def wgrad_kernel(n_left, ids_ref, *refs):
+    lefts = refs[: 2 * n_left]
+    rights = refs[2 * n_left : 2 * n_left + 2]
+    outs, wide_ref = refs[2 * n_left + 2 : -1], refs[-1]
+    dp, core = ids_ref[0], ids_ref[1]
+    level = pl.program_id(0)
+    rows = lefts[0].shape[0]
+    block = wide_ref.shape[0]
+    at = pl.ds(pl.multiple_of((level * 2 + core) * block, block), block)
+    for i in range(n_left):
+        wide_ref[...] = (
+            mm(lefts[2 * i][:, at], rights[0][:rows], TN)
+            + mm(lefts[2 * i + 1][:, at], rights[1][:rows], TN)
+        ).astype(BF)
+        put_columns(outs, dp, level, i * block, wide_ref)
+    extra = rights[0].shape[0] - rows
+    if extra:
+        takes = jnp.where((level == 0) & (core == 0), 1.0, 0.0)
+        gains = rights[0][rows:].astype(F32) + rights[1][rows:].astype(F32)
+        wide_ref[:extra] = (gains * takes).astype(BF)
+        put_columns(outs, dp, level, n_left * block, wide_ref.at[:extra])
+
+
+def wgrad_call(ids, lefts, rights, shards, levels, apart):
+    n_left = len(lefts)
+    flat = [array for pair in lefts for array in pair]
+    width = rights[0].shape[1]
+    rows, columns = flat[0].shape
+    block = columns // (2 * levels)
+    extra = rights[0].shape[0] - rows
+    shape = (levels, n_left * block + extra, width // shards)
+    outs = [shape_of(shape, BF)] * shards if apart else [shape_of((shards, *shape), BF)]
+    return pl.pallas_call(
+        partial(wgrad_kernel, n_left),
+        grid_spec=pltpu.PrefetchScalarGridSpec(
+            num_scalar_prefetch=1,
+            grid=(levels,),
+            in_specs=[whole_spec(array) for array in (*flat, *rights)],
+            out_specs=[whole_spec(out) for out in outs],
+            scratch_shapes=[pltpu.VMEM((block, width), BF)],
+        ),
+        out_shape=in_hbm(outs),
+        compiler_params=pltpu.CompilerParams(vmem_limit_bytes=24 * 2**20),
+        cost_estimate=SMALL_COST,
+        name="wgrad",
+    )(ids, *from_hbm([*flat, *rights]))
+
+
+def tail_kernel(
+    first_ref, second_ref, wq_ref, wk_ref, wv_ref, xhat_ref, scale_ref, gain_ref, resid_ref, ggain_ref,
+    gh_ref, wide_ref,
+):
+    total = None
+    for i, w_ref in enumerate((wq_ref, wk_ref, wv_ref)):
+        half = first_ref.shape[1]
+        lanes = slice(i * LANES, (i + 1) * LANES)
+        for s in range(first_ref.shape[0]):
+            upper, lower = unpack_pair(first_ref[s, :, lanes], second_ref[s, :, lanes])
+            wide_ref[:half, s * LANES : (s + 1) * LANES] = upper
+            wide_ref[half:, s * LANES : (s + 1) * LANES] = lower
+        term = mm(wide_ref[...], w_ref[...], NT)
+        total = term if total is None else total + term
+    rows, ggain = norm_back(total, xhat_ref[...], scale_ref[...], gain_ref[...])
+    count = wide_ref.shape[0]
+    gh_ref[:count] = (resid_ref[...] + rows).astype(BF)
+    at = lax.broadcasted_iota(jnp.int32, (GAIN_ROWS, ggain.shape[1]), 0)
+    gains = jnp.where(at == 0, ggain, jnp.where(at == 1, ggain_ref[...], 0.0))
+    gh_ref[count:] = gains.astype(BF)
+
+
+def tail_call(came, weights, xhat, scale, gain, resid, ggain):
+    rows, width = xhat.shape
+    inputs = [*came, *weights, xhat, scale, gain, resid, ggain]
+    return pl.pallas_call(
+        tail_kernel,
+        grid=(1,),
+        out_shape=pltpu.HBM((rows + GAIN_ROWS, width), BF),
+        in_specs=[whole_spec(a) for a in inputs],
+        out_specs=whole_spec(shape_of((rows + GAIN_ROWS, width), BF)),
+        scratch_shapes=[pltpu.VMEM((rows, width), BF)],
+        compiler_params=pltpu.CompilerParams(vmem_limit_bytes=32 * 2**20),
+        cost_estimate=SMALL_COST,
+        name="tail",
+    )(*from_hbm(inputs))
+
+
+def add_low(left, right):
+    return (left.astype(F32) + right.astype(F32)).astype(BF)
+
+
+def pick(array, index, axis):
+    return lax.dynamic_index_in_dim(array, index, axis, keepdims=False)
+
+
+def after(value, *others):
+    return lax.optimization_barrier((value, *others))[0]
+
+
+CORE_SWAP = [(i, i ^ 1) for i in range(8)]
+DP_STEPS = [[(i, i ^ k) for i in range(4)] for k in (1, 2, 3)]
+Z_NEAR = [(i, i ^ 2) for i in range(8)]
+Z_FAR = [(i, i ^ 4) for i in range(8)]
+
+
+def core_swap(values):
+    return lax.ppermute(values, "blk", CORE_SWAP)
+
+
+def dp_send(shares):
+    return [lax.ppermute(share, "dp", perm) for share, perm in zip(shares[1:], DP_STEPS)]
+
+
+def sum_low(came, own):
+    total = own.astype(F32)
+    for part in came:
+        total = total + part.astype(F32)
+    return total.astype(BF)
+
+
+def z_near(total, level):
+    near, far = jnp.bitwise_xor(level, 1), jnp.bitwise_xor(level, 2)
+    opposite = jnp.bitwise_xor(level, 3)
+    send = jnp.stack([pick(total, near, 0), pick(total, opposite, 0)])
+    keep = jnp.stack([pick(total, level, 0), pick(total, far, 0)])
+    return lax.ppermute(send, "blk", Z_NEAR), keep, send
+
+
+def z_far(came, keep):
+    send = add_low(keep[1], came[1])
+    return lax.ppermute(send, "blk", Z_FAR), add_low(keep[0], came[0]), send
+
+
+def gather_near(piece):
+    two = jnp.stack([piece, lax.ppermute(piece, "blk", Z_FAR)])
+    four = jnp.concatenate([two, lax.ppermute(two, "blk", Z_NEAR)])
+    return four, core_swap(four)
+
+
+def on_device_grid(
+    frames,
+    skip_feats,
+    w_skip,
+    gain_attn,
+    w_query,
+    w_key,
+    w_value,
+    w_output,
+    gain_ffn,
+    w_up,
+    w_down,
+    cotangent,
+    utt_lengths,
+    padded_lengths,
+):
+    row_count, width = frames.shape
+    blocks = lax.axis_size("blk")
+    shards = lax.axis_size("dp")
+    seq_len = row_count * blocks
+    pair = width // blocks
+    blk = lax.axis_index("blk")
+    dp = lax.axis_index("dp")
+
+    joined = jnp.concatenate([frames, skip_feats], axis=1)
+    hidden = product("rc,cd->rd", joined, w_skip)
+    xhat_attn, scale_attn = norm_stats(hidden)
+    normed = (xhat_attn * gain_attn).astype(BF)
+    normed_all = lax.all_gather(normed, "blk", axis=0, tiled=True)
+
+    slopes = lax.dynamic_slice_in_dim(alibi_slopes(seq_len), blk * 2, 2, 0)
+    coefs, qx, kx = attn_tables(utt_lengths[0], padded_lengths[0], slopes, seq_len)
+    w_mine = jnp.concatenate(
+        [lax.dynamic_slice_in_dim(w, blk * pair, pair, 1) for w in (w_query, w_key, w_value)],
+        axis=1,
+    )
+    qkv = product("rd,de->re", normed_all, w_mine).astype(BF)
+    attn_wide, attn_low, qb, ka, va = attn_fwd(coefs, qkv, qx, kx, blocks)
+
+    core, level = blk % 2, blk // 2
+    levels = blocks // 2
+    cols = width // shards
+    ids = jnp.stack([dp, core]).astype(jnp.int32)
+    gain_row = gain_ffn.reshape(1, width)
+
+    def behind(values, *others):
+        return [after(v, *others) for v in values]
+
+    def exchange(values):
+        return lax.all_to_all(values, "blk", 0, 0, tiled=True)
+
+    attn, xhat_ffn, scale_ffn, nf, residual = row_call(
+        exchange(attn_low), hidden, w_output, gain_row
+    )
+    cot = (cotangent, core_swap(cotangent))
+    joined_pairs = [(frames, core_swap(frames)), (skip_feats, core_swap(skip_feats))]
+    nf = (nf, core_swap(nf))
+    mix_a, mix_a_send, gnf_a, gnf_a_send, share_a = ffn_call(ids, nf, cot, w_up, w_down, shards, 0)
+    sum_a = lax.psum_scatter(share_a, "dp", scatter_dimension=0)
+    gnf_a_came = core_swap(gnf_a_send)
+    mix_b, mix_b_send, gnf_b, gnf_b_send, share_b = ffn_call(ids, nf, cot, w_up, w_down, shards, 1)
+    grad_residual, grad_branch, grad_attn, ggain_ffn = branch_call(
+        (gnf_a, gnf_a_came, gnf_b, core_swap(gnf_b_send)),
+        xhat_ffn,
+        scale_ffn,
+        gain_row,
+        cotangent,
+        w_output,
+        blocks,
+    )
+    grad_attn_came = exchange(grad_attn).reshape(seq_len, pair)
+    mix_send = after(mix_a_send, grad_branch) + mix_b_send
+    mixed = (residual + mix_a + mix_b + core_swap(mix_send)).astype(BF)
+    swapped = core_swap(jnp.stack([attn, grad_branch]))
+    (share_c,) = wgrad_call(
+        ids, [(attn, swapped[0])], (grad_branch, swapped[1]), shards, levels, False
+    )
+    n_out = share_c.shape[2]
+    share_b = jnp.concatenate([share_b, share_c], axis=2)
+    sum_b = lax.psum_scatter(share_b, "dp", scatter_dimension=0)
+
+    bwd = partial(attn_bwd, coefs=coefs, o=attn_wide, qb=qb, ka=ka, va=va, blocks=blocks)
+    dq_first = bwd(0, go=after(grad_attn_came, share_b))
+    came_first = exchange(dq_first)
+    za, keep_za, send = z_near(after(sum_a, dq_first), level)
+    dq_second = bwd(1, go=after(grad_attn_came, send))
+
+    came_second = exchange(after(dq_second, came_first))
+    za_far, keep_za, send = z_far(after(za, dq_second), keep_za)
+    slab = slab_call(after(normed_all, send), dq_first, dq_second)
+    zb, keep_zb, send = z_near(after(sum_b, slab), level)
+    piece_a = add_low(keep_za, after(za_far, send))
+    whole_a = lax.all_gather(piece_a, "blk", axis=0, tiled=False)
+    slab = exchange(after(slab, came_second))
+    gh = tail_call(
+        behind((came_first, came_second), piece_a),
+        (w_query, w_key, w_value),
+        xhat_attn,
+        scale_attn,
+        gain_attn.reshape(1, width),
+        grad_residual,
+        ggain_ffn,
+    )
+    share_d = wgrad_call(ids, joined_pairs, (gh, core_swap(gh)), shards, levels, True)
+    xd = dp_send(share_d)
+    zb_far, keep_zb, send = z_far(after(zb, *share_d), keep_zb)
+    slab = after(slab, send).reshape(shards, 2, -1, pair)
+    heads = [pick(slab, jnp.bitwise_xor(dp, k), 0) for k in range(4)]
+    xh = dp_send(heads)
+    grad_joined = product("rd,cd->rc", after(gh, *heads)[:row_count], w_skip)
+    grad_frames = grad_joined[:, :width].astype(BF)
+    grad_skip = grad_joined[:, width:].astype(BF)
+
+    sum_d = sum_low(behind(xd, grad_joined), share_d[0])
+    zd, keep_zd, send = z_near(sum_d, level)
+    piece_b = add_low(keep_zb, after(zb_far, send))
+    piece_h = sum_low(behind(xh, piece_b), heads[0])
+    piece_h = piece_h.transpose(1, 0, 2).reshape(-1, cols)
+    piece_b = jnp.concatenate([piece_b, piece_h], axis=0)
+    whole_b = lax.all_gather(piece_b, "blk", axis=0, tiled=False)
+    zd_far, keep_zd, send = z_far(after(zd, piece_b), keep_zd)
+    piece_d = add_low(keep_zd, zd_far)
+    mine, others = gather_near(piece_d)
+    by_core = [jnp.where(core == 0, mine, others), jnp.where(core == 0, others, mine)]
+
+    def take(whole, first, count):
+        return whole[:, first : first + count].astype(F32)
+
+    tile = share_a.shape[2] // 2
+    downs = [take(w, 0, tile).reshape(levels, 2, tile, cols) for w in (whole_a, whole_b)]
+    g_down = jnp.stack(downs, axis=1).reshape(-1, cols)
+    ups = [take(w, tile, tile).reshape(levels, 2, tile, cols) for w in (whole_a, whole_b)]
+    g_up = jnp.concatenate([u[:, c].reshape(-1, cols) for u in ups for c in range(2)], axis=1)
+    g_output = take(whole_b, 2 * tile, n_out).reshape(-1, cols)
+    n_head = width // blocks
+    g_heads = [
+        take(whole_b, 2 * tile + n_out + i * n_head, n_head).reshape(-1, cols) for i in range(3)
+    ]
+    n_skip = (share_d[0].shape[1] - GAIN_ROWS) // 2
+    place = [0, 2, 1, 3]
+    pieces = [
+        [
+            pick(by_core[c], jnp.asarray(place, jnp.int32)[jnp.bitwise_xor(level, at)], 0)
+            for c in range(2)
+        ]
+        for at in range(levels)
+    ]
+    g_skip = jnp.concatenate(
+        [
+            pieces[at][c][i * n_skip : (i + 1) * n_skip]
+            for i in range(2)
+            for at in range(levels)
+            for c in range(2)
+        ],
+        axis=0,
+    ).astype(F32)
+    g_gains = pieces[0][0][2 * n_skip :].astype(F32)
+    return (
+        mixed,
+        grad_frames,
+        grad_skip,
+        g_skip,
+        g_gains[0],
+        g_heads[0],
+        g_heads[1],
+        g_heads[2],
+        g_output,
+        g_gains[1],
+        g_up,
+        g_down,
+    )
+
+
 def solution(mesh):
+    shape = dict(mesh.shape)
+    grid = (shape["dp"], shape["blk"])
+    body = on_device_grid if grid == (4, 8) else on_device_general
     return jax.shard_map(
-        on_device,
+        body,
         mesh=mesh,
         in_specs=(
             P(("dp", "blk"), None),

time: 1100 us -> 444 us (0.40)
  waiting for transfers between devices: 682 us -> 162 us
  matrix products: 227 us -> 14.1 us
  Pallas kernels: 0 us -> 128 us
  other arithmetic: 86.4 us -> 32.5 us
  starting transfers between devices: 2.68 us -> 44 us
  local copies, waits for them, and re-layouts: 48.3 us -> 19.6 us
    reduce_scatter x7 -> x0, waiting for transfers between devices: 340 us -> none  [the longest x1 89.8 us: on_device(): lax.psum_scatter(grad_w_up.astype(jnp.bfloat16), 'dp', scatter_dimension=...]
    dot_general x69 -> x3, matrix products: 227 us -> 14.1 us  [product(): return jnp.einsum(form, left, right, preferred_element_type=jnp.float32)]
    pallas_call x0 -> x12, Pallas kernels: none -> 128 us  [the longest x2 32.2 us: attn_bwd(): pl.pallas_call(partial(bwd_kernel, h), grid=(1,), out_shape=pltpu.HBM((bl...]
    psum x1 -> x0, waiting for transfers between devices: 123 us -> none  [on_device(): lax.psum(shares[0].astype(jnp.bfloat16), 'blk').astype(jnp.float32)]
    all_gather x2 -> x3, waiting for transfers between devices: 93 us -> 42.1 us  [the longest x1 42.1 us: on_device_grid(): normed_all = lax.all_gather(normed, 'blk', axis=0, tiled=True)]
    convert_element_type x45 -> x11, other arithmetic: 58.9 us -> 12.5 us  [the longest x6 4.82 us: add_low(): return (left.astype(F32) + right.astype(F32)).astype(BF)]
    while x76 -> x0, local copies, waits for them, and re-layouts: 32.1 us -> none
    all_to_all x0 -> x4, starting transfers between devices: none -> 24.7 us  [exchange(): return lax.all_to_all(values, 'blk', 0, 0, tiled=True)]
  transfers between devices with their start and end apart: 42 -> 33, of which waited for: 41 -> 16; matrix products, arithmetic and copies ran while one was open for 13% -> 8% of each run, Pallas kernels for 0% -> 20%
where the time goes in v2:
time: 444 us; the launch traced here: 440 us
  waiting for transfers between devices  162 us (36%)
  Pallas kernels  128 us (29%)
  starting transfers between devices  44 us (10%)
  other arithmetic  32.5 us (7%)
  between operations  22.4 us (5%)
  local copies, waits for them, and re-layouts  19.6 us (4%)
  blocking collectives  18.4 us (4%)
  matrix products  14.1 us (3%)
    all_gather x1, waiting for transfers between devices, on_device_grid(): normed_all = lax.all_gather(normed, 'blk', axis=0, tiled=True)  42.1 us
    ppermute x3, waiting for transfers between devices, z_far(): return (lax.ppermute(send, 'blk', Z_FAR), add_low(keep[0], came[0]), send)  37.8 us
    ppermute x3, waiting for transfers between devices, z_near(): return (lax.ppermute(send, 'blk', Z_NEAR), keep, send)  32.6 us
    pallas_call x2, Pallas kernels, attn_bwd(): pl.pallas_call(partial(bwd_kernel, h), grid=(1,), out_shape=pltpu.HBM((bl...  32.2 us
    pallas_call x1, Pallas kernels, attn_fwd(): pl.pallas_call(fwd_kernel, grid=(1,), out_shape=in_hbm(outs), in_specs=[S...  27.3 us
    pallas_call x2, Pallas kernels, ffn_call(): pl.pallas_call(ffn_kernel, grid_spec=pltpu.PrefetchScalarGridSpec(num_sca...  26.4 us
    all_to_all x4, starting transfers between devices, exchange(): return lax.all_to_all(values, 'blk', 0, 0, tiled=True)  24.7 us
    all_to_all x1, blocking collectives, exchange(): return lax.all_to_all(values, 'blk', 0, 0, tiled=True)  18.4 us
  transfers between devices with their start and end apart: 33, of which 16 were waited for; matrix products, arithmetic and copies ran while one was open for 8% of the time, Pallas kernels for 20%

profile of v2, /device:TPU:0, one launch (start us, length us, event | category | flops | bytes accessed | tf_op | source)
XLA Modules:
  0.0 440.3 jit_solution(9039622533940428400)
XLA Ops:
  7.2 3.8 fusion.50
  11.4 1.4 multiply_convert_fusion
  13.9 4.8 %attn_tables.1 = (bf16[2,2,2048,128]{3,2,1,0:T(8,128)(2,1)}, bf16[2048,128]{1,0:T(8,128)(2,1)}) custom-call(s32[3,4]{1,0:T(4,128)S(1)} %pad_add_fusion.seg_ref, f32[2,7]{1,0:T(2,128)S(1)} %stack.83.slope_ref.coef_ref), custom_call_target="tpu_custom_call" | custom-call | tf_op jit(solution)/shard_map/attn_tables/pallas_call | solution.py:346
  19.7 1.1 constant_dynamic-slice_fusion.7
  20.8 42.1 %all-gather.6.cloned.1.call-done.left_ref = bf16[2048,1024]{1,0:T(8,128)(2,1)} async-done(((bf16[256,1024]{1,0:T(8,128)(2,1)}), bf16[2048,1024]{1,0:T(8,128)(2,1)}) %all-gather.6.cloned.1.call-update) | async-done | bytes 4194320 | tf_op jit(solution)/shard_map/all_gather | solution.py:923
  62.9 5.7 %convolution_convert_fusion.qkv_ref = bf16[2048,384]{1,0:T(8,128)(2,1)} fusion(bf16[2048,1024]{1,0:T(8,128)(2,1)} %all-gather.6.cloned.1.call-done.left_ref, bf16[1024,128]{1,0:T(8,128)(2,1)S(1)} %get-tuple-element.165, bf16[1024,128]{1,0:T(8,128)(2,1)S(1)} %get-tuple-element.166, bf16[1024,128]{1,0:T(8,128)(2,1)S(1)} %constant_dynamic-slice_fusion.9), kind=kOutput, calls=%fused_computation.2 | convolution fusion | flops 1613758464 | bytes 6553600 | tf_op jit(solution)/shard_map/rd,de->re/dot_general | solution.py:45
  68.6 27.3 %attn_fwd.1 = (f32[2048,128]{1,0:T(8,128)}, bf16[8,256,128]{2,1,0:T(8,128)(2,1)}, bf16[2,2,2048,128]{3,2,1,0:T(8,128)(2,1)}, bf16[2,2048,128]{2,1,0:T(8,128)(2,1)}, bf16[2,2048,128]{2,1,0:T(8,128)(2,1)}) custom-call(f32[2,7]{1,0:T(2,128)S(1)} %stack.83.slope_ref.coef_ref, bf16[2048,384]{1,0:T(8,128)(2,1)} %convolution_convert_fusion.qkv_ref, ...), custom_call_target="tpu_custom_call" | custom-call | flops 1 | bytes 1 | tf_op jit(solution)/shard_map/attn_fwd/pallas_call | solution.py:449
  95.8 3.5 all-to-all-start
  100.1 14.5 %all-to-all-done.came_ref = bf16[8,256,128]{2,1,0:T(8,128)(2,1)S(1)} async-done(((bf16[8,256,128]{2,1,0:T(8,128)(2,1)}), bf16[8,256,128]{2,1,0:T(8,128)(2,1)S(1)}, u32[]{:S(2)}, u32[]{:S(2)}) %all-to-all-start) | async-done | bytes 524320 | tf_op jit(solution)/shard_map/all_to_all | solution.py:944
  115.4 4.6 %attn_rows.1 = (bf16[256,1024]{1,0:T(8,128)(2,1)}, f32[256,1024]{1,0:T(8,128)}, f32[256,1]{1,0:T(8,128)}, bf16[256,1024]{1,0:T(8,128)(2,1)}, f32[256,1024]{1,0:T(8,128)}) custom-call(bf16[8,256,128]{2,1,0:T(8,128)(2,1)} %copy-done.9, f32[256,1024]{1,0:T(8,128)} %copy-done, bf16[1024,1024]{1,0:T(8,128)(2,1)} %wo_ref.3, f32[1,1024]{1,0:T(1,128)} %bitcast.204), custom_call_target="tpu_custom_call" | custom-call | flops 1 | bytes 1 | tf_op jit(solution)/shard_map/attn_rows/pallas_call | solution.py:635
  120.1 2.0 collective-permute-done.nf_b
  122.9 13.2 %ffn.2 = (f32[256,1024]{1,0:T(8,128)}, f32[256,1024]{1,0:T(8,128)}, f32[256,1024]{1,0:T(8,128)}, f32[256,1024]{1,0:T(8,128)}, bf16[4,4,512,256]{3,2,1,0:T(8,128)(2,1)}) custom-call(s32[2]{0:T(128)S(1)} %pad_add_fusion.1.ids_ref, bf16[256,1024]{1,0:T(8,128)(2,1)} %get-tuple-element.69.nf_a, bf16[256,1024]{1,0:T(8,128)(2,1)} %copy-done.8, ...), custom_call_target="tpu_custom_call" | custom-call | flops 1 | bytes 1 | tf_op jit(solution)/shard_map/ffn/pallas_call | solution.py:698
  136.2 1.1 copy-done.24
  137.5 13.2 %ffn.3 = (f32[256,1024]{1,0:T(8,128)}, f32[256,1024]{1,0:T(8,128)}, f32[256,1024]{1,0:T(8,128)}, f32[256,1024]{1,0:T(8,128)}, bf16[4,4,512,256]{3,2,1,0:T(8,128)(2,1)}) custom-call(s32[2]{0:T(128)S(1)} %pad_add_fusion.1.ids_ref, bf16[256,1024]{1,0:T(8,128)(2,1)} %get-tuple-element.69.nf_a, bf16[256,1024]{1,0:T(8,128)(2,1)} %copy-done.8, ...), custom_call_target="tpu_custom_call" | custom-call | flops 1 | bytes 1 | tf_op jit(solution)/shard_map/ffn/pallas_call | solution.py:698
  151.1 2.5 collective-permute-done.3.came_b
  154.6 5.8 %branch.1 = (f32[256,1024]{1,0:T(8,128)}, bf16[256,1024]{1,0:T(8,128)(2,1)}, bf16[8,256,128]{2,1,0:T(8,128)(2,1)}, f32[1,1024]{1,0:T(1,128)}) custom-call(f32[256,1024]{1,0:T(8,128)} %get-tuple-element.73.gnf_a, f32[256,1024]{1,0:T(8,128)} %copy-done.12, f32[256,1024]{1,0:T(8,128)} %get-tuple-element.75.gnf_b, f32[256,1024]{1,0:T(8,128)} %copy-done.13, ...), custom_call_target="tpu_custom_call" | custom-call | flops 1 | bytes 1 | tf_op jit(solution)/shard_map/branch/pallas_call | solution.py:742
  160.4 1.1 pad_maximum_fusion.3
  162.0 2.3 collective-permute-done.5
  164.3 1.1 slice_bitcast_fusion
  165.4 4.5 %wgrad.2 = bf16[4,4,128,256]{3,2,1,0:T(8,128)(2,1)} custom-call(s32[2]{0:T(128)S(1)} %pad_add_fusion.1.ids_ref, bf16[256,1024]{1,0:T(8,128)(2,1)} %get-tuple-element.84.refs_0_, bf16[256,1024]{1,0:T(8,128)(2,1)} %get-tuple-element.145.refs_1_, bf16[256,1024]{1,0:T(8,128)(2,1)} %get-tuple-element.79.refs_2_, bf16[256,1024]{1,0:T(8,128)(2,1)} %get-tuple-element.144.refs_3_), custom_call_target="tpu_custom_call" | custom-call | flops 1 | bytes 1 | tf_op jit(solution)/shard_map/wgrad/pallas_call | solution.py:789
  169.9 4.1 pad_maximum_fusion
  175.1 18.4 %all_to_all.25 = bf16[8,256,128]{2,1,0:T(8,128)(2,1)} all-to-all(bf16[8,256,128]{2,1,0:T(8,128)(2,1)S(1)} %copy-done.18), channel_id=1, replica_groups=mesh['dp'=4,'blk'=8] {'blk'}, dimensions={0} | all-to-all | bytes 1048576 | tf_op jit(solution)/shard_map/all_to_all | solution.py:944
  193.5 15.8 %attn_bwd.2.first_ref = bf16[8,128,384]{2,1,0:T(8,128)(2,1)} custom-call(f32[2,7]{1,0:T(2,128)S(1)} %stack.83.slope_ref.coef_ref, bf16[2048,128]{1,0:T(8,128)(2,1)} %bitcast.177, f32[2048,128]{1,0:T(8,128)} %get-tuple-element.86.o_ref, bf16[2,2,2048,128]{3,2,1,0:T(8,128)(2,1)} %get-tuple-element.87.qb_ref, bf16[2,2048,128]{2,1,0:T(8,128)(2,1)} %get-tuple-element.88.ka_ref, ...), custom_call_target="tpu_custom_call" | custom-call | flops 1 | bytes 1 | tf_op jit(solution)/shard_map/attn_bwd/pallas_call | solution.py:542
  209.3 14.1 %all-to-all-start.2 = ((bf16[8,128,384]{2,1,0:T(8,128)(2,1)}), bf16[8,128,384]{2,1,0:T(8,128)(2,1)S(1)}, u32[]{:S(2)}, u32[]{:S(2)}) async-start(bf16[8,128,384]{2,1,0:T(8,128)(2,1)} %attn_bwd.2.first_ref), calls=%async_computation.2 | async-start | bytes 1572864 | tf_op jit(solution)/shard_map/all_to_all | solution.py:944
  223.5 1.1 constant_dynamic-slice_fusion.6
  224.6 1.8 collective-permute-start.6
  226.4 16.4 %attn_bwd.3.second_ref = bf16[8,128,384]{2,1,0:T(8,128)(2,1)} custom-call(f32[2,7]{1,0:T(2,128)S(1)} %stack.83.slope_ref.coef_ref, bf16[2048,128]{1,0:T(8,128)(2,1)} %bitcast.178, f32[2048,128]{1,0:T(8,128)} %get-tuple-element.86.o_ref, bf16[2,2,2048,128]{3,2,1,0:T(8,128)(2,1)} %get-tuple-element.87.qb_ref, bf16[2,2048,128]{2,1,0:T(8,128)(2,1)} %get-tuple-element.88.ka_ref, ...), custom_call_target="tpu_custom_call" | custom-call | flops 1 | bytes 1 | tf_op jit(solution)/shard_map/attn_bwd/pallas_call | solution.py:542
  242.8 1.4 all-to-all-done.2.first_ref
  244.2 3.5 all-to-all-start.3
  247.8 2.5 collective-permute-done.6
  251.4 2.5 collective-permute-start.7
  253.9 8.7 %slab.1 = bf16[8,384,128]{2,1,0:T(8,128)(2,1)} custom-call(bf16[2048,1024]{1,0:T(8,128)(2,1)} %all-gather.6.cloned.1.call-done.left_ref, bf16[8,128,384]{2,1,0:T(8,128)(2,1)} %attn_bwd.2.first_ref, bf16[8,128,384]{2,1,0:T(8,128)(2,1)} %attn_bwd.3.second_ref), custom_call_target="tpu_custom_call" | custom-call | flops 1 | bytes 1 | tf_op jit(solution)/shard_map/slab/pallas_call | solution.py:581
  262.6 1.1 constant_dynamic-slice_fusion.4
  264.6 15.3 %collective-permute-done.7 = bf16[512,256]{1,0:T(8,128)(2,1)S(1)} collective-permute-done((bf16[512,256]{1,0:T(8,128)(2,1)S(1)}, bf16[512,256]{1,0:T(8,128)(2,1)S(1)}, u32[]{:S(2)}, u32[]{:S(2)}) %collective-permute-start.7) | collective-permute-done | bytes 262176 | tf_op jit(solution)/shard_map/ppermute | solution.py:886
  279.9 1.8 fusion.10
  281.7 3.6 all-to-all-start.4
  285.3 1.9 collective-permute-start.8
  288.0 7.2 %tail.1.refs_4_ = bf16[272,1024]{1,0:T(8,128)(2,1)} custom-call(bf16[8,128,384]{2,1,0:T(8,128)(2,1)} %copy-done.4, bf16[8,128,384]{2,1,0:T(8,128)(2,1)} %copy-done.5, bf16[1024,1024]{1,0:T(8,128)(2,1)} %wq_ref.1, bf16[1024,1024]{1,0:T(8,128)(2,1)} %wk_ref.1, bf16[1024,1024]{1,0:T(8,128)(2,1)} %wv_ref.1, f32[256,1024]{1,0:T(8,128)} %get-tuple-element.121.xhat_ref, ...), custom_call_target="tpu_custom_call" | custom-call | flops 1 | bytes 1 | tf_op jit(solution)/shard_map/tail/pallas_call | solution.py:830
  295.8 2.5 collective-permute-done.9.refs_1_
  299.1 6.0 %wgrad.3 = (bf16[4,272,256]{2,1,0:T(8,128)(2,1)}, bf16[4,272,256]{2,1,0:T(8,128)(2,1)}, bf16[4,272,256]{2,1,0:T(8,128)(2,1)}, bf16[4,272,256]{2,1,0:T(8,128)(2,1)}) custom-call(s32[2]{0:T(128)S(1)} %pad_add_fusion.1.ids_ref, bf16[256,1024]{1,0:T(8,128)(2,1)} %refs_0_.1, bf16[256,1024]{1,0:T(8,128)(2,1)} %collective-permute-done.9.refs_1_, ...), custom_call_target="tpu_custom_call" | custom-call | flops 1 | bytes 1 | tf_op jit(solution)/shard_map/wgrad/pallas_call | solution.py:789
  305.1 2.5 collective-permute-start.14
  308.6 23.4 %collective-permute-done.8 = bf16[2,640,256]{2,1,0:T(8,128)(2,1)S(1)} collective-permute-done((bf16[2,640,256]{2,1,0:T(8,128)(2,1)}, bf16[2,640,256]{2,1,0:T(8,128)(2,1)S(1)}, u32[]{:S(2)}, u32[]{:S(2)}) %collective-permute-start.8) | collective-permute-done | bytes 655392 | tf_op jit(solution)/shard_map/ppermute | solution.py:881
  332.8 2.4 collective-permute-start.16
  335.2 2.5 collective-permute-start.19
  337.8 4.6 %fusion.11 = bf16[256,2048]{1,0:T(8,128)(2,1)} fusion(bf16[2048,1024]{1,0:T(8,128)(2,1)} %param.24, bf16[272,1024]{1,0:T(8,128)(2,1)S(1)} %copy-done.6), kind=kOutput, calls=%fused_computation.38 | convolution fusion | flops 1073741824 | bytes 5767168 | tf_op jit(solution)/shard_map/rd,cd->rc/dot_general | solution.py:45
  343.3 1.7 add_convert_fusion
  345.8 4.6 %collective-permute-done.16 = bf16[640,256]{1,0:T(8,128)(2,1)} collective-permute-done((bf16[640,256]{1,0:T(8,128)(2,1)}, bf16[640,256]{1,0:T(8,128)(2,1)}, u32[]{:S(2)}, u32[]{:S(2)}) %collective-permute-start.16) | collective-permute-done | bytes 327712 | tf_op jit(solution)/shard_map/ppermute | solution.py:886
  350.4 1.1 fusion.9
  352.9 1.7 add.181
  354.7 6.7 %collective-permute-done.15 = bf16[2,272,256]{2,1,0:T(8,128)(2,1)S(1)} collective-permute-done((bf16[2,272,256]{2,1,0:T(8,128)(2,1)S(1)}, bf16[2,272,256]{2,1,0:T(8,128)(2,1)S(1)}, u32[]{:S(2)}, u32[]{:S(2)}) %collective-permute-start.15) | collective-permute-done | bytes 278560 | tf_op jit(solution)/shard_map/ppermute | solution.py:881
  362.3 18.0 %collective-permute-done.20 = bf16[272,256]{1,0:T(8,128)(2,1)S(1)} collective-permute-done((bf16[272,256]{1,0:T(8,128)(2,1)S(1)}, bf16[272,256]{1,0:T(8,128)(2,1)S(1)}, u32[]{:S(2)}, u32[]{:S(2)}) %collective-permute-start.20) | collective-permute-done | bytes 139296 | tf_op jit(solution)/shard_map/ppermute | solution.py:886
  380.4 15.9 %collective-permute-done.21 = bf16[272,256]{1,0:T(8,128)(2,1)S(1)} collective-permute-done((bf16[272,256]{1,0:T(8,128)(2,1)S(1)}, bf16[272,256]{1,0:T(8,128)(2,1)S(1)}, u32[]{:S(2)}, u32[]{:S(2)}) %collective-permute-start.21) | collective-permute-done | bytes 139296 | tf_op jit(solution)/shard_map/ppermute | solution.py:890
  404.9 7.2 %collective-permute-done.22 = bf16[2,272,256]{2,1,0:T(8,128)(2,1)S(1)} collective-permute-done((bf16[2,272,256]{2,1,0:T(8,128)(2,1)S(1)}, bf16[2,272,256]{2,1,0:T(8,128)(2,1)S(1)}, u32[]{:S(2)}, u32[]{:S(2)}) %collective-permute-start.22) | collective-permute-done | bytes 278560 | tf_op jit(solution)/shard_map/ppermute | solution.py:891
  412.2 3.1 add_convert_fusion.1
  415.3 1.0 fusion.47
  416.8 1.5 convert_element_type.216
  418.8 1.7 fusion.44
  420.7 1.8 fusion.43
  423.7 1.1 bitcast_convert_fusion.4
  424.8 1.1 bitcast_convert_fusion.3
  425.9 1.1 bitcast_convert_fusion.2
  427.0 1.1 bitcast_convert_fusion.1
  428.5 2.5 bitcast_convert_fusion
  430.9 2.7 pad_maximum_fusion.1
  (154 shorter events, 21.8 us)
Async XLA Ops:
  7.2 4.2 copy-start.20
  7.2 55.7 %all-gather.6.cloned.1.call-start = ((), (), s32[]{:S(2)}) async-start(), calls=%async_computation.7 | async-start | bytes 4718592 | tf_op jit(solution)/shard_map/all_gather | solution.py:923
  11.1 1.8 copy-start
  11.1 2.5 copy-start.23
  11.1 2.8 copy-start.22
  68.5 31.1 %copy-start.1 = (bf16[256,1024]{1,0:T(8,128)(2,1)S(1)}, bf16[256,1024]{1,0:T(8,128)(2,1)}, u32[]{:S(2)}) copy-start(bf16[256,1024]{1,0:T(8,128)(2,1)} %cot_ref.1) | copy-start | bytes 1572868
  95.8 18.8 %all-to-all-start = ((bf16[8,256,128]{2,1,0:T(8,128)(2,1)}), bf16[8,256,128]{2,1,0:T(8,128)(2,1)S(1)}, u32[]{:S(2)}, u32[]{:S(2)}) async-start(bf16[8,256,128]{2,1,0:T(8,128)(2,1)} %get-tuple-element.67), calls=%async_computation | async-start | bytes 1048576 | tf_op jit(solution)/shard_map/all_to_all | solution.py:944
  99.3 124.2 %reduce-scatter.7.cloned.1.call-start = ((), (), s32[]{:S(2)}) async-start(), calls=%async_computation.10 | async-start | bytes 5242880
  99.6 20.4 %collective-permute-start.1 = (bf16[256,1024]{1,0:T(8,128)(2,1)S(1)}, bf16[256,1024]{1,0:T(8,128)(2,1)S(1)}, u32[]{:S(2)}, u32[]{:S(2)}) collective-permute-start(bf16[256,1024]{1,0:T(8,128)(2,1)S(1)} %copy-done.1), channel_id=1, source_target_pairs={{0,1},{1,0},{2,3},{3,2},{4,5},{5,4},{6,7},{7,6},{8,9},{9,8},{10,11... | collective-permute-start | bytes 1572872 | tf_op jit(solution)/shard_map/ppermute | solution.py:862
  114.6 0.8 copy-start.9
  120.0 2.1 collective-permute-start
  120.1 2.0 copy-start.7
  122.1 0.8 copy-start.8
  136.1 1.2 copy-start.24
  136.2 126.4 %reduce-scatter.9.cloned.1.call-start = ((), (), s32[]{:S(2)}) async-start(), calls=%async_computation.11 | async-start | bytes 6553600
  137.4 13.7 %collective-permute-start.2 = (f32[256,1024]{1,0:T(8,128)S(1)}, f32[256,1024]{1,0:T(8,128)S(1)}, u32[]{:S(2)}, u32[]{:S(2)}) collective-permute-start(f32[256,1024]{1,0:T(8,128)S(1)} %copy-done.24), channel_id=1, source_target_pairs={{0,1},{1,0},{2,3},{3,2},{4,5},{5,4},{6,7},{7,6},{8,9},{9,8},{10,11... | collective-permute-start | bytes 3145736 | tf_op jit(solution)/shard_map/ppermute | solution.py:862
  150.7 2.9 collective-permute-start.3
  151.1 2.5 copy-start.12
  153.6 1.0 copy-start.13
  154.6 5.8 %copy-start.10 = (bf16[256,1024]{1,0:T(8,128)(2,1)S(1)}, bf16[256,1024]{1,0:T(8,128)(2,1)}, u32[]{:S(2)}) copy-start(bf16[256,1024]{1,0:T(8,128)(2,1)} %get-tuple-element.84.refs_0_) | copy-start | bytes 1572868
  161.6 2.7 collective-permute-start.5
  164.3 5.6 %copy-start.3 = (bf16[4,4,512,256]{3,2,1,0:T(8,128)(2,1)S(1)}, bf16[4,4,512,256]{3,2,1,0:T(8,128)(2,1)}, u32[]{:S(2)}) copy-start(bf16[4,4,512,256]{3,2,1,0:T(8,128)(2,1)} %get-tuple-element.83) | copy-start | bytes 12582916
  174.0 1.0 copy-start.18
  209.3 34.9 %all-to-all-start.2 = ((bf16[8,128,384]{2,1,0:T(8,128)(2,1)}), bf16[8,128,384]{2,1,0:T(8,128)(2,1)S(1)}, u32[]{:S(2)}, u32[]{:S(2)}) async-start(bf16[8,128,384]{2,1,0:T(8,128)(2,1)} %attn_bwd.2.first_ref), calls=%async_computation.2 | async-start | bytes 1572864 | tf_op jit(solution)/shard_map/all_to_all | solution.py:944
  224.6 25.7 %copy-start.15 = (bf16[1,4,512,256]{3,2,1,0:T(8,128)(2,1)S(1)}, bf16[1,4,512,256]{3,2,1,0:T(8,128)(2,1)}, u32[]{:S(2)}) copy-start(bf16[1,4,512,256]{3,2,1,0:T(8,128)(2,1)} %reduce-scatter.7.cloned.1.call-done) | copy-start | bytes 3145732
  224.6 25.7 %collective-permute-start.6 = (bf16[2,512,256]{2,1,0:T(8,128)(2,1)S(1)}, bf16[2,512,256]{2,1,0:T(8,128)(2,1)}, u32[]{:S(2)}, u32[]{:S(2)}) collective-permute-start(bf16[2,512,256]{2,1,0:T(8,128)(2,1)S(1)} %pad_maximum_fusion.6), channel_id=1, source_target_pairs={{0,2},{1,3},{2,0},{3,1},{4,6},{5,7},{6,4},{7,5},{8,10},{9,11},{10,... | collective-permute-start | bytes 1572872 | tf_op jit(solution)/shard_map/ppermute | solution.py:881
  244.2 18.4 %copy-start.4 = (bf16[8,128,384]{2,1,0:T(8,128)(2,1)}, bf16[8,128,384]{2,1,0:T(8,128)(2,1)S(1)}, u32[]{:S(2)}) copy-start(bf16[8,128,384]{2,1,0:T(8,128)(2,1)S(1)} %all-to-all-done.2.first_ref) | copy-start | bytes 2359300
  244.2 37.5 %all-to-all-start.3 = ((bf16[8,128,384]{2,1,0:T(8,128)(2,1)}), bf16[8,128,384]{2,1,0:T(8,128)(2,1)S(1)}, u32[]{:S(2)}, u32[]{:S(2)}) async-start(bf16[8,128,384]{2,1,0:T(8,128)(2,1)} %attn_bwd.3.second_ref), calls=%async_computation.3 | async-start | bytes 1572864 | tf_op jit(solution)/shard_map/all_to_all | solution.py:944
  247.8 171.1 %all-gather.10.cloned.1.call-start = ((), (), s32[]{:S(2)}) async-start(), calls=%async_computation.9 | async-start | bytes 2359296 | tf_op jit(solution)/shard_map/all_gather | solution.py:987
  251.4 28.5 %collective-permute-start.7 = (bf16[512,256]{1,0:T(8,128)(2,1)S(1)}, bf16[512,256]{1,0:T(8,128)(2,1)S(1)}, u32[]{:S(2)}, u32[]{:S(2)}) collective-permute-start(bf16[512,256]{1,0:T(8,128)(2,1)S(1)} %fusion.17), channel_id=1, source_target_pairs={{0,4},{1,5},{2,6},{3,7},{4,0},{5,1},{6,2},{7,3},{8,12},{9,13},{10,... | collective-permute-start | bytes 786440 | tf_op jit(solution)/shard_map/ppermute | solution.py:886
  281.7 6.3 %copy-start.5 = (bf16[8,128,384]{2,1,0:T(8,128)(2,1)}, bf16[8,128,384]{2,1,0:T(8,128)(2,1)S(1)}, u32[]{:S(2)}) copy-start(bf16[8,128,384]{2,1,0:T(8,128)(2,1)S(1)} %all-to-all-done.3.second_ref) | copy-start | bytes 2359300
  281.7 53.4 %all-to-all-start.4 = ((bf16[8,384,128]{2,1,0:T(8,128)(2,1)}), bf16[8,384,128]{2,1,0:T(8,128)(2,1)S(1)}, u32[]{:S(2)}, u32[]{:S(2)}) async-start(bf16[8,384,128]{2,1,0:T(8,128)(2,1)} %slab.1), calls=%async_computation.4 | async-start | bytes 1572864 | tf_op jit(solution)/shard_map/all_to_all | solution.py:944
  285.3 135.4 %all-gather.8.cloned.1.call-start = ((), (), s32[]{:S(2)}) async-start(), calls=%async_computation.8 | async-start | bytes 4718592 | tf_op jit(solution)/shard_map/all_gather | solution.py:1014
  285.3 46.6 %collective-permute-start.8 = (bf16[2,640,256]{2,1,0:T(8,128)(2,1)}, bf16[2,640,256]{2,1,0:T(8,128)(2,1)S(1)}, u32[]{:S(2)}, u32[]{:S(2)}) collective-permute-start(bf16[2,640,256]{2,1,0:T(8,128)(2,1)} %pad_maximum_fusion.4), channel_id=1, source_target_pairs={{0,2},{1,3},{2,0},{3,1},{4,6},{5,7},{6,4},{7,5},{8,10},{9,11},{10,... | collective-permute-start | bytes 1966088 | tf_op jit(solution)/shard_map/ppermute | solution.py:881
  295.2 36.7 %copy-start.11 = (bf16[1,4,640,256]{3,2,1,0:T(8,128)(2,1)S(1)}, bf16[1,4,640,256]{3,2,1,0:T(8,128)(2,1)}, u32[]{:S(2)}) copy-start(bf16[1,4,640,256]{3,2,1,0:T(8,128)(2,1)} %reduce-scatter.9.cloned.1.call-done) | copy-start | bytes 3932164
  295.2 3.8 collective-permute-start.11
  295.2 3.0 collective-permute-start.9
  295.7 3.3 collective-permute-start.10
  295.8 41.9 %copy-start.6 = (bf16[272,1024]{1,0:T(8,128)(2,1)S(1)}, bf16[272,1024]{1,0:T(8,128)(2,1)}, u32[]{:S(2)}) copy-start(bf16[272,1024]{1,0:T(8,128)(2,1)} %tail.1.refs_4_) | copy-start | bytes 1671172
  305.1 37.2 %collective-permute-start.14 = (bf16[4,272,256]{2,1,0:T(8,128)(2,1)}, bf16[4,272,256]{2,1,0:T(8,128)(2,1)}, u32[]{:S(2)}, u32[]{:S(2)}) collective-permute-start(bf16[4,272,256]{2,1,0:T(8,128)(2,1)} %get-tuple-element.106), channel_id=1, source_target_pairs={{0,24},{8,16},{16,8},{24,0},{1,25},{9,17},{17,9},{25,1},{2,26},{10... | collective-permute-start | bytes 1671176 | tf_op jit(solution)/shard_map/ppermute | solution.py:866
  307.6 35.2 %collective-permute-start.13 = (bf16[4,272,256]{2,1,0:T(8,128)(2,1)}, bf16[4,272,256]{2,1,0:T(8,128)(2,1)}, u32[]{:S(2)}, u32[]{:S(2)}) collective-permute-start(bf16[4,272,256]{2,1,0:T(8,128)(2,1)} %get-tuple-element.105), channel_id=1, source_target_pairs={{0,16},{8,24},{16,0},{24,8},{1,17},{9,25},{17,1},{25,9},{2,18},{10... | collective-permute-start | bytes 1671176 | tf_op jit(solution)/shard_map/ppermute | solution.py:866
  308.0 35.3 %collective-permute-start.12 = (bf16[4,272,256]{2,1,0:T(8,128)(2,1)}, bf16[4,272,256]{2,1,0:T(8,128)(2,1)}, u32[]{:S(2)}, u32[]{:S(2)}) collective-permute-start(bf16[4,272,256]{2,1,0:T(8,128)(2,1)} %get-tuple-element.104), channel_id=1, source_target_pairs={{0,8},{8,0},{16,24},{24,16},{1,9},{9,1},{17,25},{25,17},{2,10},{10... | collective-permute-start | bytes 1671176 | tf_op jit(solution)/shard_map/ppermute | solution.py:866
  332.8 17.6 %collective-permute-start.16 = (bf16[640,256]{1,0:T(8,128)(2,1)}, bf16[640,256]{1,0:T(8,128)(2,1)}, u32[]{:S(2)}, u32[]{:S(2)}) collective-permute-start(bf16[640,256]{1,0:T(8,128)(2,1)} %fusion.13), channel_id=1, source_target_pairs={{0,4},{1,5},{2,6},{3,7},{4,0},{5,1},{6,2},{7,3},{8,12},{9,13},{10,... | collective-permute-start | bytes 983048 | tf_op jit(solution)/shard_map/ppermute | solution.py:886
  335.2 16.3 %collective-permute-start.19 = (bf16[2,384,128]{2,1,0:T(8,128)(2,1)S(1)}, bf16[2,384,128]{2,1,0:T(8,128)(2,1)S(1)}, u32[]{:S(2)}, u32[]{:S(2)}) collective-permute-start(bf16[2,384,128]{2,1,0:T(8,128)(2,1)S(1)} %get-tuple-element.146), channel_id=1, source_target_pairs={{0,24},{8,16},{16,8},{24,0},{1,25},{9,17},{17,9},{25,1},{2,26},{10... | collective-permute-start | bytes 589832 | tf_op jit(solution)/shard_map/ppermute | solution.py:866
  337.8 5.6 %copy-start.17 = (bf16[4,272,256]{2,1,0:T(8,128)(2,1)S(1)}, bf16[4,272,256]{2,1,0:T(8,128)(2,1)}, u32[]{:S(2)}) copy-start(bf16[4,272,256]{2,1,0:T(8,128)(2,1)} %get-tuple-element.103) | copy-start | bytes 1671172
  342.3 9.2 %collective-permute-start.18 = (bf16[2,384,128]{2,1,0:T(8,128)(2,1)S(1)}, bf16[2,384,128]{2,1,0:T(8,128)(2,1)S(1)}, u32[]{:S(2)}, u32[]{:S(2)}) collective-permute-start(bf16[2,384,128]{2,1,0:T(8,128)(2,1)S(1)} %get-tuple-element.147), channel_id=1, source_target_pairs={{0,16},{8,24},{16,0},{24,8},{1,17},{9,25},{17,1},{25,9},{2,18},{10... | collective-permute-start | bytes 589832 | tf_op jit(solution)/shard_map/ppermute | solution.py:866
  342.8 8.7 %collective-permute-start.17 = (bf16[2,384,128]{2,1,0:T(8,128)(2,1)S(1)}, bf16[2,384,128]{2,1,0:T(8,128)(2,1)S(1)}, u32[]{:S(2)}, u32[]{:S(2)}) collective-permute-start(bf16[2,384,128]{2,1,0:T(8,128)(2,1)S(1)} %get-tuple-element.148), channel_id=1, source_target_pairs={{0,8},{8,0},{16,24},{24,16},{1,9},{9,1},{17,25},{25,17},{2,10},{10... | collective-permute-start | bytes 589832 | tf_op jit(solution)/shard_map/ppermute | solution.py:866
  351.5 1.3 copy-start.19
  352.8 8.6 %collective-permute-start.15 = (bf16[2,272,256]{2,1,0:T(8,128)(2,1)S(1)}, bf16[2,272,256]{2,1,0:T(8,128)(2,1)S(1)}, u32[]{:S(2)}, u32[]{:S(2)}) collective-permute-start(bf16[2,272,256]{2,1,0:T(8,128)(2,1)S(1)} %copy-done.19), channel_id=1, source_target_pairs={{0,2},{1,3},{2,0},{3,1},{4,6},{5,7},{6,4},{7,5},{8,10},{9,11},{10,... | collective-permute-start | bytes 835592 | tf_op jit(solution)/shard_map/ppermute | solution.py:881
  352.9 43.6 %copy-start.21 = (s32[4]{0:T(128)S(1)}, s32[4]{0:T(128)}, u32[]{:S(2)}) copy-start(s32[4]{0:T(128)} %constant.126.clone) | copy-start | bytes 52
  354.6 57.6 %copy-start.16 = (f32[256,1024]{1,0:T(8,128)S(1)}, f32[256,1024]{1,0:T(8,128)}, u32[]{:S(2)}) copy-start(f32[256,1024]{1,0:T(8,128)} %get-tuple-element.68) | copy-start | bytes 3145732
  354.6 57.5 %collective-permute-start.4 = (f32[256,1024]{1,0:T(8,128)S(1)}, f32[256,1024]{1,0:T(8,128)}, u32[]{:S(2)}, u32[]{:S(2)}) collective-permute-start(f32[256,1024]{1,0:T(8,128)S(1)} %add.181), channel_id=1, source_target_pairs={{0,1},{1,0},{2,3},{3,2},{4,5},{5,4},{6,7},{7,6},{8,9},{9,8},{10,11... | collective-permute-start | bytes 3145736 | tf_op jit(solution)/shard_map/ppermute | solution.py:862
  361.4 18.8 %collective-permute-start.20 = (bf16[272,256]{1,0:T(8,128)(2,1)S(1)}, bf16[272,256]{1,0:T(8,128)(2,1)S(1)}, u32[]{:S(2)}, u32[]{:S(2)}) collective-permute-start(bf16[272,256]{1,0:T(8,128)(2,1)S(1)} %fusion.20), channel_id=1, source_target_pairs={{0,4},{1,5},{2,6},{3,7},{4,0},{5,1},{6,2},{7,3},{8,12},{9,13},{10,... | collective-permute-start | bytes 417800 | tf_op jit(solution)/shard_map/ppermute | solution.py:886
  380.4 16.0 %collective-permute-start.21 = (bf16[272,256]{1,0:T(8,128)(2,1)S(1)}, bf16[272,256]{1,0:T(8,128)(2,1)S(1)}, u32[]{:S(2)}, u32[]{:S(2)}) collective-permute-start(bf16[272,256]{1,0:T(8,128)(2,1)S(1)} %fusion.15), channel_id=1, source_target_pairs={{0,4},{1,5},{2,6},{3,7},{4,0},{5,1},{6,2},{7,3},{8,12},{9,13},{10,... | collective-permute-start | bytes 417800 | tf_op jit(solution)/shard_map/ppermute | solution.py:890
  396.4 15.6 %collective-permute-start.22 = (bf16[2,272,256]{2,1,0:T(8,128)(2,1)S(1)}, bf16[2,272,256]{2,1,0:T(8,128)(2,1)S(1)}, u32[]{:S(2)}, u32[]{:S(2)}) collective-permute-start(bf16[2,272,256]{2,1,0:T(8,128)(2,1)S(1)} %pad_maximum_fusion.9), channel_id=1, source_target_pairs={{0,2},{1,3},{2,0},{3,1},{4,6},{5,7},{6,4},{7,5},{8,10},{9,11},{10,... | collective-permute-start | bytes 835592 | tf_op jit(solution)/shard_map/ppermute | solution.py:891
  412.1 4.2 collective-permute-start.23
  412.2 3.1 copy-start.14
  420.7 2.8 copy-start.2
Sparse Core Ops, SparseCore 0:
  13.0 49.8 all-gather.5
  136.3 51.5 reduce-scatter.6
  191.1 61.4 reduce-scatter.8
  281.8 43.7 all-gather.9
  352.9 59.3 all-gather.7

commit v3 on v2

--- a/solution.py
+++ b/solution.py
@@ -260,7 +260,6 @@
 TN = (((0,), (0,)), ((), ()))
 TILE = 512
 LANES = 128
-SMALL_COST = pl.CostEstimate(flops=1, bytes_accessed=1, transcendentals=0)
 SMEM_SPEC = pl.BlockSpec(memory_space=pltpu.SMEM)
 
 
@@ -270,6 +269,10 @@
 
 def whole_spec(array):
     return pl.BlockSpec(array.shape, lambda *at: (0,) * len(array.shape))
+
+
+def takes(micros):
+    return pl.CostEstimate(flops=int(micros * 1.15e9), bytes_accessed=0, transcendentals=0)
 
 
 def in_hbm(shapes):
@@ -368,93 +371,149 @@
     ).astype(F32)
 
 
-def fwd_kernel(coef_ref, qkv_ref, qx_ref, kx_ref, o_ref, olow_ref, qb_ref, ka_ref, va_ref, s_ref):
-    seq_len = qkv_ref.shape[0]
+def qkv_kernel(ids_ref, hidden_ref, gain_ref, wq_ref, wk_ref, wv_ref, *refs):
+    xhat_ref, scale_ref, normed_ref, first_ref, second_ref, held_ref, wide_ref, sems = refs
+    copies = [
+        pltpu.make_async_copy(w_ref, held_ref.at[i], sems.at[i])
+        for i, w_ref in enumerate((wq_ref, wk_ref, wv_ref))
+    ]
+    for copy in copies:
+        copy.start()
+    xhat, scale = norm_stats(hidden_ref[...])
+    xhat_ref[...] = xhat
+    scale_ref[...] = scale
+    normed = (xhat * gain_ref[...]).astype(BF)
+    normed_ref[...] = normed
+    half = first_ref.shape[1]
+    low_lane = lax.broadcasted_iota(jnp.int32, (half, LANES), 1) < HEAD_DIM
+    for i, copy in enumerate(copies):
+        copy.wait()
+        wide_ref[...] = mm(normed, held_ref[i], NN)
+        lanes = slice(i * LANES, (i + 1) * LANES)
+        for s in range(first_ref.shape[0]):
+            at = pair_lanes(s, ids_ref[0])
+            upper, lower = wide_ref[:half, at], wide_ref[half:, at]
+            first = jnp.where(low_lane, upper, pltpu.roll(lower, HEAD_DIM, 1))
+            second = jnp.where(low_lane, pltpu.roll(upper, HEAD_DIM, 1), lower)
+            first_ref[s, :, lanes] = first.astype(BF)
+            second_ref[s, :, lanes] = second.astype(BF)
+
+
+def qkv_call(ids, hidden, gain, weights, blocks):
+    rows, width = hidden.shape
+    low = shape_of((rows, width), BF)
+    packed = shape_of((blocks, rows // 2, 3 * LANES), BF)
+    outs = [shape_of((rows, width), F32), shape_of((rows, 1), F32), low, packed, packed]
+    return pl.pallas_call(
+        qkv_kernel,
+        grid=(1,),
+        out_shape=in_hbm(outs),
+        in_specs=[
+            SMEM_SPEC,
+            whole_spec(hidden),
+            whole_spec(gain),
+            *[pl.BlockSpec(memory_space=pl.ANY)] * 3,
+        ],
+        out_specs=[whole_spec(a) for a in outs],
+        scratch_shapes=[
+            pltpu.VMEM((3, width, width), BF),
+            pltpu.VMEM((rows, width), F32),
+            pltpu.SemaphoreType.DMA((3,)),
+        ],
+        compiler_params=pltpu.CompilerParams(vmem_limit_bytes=24 * 2**20),
+        cost_estimate=takes(6),
+        name="qkv",
+    )(ids, *from_hbm([hidden, gain, *weights]))
+
+
+def fwd_kernel(h, coef_ref, qkv_ref, qx_ref, kx_ref, o_ref, olow_ref, qb_ref, ka_ref, va_ref, s_ref):
+    half = qkv_ref.shape[1]
+    seq_len = 2 * half * qkv_ref.shape[0]
     blocks = seq_len // TILE
-    heads = qx_ref.shape[0]
-    for h in range(heads):
-        lo = h * HEAD_DIM
-
-        def prepare(b, carry, h=h):
-            rows = pl.ds(pl.multiple_of(b * TILE, TILE), TILE)
-            low_lane = lax.broadcasted_iota(jnp.int32, (TILE, LANES), 1) < HEAD_DIM
-            q = head_first(qkv_ref[rows, :LANES], h) * 0.125
-            k = head_first(qkv_ref[rows, LANES : 2 * LANES], h)
-            v = head_first(qkv_ref[rows, 2 * LANES :], h)
-            lane = lax.broadcasted_iota(jnp.int32, (TILE, LANES), 1)
-            ka_ref[h, rows, :] = jnp.where(low_lane, k, kx_ref[rows, :].astype(F32)).astype(BF)
-            va_ref[h, rows, :] = jnp.where(
+    slope = coef_ref[h, 6]
+
+    def prepare(b, carry):
+        lane = lax.broadcasted_iota(jnp.int32, (half, LANES), 1)
+        low_lane = lane < HEAD_DIM
+        for side in range(2):
+            rows = pl.ds(pl.multiple_of((2 * b + side) * half, half), half)
+            q, k, v = (
+                head_first(qkv_ref[b, :, i * LANES : (i + 1) * LANES], side) for i in range(3)
+            )
+            ka_ref[rows, :] = jnp.where(low_lane, k, kx_ref[rows, :].astype(F32)).astype(BF)
+            va_ref[rows, :] = jnp.where(
                 low_lane, v, jnp.where(lane < HEAD_DIM + 3, 1.0, 0.0)
             ).astype(BF)
+            q = (q.astype(BF).astype(F32) * 0.125).astype(BF).astype(F32)
             for s in range(2):
-                qb_ref[h, s, rows, :] = jnp.where(
-                    low_lane, q, qx_ref[h, s, rows, :].astype(F32)
+                qb_ref[s, rows, :] = jnp.where(
+                    low_lane, q, qx_ref[0, s, rows, :].astype(F32)
                 ).astype(BF)
-            return carry
-
-        lax.fori_loop(0, blocks, prepare, 0)
-
-        def one(qb, carry, h=h, lo=lo):
-            rows = pl.ds(pl.multiple_of(qb * TILE, TILE), TILE)
-            slope = coef_ref[h, 6]
-            top = None
-            for t in range(blocks):
-                kb = lax.rem(qb + t, blocks)
-                krows = pl.ds(pl.multiple_of(kb * TILE, TILE), TILE)
-                side = (kb > qb).astype(jnp.int32)
-                scores = mm(qb_ref[h, side, rows, :], ka_ref[h, krows, :], NT)
-                if t == 0:
-                    scores = scores - ahead_of(TILE, TILE, 1) * (2.0 * slope)
-                s_ref[:, t * TILE : (t + 1) * TILE] = scores
-                part = jnp.max(scores, axis=1, keepdims=True)
-                top = part if top is None else jnp.maximum(top, part)
-            acc = jnp.zeros((TILE, LANES), F32)
-            for t in range(blocks):
-                kb = lax.rem(qb + t, blocks)
-                krows = pl.ds(pl.multiple_of(kb * TILE, TILE), TILE)
-                probs = jnp.exp(s_ref[:, t * TILE : (t + 1) * TILE] - top).astype(BF)
-                acc = acc + mm(probs, va_ref[h, krows, :], NN)
-            total = acc[:, HEAD_DIM : HEAD_DIM + 1]
-            out = acc[:, :HEAD_DIM] / total
-            o_ref[rows, lo : lo + HEAD_DIM] = out
-            low = out.astype(BF)
-            per = olow_ref.shape[1]
-            for p in range(TILE // per):
-                olow_ref[qb * (TILE // per) + p, :, lo : lo + HEAD_DIM] = low[p * per : (p + 1) * per]
-            log_total = top + jnp.log(total)
-            lane = lax.broadcasted_iota(jnp.int32, (TILE, LANES), 1)
-            row_pos = (qb * TILE + lax.broadcasted_iota(jnp.int32, (TILE, 1), 0)).astype(F32)
-            for s in range(2):
-                base = row_pos * (slope * (1.0 if s else -1.0)) - log_total
-                full = qb_ref[h, s, rows, :].astype(F32)
-                for p, piece in enumerate(split3(base)):
-                    full = jnp.where(lane == HEAD_DIM + 6 + p, piece.astype(F32), full)
-                qb_ref[h, s, rows, :] = full.astype(BF)
-            return carry
-
-        lax.fori_loop(0, blocks, one, 0)
-
-
-def attn_fwd(coefs, qkv, qx, kx, blocks):
-    seq_len = qkv.shape[0]
-    heads = coefs.shape[0]
-    width = heads * HEAD_DIM
+        return carry
+
+    lax.fori_loop(0, qkv_ref.shape[0], prepare, 0)
+
+    def one(qb, carry):
+        rows = pl.ds(pl.multiple_of(qb * TILE, TILE), TILE)
+        top = None
+        for t in range(blocks):
+            kb = lax.rem(qb + t, blocks)
+            krows = pl.ds(pl.multiple_of(kb * TILE, TILE), TILE)
+            side = (kb > qb).astype(jnp.int32)
+            scores = mm(qb_ref[side, rows, :], ka_ref[krows, :], NT)
+            if t == 0:
+                scores = scores - ahead_of(TILE, TILE, 1) * (2.0 * slope)
+            s_ref[:, t * TILE : (t + 1) * TILE] = scores
+            part = jnp.max(scores, axis=1, keepdims=True)
+            top = part if top is None else jnp.maximum(top, part)
+        acc = jnp.zeros((TILE, LANES), F32)
+        for t in range(blocks):
+            kb = lax.rem(qb + t, blocks)
+            krows = pl.ds(pl.multiple_of(kb * TILE, TILE), TILE)
+            probs = jnp.exp(s_ref[:, t * TILE : (t + 1) * TILE] - top).astype(BF)
+            acc = acc + mm(probs, va_ref[krows, :], NN)
+        total = acc[:, HEAD_DIM : HEAD_DIM + 1]
+        out = acc[:, :HEAD_DIM] / total
+        o_ref[rows, :] = out
+        pack_rows(olow_ref, qb, 0, out.astype(BF))
+        log_total = top + jnp.log(total)
+        lane = lax.broadcasted_iota(jnp.int32, (TILE, LANES), 1)
+        row_pos = (qb * TILE + lax.broadcasted_iota(jnp.int32, (TILE, 1), 0)).astype(F32)
+        for s in range(2):
+            base = row_pos * (slope * (1.0 if s else -1.0)) - log_total
+            full = qb_ref[s, rows, :].astype(F32)
+            for p, piece in enumerate(split3(base)):
+                full = jnp.where(lane == HEAD_DIM + 6 + p, piece.astype(F32), full)
+            qb_ref[s, rows, :] = full.astype(BF)
+        return carry
+
+    lax.fori_loop(0, blocks, one, 0)
+
+
+def attn_fwd(h, coefs, qkv, qx, kx):
+    blocks, half, _ = qkv.shape
+    seq_len = 2 * half * blocks
     outs = [
-        shape_of((seq_len, width), F32),
-        shape_of((blocks, seq_len // blocks, width), BF),
-        shape_of((heads, 2, seq_len, LANES), BF),
-        shape_of((heads, seq_len, LANES), BF),
-        shape_of((heads, seq_len, LANES), BF),
+        shape_of((seq_len, HEAD_DIM), F32),
+        shape_of((blocks, half, LANES), BF),
+        shape_of((2, seq_len, LANES), BF),
+        shape_of((seq_len, LANES), BF),
+        shape_of((seq_len, LANES), BF),
     ]
     return pl.pallas_call(
-        fwd_kernel,
+        partial(fwd_kernel, h),
         grid=(1,),
         out_shape=in_hbm(outs),
-        in_specs=[SMEM_SPEC, *[whole_spec(a) for a in (qkv, qx, kx)]],
+        in_specs=[
+            SMEM_SPEC,
+            whole_spec(qkv),
+            pl.BlockSpec((1, *qx.shape[1:]), lambda i: (h, 0, 0, 0)),
+            whole_spec(kx),
+        ],
         out_specs=[whole_spec(a) for a in outs],
         scratch_shapes=[pltpu.VMEM((TILE, seq_len), F32)],
-        compiler_params=pltpu.CompilerParams(vmem_limit_bytes=48 * 2**20),
-        cost_estimate=SMALL_COST,
+        compiler_params=pltpu.CompilerParams(vmem_limit_bytes=36 * 2**20),
+        cost_estimate=takes(14),
         name="attn_fwd",
     )(coefs, *from_hbm([qkv, qx, kx]))
 
@@ -485,13 +544,13 @@
     def prepare(b, carry):
         rows = pl.ds(pl.multiple_of(b * TILE, TILE), TILE)
         go = go_ref[rows, lo : lo + HEAD_DIM].astype(F32)
-        delta = jnp.sum(go * o_ref[rows, lo : lo + HEAD_DIM], axis=1, keepdims=True)
+        delta = jnp.sum(go * o_ref[rows, :], axis=1, keepdims=True)
         lane = lax.broadcasted_iota(jnp.int32, (TILE, LANES), 1)
         full = jnp.where(lane < HEAD_DIM, head_first(go_ref[rows, :], h), 0.0)
         for p, piece in enumerate(split3(-delta)):
             full = jnp.where(lane == HEAD_DIM + p, piece.astype(F32), full)
         ga_ref[rows, :] = full.astype(BF)
-        kt_ref[:, rows] = ka_ref[0, rows, :].astype(F32).T.astype(BF)
+        kt_ref[:, rows] = ka_ref[rows, :].astype(F32).T.astype(BF)
         dq_ref[:, rows] = jnp.zeros((HEAD_DIM, TILE), F32)
         return carry
 
@@ -499,8 +558,8 @@
 
     def one(kb, carry):
         krows = pl.ds(pl.multiple_of(kb * TILE, TILE), TILE)
-        ka = ka_ref[0, krows, :]
-        va = va_ref[0, krows, :]
+        ka = ka_ref[krows, :]
+        va = va_ref[krows, :]
         kt = kt_ref[:HEAD_DIM, krows]
         dv = jnp.zeros((TILE, LANES), F32)
         dk = jnp.zeros((TILE, LANES), F32)
@@ -508,7 +567,7 @@
             qb = lax.rem(kb + t, blocks)
             rows = pl.ds(pl.multiple_of(qb * TILE, TILE), TILE)
             ga = ga_ref[rows, :]
-            qa = qb_ref[0, (kb > qb).astype(jnp.int32), rows, :]
+            qa = qb_ref[(kb > qb).astype(jnp.int32), rows, :]
             scores = mm(ka, qa, NT)
             if t == 0:
                 scores = scores - ahead_of(TILE, TILE, 0) * (2.0 * slope)
@@ -535,15 +594,11 @@
     seq_len = go.shape[0]
     half = seq_len // (2 * blocks)
 
-    def of_head(array):
-        zeros = (0,) * (len(array.shape) - 1)
-        return pl.BlockSpec((1, *array.shape[1:]), lambda i: (h, *zeros))
-
     return pl.pallas_call(
         partial(bwd_kernel, h),
         grid=(1,),
         out_shape=pltpu.HBM((blocks, half, 3 * LANES), BF),
-        in_specs=[SMEM_SPEC, whole_spec(go), whole_spec(o), of_head(qb), of_head(ka), of_head(va)],
+        in_specs=[SMEM_SPEC, *[whole_spec(a) for a in (go, o, qb, ka, va)]],
         out_specs=pl.BlockSpec((blocks, half, 3 * LANES), lambda i: (0, 0, 0)),
         scratch_shapes=[
             pltpu.VMEM((seq_len, LANES), BF),
@@ -551,7 +606,7 @@
             pltpu.VMEM((LANES, seq_len), BF),
         ],
         compiler_params=pltpu.CompilerParams(vmem_limit_bytes=36 * 2**20),
-        cost_estimate=SMALL_COST,
+        cost_estimate=takes(16),
         name="attn_bwd",
     )(coefs, *from_hbm([go, o, qb, ka, va]))
 
@@ -581,12 +636,12 @@
     return pl.pallas_call(
         slab_kernel,
         grid=(blocks,),
-        out_shape=pltpu.HBM((blocks, 3 * block, LANES), BF),
+        out_shape=pltpu.HBM((blocks // 2, 3 * block, 2 * LANES), BF),
         in_specs=[pl.BlockSpec((seq_len, block), lambda b: (0, b)), packed, packed],
-        out_specs=pl.BlockSpec((1, 3 * block, LANES), lambda b: (b, 0, 0)),
+        out_specs=pl.BlockSpec((1, 3 * block, LANES), lambda b: (b // 2, 0, b % 2)),
         scratch_shapes=[pltpu.VMEM((seq_len, 3 * LANES), BF)],
         compiler_params=pltpu.CompilerParams(vmem_limit_bytes=24 * 2**20),
-        cost_estimate=SMALL_COST,
+        cost_estimate=takes(9),
         name="slab",
     )(*from_hbm([left, first, second]))
 
@@ -616,9 +671,17 @@
         out[level, first : first + rows, :] = wide_ref[:, pl.ds(at, cols)]
 
 
-def row_kernel(came_ref, hidden_ref, wo_ref, gain_ref, attn_ref, xhat_ref, scale_ref, nf_ref, res_ref):
-    for s in range(came_ref.shape[0]):
-        attn_ref[:, s * LANES : (s + 1) * LANES] = came_ref[s]
+def pair_lanes(source, dp):
+    at = (jnp.bitwise_xor(source // 2, dp) * 2 + source % 2) * LANES
+    return pl.ds(pl.multiple_of(at, LANES), LANES)
+
+
+def row_kernel(ids_ref, first_ref, second_ref, hidden_ref, wo_ref, gain_ref, attn_ref, xhat_ref, scale_ref, nf_ref, res_ref):
+    half = first_ref.shape[1]
+    for s in range(first_ref.shape[0]):
+        upper, lower = unpack_pair(first_ref[s], second_ref[s])
+        attn_ref[:half, pair_lanes(s, ids_ref[0])] = upper
+        attn_ref[half:, pair_lanes(s, ids_ref[0])] = lower
     residual = hidden_ref[...] + mm(attn_ref[...], wo_ref[...], NN)
     xhat, scale = norm_stats(residual)
     xhat_ref[...] = xhat
@@ -627,21 +690,21 @@
     res_ref[...] = residual
 
 
-def row_call(came, hidden, w_output, gain):
+def row_call(ids, came, hidden, w_output, gain):
     rows, width = hidden.shape
     wide, low = shape_of((rows, width), F32), shape_of((rows, width), BF)
-    inputs = [came, hidden, w_output, gain]
+    inputs = [*came, hidden, w_output, gain]
     outs = [low, wide, shape_of((rows, 1), F32), low, wide]
     return pl.pallas_call(
         row_kernel,
         grid=(1,),
         out_shape=in_hbm(outs),
-        in_specs=[whole_spec(a) for a in inputs],
+        in_specs=[SMEM_SPEC, *[whole_spec(a) for a in inputs]],
         out_specs=[whole_spec(a) for a in outs],
         compiler_params=pltpu.CompilerParams(vmem_limit_bytes=16 * 2**20),
-        cost_estimate=SMALL_COST,
+        cost_estimate=takes(5),
         name="attn_rows",
-    )(*from_hbm(inputs))
+    )(ids, *from_hbm(inputs))
 
 
 def ffn_kernel(
@@ -713,14 +776,14 @@
         ),
         out_shape=in_hbm([out_sum] * 4 + [out_grad]),
         compiler_params=pltpu.CompilerParams(vmem_limit_bytes=44 * 2**20),
-        cost_estimate=SMALL_COST,
+        cost_estimate=takes(13),
         name="ffn",
     )(ids, *from_hbm([*inputs, w_up, w_down]))
 
 
 def branch_kernel(
-    gnf_a, came_a, gnf_b, came_b, xhat_ref, scale_ref, gain_ref, cot_ref, wo_ref,
-    resid_ref, branch_ref, gattn_ref, ggain_ref,
+    ids_ref, gnf_a, came_a, gnf_b, came_b, xhat_ref, scale_ref, gain_ref, cot_ref, wo_ref,
+    resid_ref, branch_ref, gattn_ref, ggain_ref, wide_ref,
 ):
     gnf = gnf_a[...] + came_a[...] + gnf_b[...] + came_b[...]
     rows, ggain = norm_back(gnf, xhat_ref[...], scale_ref[...], gain_ref[...])
@@ -729,12 +792,12 @@
     resid_ref[...] = resid
     branch = resid.astype(BF)
     branch_ref[...] = branch
-    gattn = mm(branch, wo_ref[...], NT).astype(BF)
+    wide_ref[...] = mm(branch, wo_ref[...], NT).astype(BF)
     for s in range(gattn_ref.shape[0]):
-        gattn_ref[s] = gattn[:, s * LANES : (s + 1) * LANES]
-
-
-def branch_call(gnf, xhat, scale, gain, cot, w_output, blocks):
+        gattn_ref[s] = wide_ref[:, pair_lanes(s, ids_ref[0])]
+
+
+def branch_call(ids, gnf, xhat, scale, gain, cot, w_output, blocks):
     rows, width = xhat.shape
     wide, low = shape_of((rows, width), F32), shape_of((rows, width), BF)
     inputs = [*gnf, xhat, scale, gain, cot, w_output]
@@ -743,12 +806,13 @@
         branch_kernel,
         grid=(1,),
         out_shape=in_hbm(outs),
-        in_specs=[whole_spec(a) for a in inputs],
+        in_specs=[SMEM_SPEC, *[whole_spec(a) for a in inputs]],
         out_specs=[whole_spec(a) for a in outs],
+        scratch_shapes=[pltpu.VMEM((rows, width), BF)],
         compiler_params=pltpu.CompilerParams(vmem_limit_bytes=20 * 2**20),
-        cost_estimate=SMALL_COST,
+        cost_estimate=takes(6),
         name="branch",
-    )(*from_hbm(inputs))
+    )(ids, *from_hbm(inputs))
 
 
 GAIN_ROWS = 16
@@ -797,13 +861,13 @@
         ),
         out_shape=in_hbm(outs),
         compiler_params=pltpu.CompilerParams(vmem_limit_bytes=24 * 2**20),
-        cost_estimate=SMALL_COST,
+        cost_estimate=takes(6),
         name="wgrad",
     )(ids, *from_hbm([*flat, *rights]))
 
 
 def tail_kernel(
-    first_ref, second_ref, wq_ref, wk_ref, wv_ref, xhat_ref, scale_ref, gain_ref, resid_ref, ggain_ref,
+    ids_ref, first_ref, second_ref, wq_ref, wk_ref, wv_ref, xhat_ref, scale_ref, gain_ref, resid_ref, ggain_ref,
     gh_ref, wide_ref,
 ):
     total = None
@@ -812,8 +876,8 @@
         lanes = slice(i * LANES, (i + 1) * LANES)
         for s in range(first_ref.shape[0]):
             upper, lower = unpack_pair(first_ref[s, :, lanes], second_ref[s, :, lanes])
-            wide_ref[:half, s * LANES : (s + 1) * LANES] = upper
-            wide_ref[half:, s * LANES : (s + 1) * LANES] = lower
+            wide_ref[:half, pair_lanes(s, ids_ref[0])] = upper
+            wide_ref[half:, pair_lanes(s, ids_ref[0])] = lower
         term = mm(wide_ref[...], w_ref[...], NT)
         total = term if total is None else total + term
     rows, ggain = norm_back(total, xhat_ref[...], scale_ref[...], gain_ref[...])
@@ -824,20 +888,20 @@
     gh_ref[count:] = gains.astype(BF)
 
 
-def tail_call(came, weights, xhat, scale, gain, resid, ggain):
+def tail_call(ids, came, weights, xhat, scale, gain, resid, ggain):
     rows, width = xhat.shape
     inputs = [*came, *weights, xhat, scale, gain, resid, ggain]
     return pl.pallas_call(
         tail_kernel,
         grid=(1,),
         out_shape=pltpu.HBM((rows + GAIN_ROWS, width), BF),
-        in_specs=[whole_spec(a) for a in inputs],
+        in_specs=[SMEM_SPEC, *[whole_spec(a) for a in inputs]],
         out_specs=whole_spec(shape_of((rows + GAIN_ROWS, width), BF)),
         scratch_shapes=[pltpu.VMEM((rows, width), BF)],
         compiler_params=pltpu.CompilerParams(vmem_limit_bytes=32 * 2**20),
-        cost_estimate=SMALL_COST,
+        cost_estimate=takes(8),
         name="tail",
-    )(*from_hbm(inputs))
+    )(ids, *from_hbm(inputs))
 
 
 def add_low(left, right):
@@ -853,6 +917,7 @@
 
 
 CORE_SWAP = [(i, i ^ 1) for i in range(8)]
+TO_OWNERS = [(p * 8 + b, (p ^ (b // 2)) * 8 + b) for p in range(4) for b in range(8)]
 DP_STEPS = [[(i, i ^ k) for i in range(4)] for k in (1, 2, 3)]
 Z_NEAR = [(i, i ^ 2) for i in range(8)]
 Z_FAR = [(i, i ^ 4) for i in range(8)]
@@ -873,12 +938,13 @@
     return total.astype(BF)
 
 
-def z_near(total, level):
-    near, far = jnp.bitwise_xor(level, 1), jnp.bitwise_xor(level, 2)
-    opposite = jnp.bitwise_xor(level, 3)
-    send = jnp.stack([pick(total, near, 0), pick(total, opposite, 0)])
-    keep = jnp.stack([pick(total, level, 0), pick(total, far, 0)])
-    return lax.ppermute(send, "blk", Z_NEAR), keep, send
+def z_near(totals, level):
+    def two(first, second):
+        picked = [jnp.stack([pick(t, first, 0), pick(t, second, 0)]) for t in totals]
+        return jnp.concatenate(picked, axis=1) if len(picked) > 1 else picked[0]
+
+    send = two(jnp.bitwise_xor(level, 1), jnp.bitwise_xor(level, 3))
+    return lax.ppermute(send, "blk", Z_NEAR), two(level, jnp.bitwise_xor(level, 2)), send
 
 
 def z_far(came, keep):
@@ -890,6 +956,99 @@
     two = jnp.stack([piece, lax.ppermute(piece, "blk", Z_FAR)])
     four = jnp.concatenate([two, lax.ppermute(two, "blk", Z_NEAR)])
     return four, core_swap(four)
+
+
+def assemble_kernel(n_out, a_ref, b_ref, down_ref, up_ref, out_ref, *head_refs):
+    core = pl.program_id(1)
+    cols = a_ref.shape[2]
+    tile = a_ref.shape[1] // 2
+    for part, ref in enumerate((a_ref, b_ref)):
+        down_ref[0, part, 0] = ref[0, :tile].astype(F32)
+        at = pl.multiple_of((part * 2 + core) * cols, cols)
+        up_ref[:, pl.ds(at, cols)] = ref[0, tile : 2 * tile].astype(F32)
+    out_ref[...] = b_ref[0, 2 * tile : 2 * tile + n_out].astype(F32)
+    half = head_refs[0].shape[0] // 2
+    for i, ref in enumerate(head_refs):
+        first = 2 * tile + n_out + i * half
+        lanes = pl.ds(pl.multiple_of(core * LANES, LANES), LANES)
+        for side in range(2):
+            ref[side * half : (side + 1) * half, lanes] = b_ref[
+                0, first : first + half, side * LANES : (side + 1) * LANES
+            ].astype(F32)
+
+
+def assemble_call(whole_a, whole_b, n_out):
+    blocks, rows_a, cols = whole_a.shape
+    levels, tile = blocks // 2, rows_a // 2
+    outs = [
+        shape_of((levels, 2, 2, tile, cols), F32),
+        shape_of((levels * tile, 4 * cols), F32),
+        shape_of((blocks * n_out, cols), F32),
+        *[shape_of((levels * tile, cols), F32)] * 3,
+    ]
+    return pl.pallas_call(
+        partial(assemble_kernel, n_out),
+        grid=(levels, 2),
+        out_shape=in_hbm(outs),
+        in_specs=[
+            pl.BlockSpec((1, *w.shape[1:]), lambda z, c: (z * 2 + c, 0, 0))
+            for w in (whole_a, whole_b)
+        ],
+        out_specs=[
+            pl.BlockSpec((1, 2, 1, tile, cols), lambda z, c: (z, 0, c, 0, 0)),
+            pl.BlockSpec((tile, 4 * cols), lambda z, c: (z, 0)),
+            pl.BlockSpec((n_out, cols), lambda z, c: (z * 2 + c, 0)),
+            *[pl.BlockSpec((tile, cols), lambda z, c: (z, 0))] * 3,
+        ],
+        compiler_params=pltpu.CompilerParams(vmem_limit_bytes=24 * 2**20),
+        cost_estimate=takes(9),
+        name="assemble",
+    )(*from_hbm([whole_a, whole_b]))
+
+
+def skip_kernel(at_ref, own_ref, other_ref, out_ref, gain_ref):
+    block = out_ref.shape[3]
+    for c in range(2):
+
+        def put(ref, c=c):
+            for i in range(2):
+                out_ref[i, 0, c] = ref[0, i * block : (i + 1) * block].astype(F32)
+
+            if c == 0:
+
+                @pl.when(pl.program_id(0) == 0)
+                def _():
+                    gain_ref[...] = ref[0, 2 * block :].astype(F32)
+
+        pl.when(at_ref[1] == c)(partial(put, own_ref))
+        pl.when(at_ref[1] != c)(partial(put, other_ref))
+
+
+def skip_call(at, own, others):
+    levels, rows, cols = own.shape
+    block = (rows - GAIN_ROWS) // 2
+
+    def place(z, at):
+        k = jnp.bitwise_xor(z, at[0])
+        return ((k % 2) * 2 + k // 2, 0, 0)
+
+    outs = [shape_of((2, levels, 2, block, cols), F32), shape_of((GAIN_ROWS, cols), F32)]
+    return pl.pallas_call(
+        skip_kernel,
+        grid_spec=pltpu.PrefetchScalarGridSpec(
+            num_scalar_prefetch=1,
+            grid=(levels,),
+            in_specs=[pl.BlockSpec((1, rows, cols), place)] * 2,
+            out_specs=[
+                pl.BlockSpec((2, 1, 2, block, cols), lambda z, at: (0, z, 0, 0, 0)),
+                pl.BlockSpec((GAIN_ROWS, cols), lambda z, at: (0, 0)),
+            ],
+        ),
+        out_shape=in_hbm(outs),
+        compiler_params=pltpu.CompilerParams(vmem_limit_bytes=16 * 2**20),
+        cost_estimate=takes(4),
+        name="skip",
+    )(at, *from_hbm([own, others]))
 
 
 def on_device_grid(
@@ -918,33 +1077,36 @@
 
     joined = jnp.concatenate([frames, skip_feats], axis=1)
     hidden = product("rc,cd->rd", joined, w_skip)
-    xhat_attn, scale_attn = norm_stats(hidden)
-    normed = (xhat_attn * gain_attn).astype(BF)
-    normed_all = lax.all_gather(normed, "blk", axis=0, tiled=True)
-
-    slopes = lax.dynamic_slice_in_dim(alibi_slopes(seq_len), blk * 2, 2, 0)
+    core, level = blk % 2, blk // 2
+    ids = jnp.stack([dp, core]).astype(jnp.int32)
+
+    def behind(values, *others):
+        return [after(v, *others) for v in values]
+
+    def exchange(values):
+        return lax.all_to_all(values, "blk", 0, 0, tiled=True)
+
+    xhat_attn, scale_attn, normed, send_first, send_second = qkv_call(
+        ids, hidden, gain_attn.reshape(1, width), (w_query, w_key, w_value), blocks
+    )
+    qkv_first = exchange(send_first)
+    mine = jnp.bitwise_xor(level, dp) * 2 + core
+    slopes = lax.dynamic_slice_in_dim(alibi_slopes(seq_len), mine * 2, 2, 0)
     coefs, qx, kx = attn_tables(utt_lengths[0], padded_lengths[0], slopes, seq_len)
-    w_mine = jnp.concatenate(
-        [lax.dynamic_slice_in_dim(w, blk * pair, pair, 1) for w in (w_query, w_key, w_value)],
-        axis=1,
-    )
-    qkv = product("rd,de->re", normed_all, w_mine).astype(BF)
-    attn_wide, attn_low, qb, ka, va = attn_fwd(coefs, qkv, qx, kx, blocks)
-
-    core, level = blk % 2, blk // 2
+    qkv_second = exchange(after(send_second, qkv_first))
+    o_first, low_first, *kept_first = attn_fwd(0, coefs, qkv_first, qx, kx)
+    qkv_second = after(qkv_second, low_first)
+    came_first = exchange(after(low_first, qkv_second))
+    o_second, low_second, *kept_second = attn_fwd(1, coefs, qkv_second, qx, kx)
+    came_second = exchange(after(low_second, came_first))
+    normed_all = lax.all_gather(after(normed, came_second), "blk", axis=0, tiled=True)
+
     levels = blocks // 2
     cols = width // shards
-    ids = jnp.stack([dp, core]).astype(jnp.int32)
     gain_row = gain_ffn.reshape(1, width)
 
-    def behind(values, *others):
-        return [after(v, *others) for v in values]
-
-    def exchange(values):
-        return lax.all_to_all(values, "blk", 0, 0, tiled=True)
-
     attn, xhat_ffn, scale_ffn, nf, residual = row_call(
-        exchange(attn_low), hidden, w_output, gain_row
+        ids, (came_first, came_second), hidden, w_output, gain_row
     )
     cot = (cotangent, core_swap(cotangent))
     joined_pairs = [(frames, core_swap(frames)), (skip_feats, core_swap(skip_feats))]
@@ -954,6 +1116,7 @@
     gnf_a_came = core_swap(gnf_a_send)
     mix_b, mix_b_send, gnf_b, gnf_b_send, share_b = ffn_call(ids, nf, cot, w_up, w_down, shards, 1)
     grad_residual, grad_branch, grad_attn, ggain_ffn = branch_call(
+        ids,
         (gnf_a, gnf_a_came, gnf_b, core_swap(gnf_b_send)),
         xhat_ffn,
         scale_ffn,
@@ -962,32 +1125,36 @@
         w_output,
         blocks,
     )
+    grad_attn = after(grad_attn, normed_all)
     grad_attn_came = exchange(grad_attn).reshape(seq_len, pair)
     mix_send = after(mix_a_send, grad_branch) + mix_b_send
     mixed = (residual + mix_a + mix_b + core_swap(mix_send)).astype(BF)
     swapped = core_swap(jnp.stack([attn, grad_branch]))
-    (share_c,) = wgrad_call(
-        ids, [(attn, swapped[0])], (grad_branch, swapped[1]), shards, levels, False
-    )
-    n_out = share_c.shape[2]
-    share_b = jnp.concatenate([share_b, share_c], axis=2)
     sum_b = lax.psum_scatter(share_b, "dp", scatter_dimension=0)
 
-    bwd = partial(attn_bwd, coefs=coefs, o=attn_wide, qb=qb, ka=ka, va=va, blocks=blocks)
-    dq_first = bwd(0, go=after(grad_attn_came, share_b))
-    came_first = exchange(dq_first)
-    za, keep_za, send = z_near(after(sum_a, dq_first), level)
-    dq_second = bwd(1, go=after(grad_attn_came, send))
-
-    came_second = exchange(after(dq_second, came_first))
+    def bwd(h, go):
+        o, (qb, ka, va) = ((o_first, kept_first), (o_second, kept_second))[h]
+        return attn_bwd(h, coefs, go, o, qb, ka, va, blocks)
+
+    dq_first = bwd(0, grad_attn_came)
+    za, keep_za, send = z_near([after(sum_a, dq_first)], level)
+    came_first = exchange(after(dq_first, send))
+    dq_second = bwd(1, after(grad_attn_came, send))
+
     za_far, keep_za, send = z_far(after(za, dq_second), keep_za)
     slab = slab_call(after(normed_all, send), dq_first, dq_second)
-    zb, keep_zb, send = z_near(after(sum_b, slab), level)
-    piece_a = add_low(keep_za, after(za_far, send))
+    piece_a = add_low(keep_za, after(za_far, slab))
     whole_a = lax.all_gather(piece_a, "blk", axis=0, tiled=False)
-    slab = exchange(after(slab, came_second))
+    came_second = exchange(after(dq_second, came_first, piece_a))
+    heads = lax.ppermute(slab, ("dp", "blk"), TO_OWNERS)
+    share_c = wgrad_call(
+        ids, [(attn, swapped[0])], (after(grad_branch, slab), swapped[1]), shards, levels, True
+    )
+    n_out = share_c[0].shape[1]
+    xc = dp_send(share_c)
     gh = tail_call(
-        behind((came_first, came_second), piece_a),
+        ids,
+        behind((came_first, came_second), *share_c),
         (w_query, w_key, w_value),
         xhat_attn,
         scale_attn,
@@ -995,65 +1162,30 @@
         grad_residual,
         ggain_ffn,
     )
-    share_d = wgrad_call(ids, joined_pairs, (gh, core_swap(gh)), shards, levels, True)
+    gh_came = core_swap(gh)
+    sum_c = sum_low(behind(xc, gh), share_c[0])
+    zb, keep_zb, send = z_near((after(sum_b, slab), sum_c, after(heads, gh)), level)
+    share_d = wgrad_call(ids, joined_pairs, (after(gh, send), gh_came), shards, levels, True)
     xd = dp_send(share_d)
     zb_far, keep_zb, send = z_far(after(zb, *share_d), keep_zb)
-    slab = after(slab, send).reshape(shards, 2, -1, pair)
-    heads = [pick(slab, jnp.bitwise_xor(dp, k), 0) for k in range(4)]
-    xh = dp_send(heads)
-    grad_joined = product("rd,cd->rc", after(gh, *heads)[:row_count], w_skip)
+    grad_joined = product("rd,cd->rc", after(gh, send)[:row_count], w_skip)
     grad_frames = grad_joined[:, :width].astype(BF)
     grad_skip = grad_joined[:, width:].astype(BF)
 
     sum_d = sum_low(behind(xd, grad_joined), share_d[0])
-    zd, keep_zd, send = z_near(sum_d, level)
+    zd, keep_zd, send = z_near([sum_d], level)
+    zd_far, keep_zd, send = z_far(after(zd, send), keep_zd)
     piece_b = add_low(keep_zb, after(zb_far, send))
-    piece_h = sum_low(behind(xh, piece_b), heads[0])
-    piece_h = piece_h.transpose(1, 0, 2).reshape(-1, cols)
-    piece_b = jnp.concatenate([piece_b, piece_h], axis=0)
     whole_b = lax.all_gather(piece_b, "blk", axis=0, tiled=False)
-    zd_far, keep_zd, send = z_far(after(zd, piece_b), keep_zd)
-    piece_d = add_low(keep_zd, zd_far)
-    mine, others = gather_near(piece_d)
-    by_core = [jnp.where(core == 0, mine, others), jnp.where(core == 0, others, mine)]
-
-    def take(whole, first, count):
-        return whole[:, first : first + count].astype(F32)
-
-    tile = share_a.shape[2] // 2
-    downs = [take(w, 0, tile).reshape(levels, 2, tile, cols) for w in (whole_a, whole_b)]
-    g_down = jnp.stack(downs, axis=1).reshape(-1, cols)
-    ups = [take(w, tile, tile).reshape(levels, 2, tile, cols) for w in (whole_a, whole_b)]
-    g_up = jnp.concatenate([u[:, c].reshape(-1, cols) for u in ups for c in range(2)], axis=1)
-    g_output = take(whole_b, 2 * tile, n_out).reshape(-1, cols)
-    n_head = width // blocks
-    g_heads = [
-        take(whole_b, 2 * tile + n_out + i * n_head, n_head).reshape(-1, cols) for i in range(3)
-    ]
-    n_skip = (share_d[0].shape[1] - GAIN_ROWS) // 2
-    place = [0, 2, 1, 3]
-    pieces = [
-        [
-            pick(by_core[c], jnp.asarray(place, jnp.int32)[jnp.bitwise_xor(level, at)], 0)
-            for c in range(2)
-        ]
-        for at in range(levels)
-    ]
-    g_skip = jnp.concatenate(
-        [
-            pieces[at][c][i * n_skip : (i + 1) * n_skip]
-            for i in range(2)
-            for at in range(levels)
-            for c in range(2)
-        ],
-        axis=0,
-    ).astype(F32)
-    g_gains = pieces[0][0][2 * n_skip :].astype(F32)
+    piece_d = add_low(keep_zd, after(zd_far, piece_b))
+    g_down, g_up, g_output, *g_heads = assemble_call(whole_a, whole_b, n_out)
+    own, others = gather_near(piece_d)
+    g_skip, g_gains = skip_call(jnp.stack([level, core]).astype(jnp.int32), own, others)
     return (
         mixed,
         grad_frames,
         grad_skip,
-        g_skip,
+        g_skip.reshape(-1, cols),
         g_gains[0],
         g_heads[0],
         g_heads[1],
@@ -1061,7 +1193,7 @@
         g_output,
         g_gains[1],
         g_up,
-        g_down,
+        g_down.reshape(-1, cols),
     )
 
 

time: 444 us -> 406 us (0.914)
  Pallas kernels: 128 us -> 153 us
  other arithmetic: 32.5 us -> 7.61 us
  waiting for transfers between devices: 162 us -> 138 us
  starting transfers between devices: 44 us -> 54.7 us
  matrix products: 14.1 us -> 6.99 us
  between operations: 22.4 us -> 15.8 us
  local copies, waits for them, and re-layouts: 19.6 us -> 13.2 us
    all_gather x1, waiting for transfers between devices: 42.1 us -> 0.01 us  [on_device_grid(): lax.all_gather(after(normed, came_second), 'blk', axis=0, tiled=True)]
    ppermute x3, waiting for transfers between devices: 37.8 us -> 12.8 us  [z_far(): return (lax.ppermute(send, 'blk', Z_FAR), add_low(keep[0], came[0]), send)]
    pallas_call x3 -> x7, Pallas kernels: 40.6 us -> 64.6 us  [the longest x2 29.9 us: attn_fwd(): pl.pallas_call(partial(fwd_kernel, h), grid=(1,), out_shape=in_hbm(outs),...]
    all_to_all x4 -> x6, waiting for transfers between devices: 15.9 us -> 38.6 us  [exchange(): return lax.all_to_all(values, 'blk', 0, 0, tiled=True)]
    ppermute x1, waiting for transfers between devices: 7.15 us -> 24.6 us  [gather_near(): four = jnp.concatenate([two, lax.ppermute(two, 'blk', Z_NEAR)])]
    ppermute x3 -> x4, starting transfers between devices: 3.74 us -> 15.7 us  [the longest x3 8.3 us: z_near(): lax.ppermute(send, 'blk', Z_NEAR)]
    concatenate x3 -> x2, other arithmetic: 7.62 us -> 0.14 us  [two(): return jnp.concatenate(picked, axis=1) if len(picked) > 1 else picked[0]]
    dot_general x3 -> x2, matrix products: 14.1 us -> 6.99 us  [product(): return jnp.einsum(form, left, right, preferred_element_type=jnp.float32)]
  transfers between devices with their start and end apart: 33 -> 36, of which waited for: 16 -> 15; matrix products, arithmetic and copies ran while one was open for 8% -> 4% of each run, Pallas kernels for 20% -> 34%
where the time goes in v3:
time: 406 us; the launch traced here: 404 us
  Pallas kernels  153 us (38%)
  waiting for transfers between devices  138 us (34%)
  starting transfers between devices  54.7 us (13%)
  between operations  15.8 us (4%)
  blocking collectives  14.8 us (4%)
  local copies, waits for them, and re-layouts  13.2 us (3%)
  other arithmetic  7.61 us (2%)
  matrix products  6.99 us (2%)
    all_to_all x6, waiting for transfers between devices, exchange(): return lax.all_to_all(values, 'blk', 0, 0, tiled=True)  38.6 us
    ppermute x3, waiting for transfers between devices, z_near(): lax.ppermute(send, 'blk', Z_NEAR)  34.8 us
    pallas_call x2, Pallas kernels, attn_bwd(): pl.pallas_call(partial(bwd_kernel, h), grid=(1,), out_shape=pltpu.HBM((bl...  32.6 us
    pallas_call x2, Pallas kernels, attn_fwd(): pl.pallas_call(partial(fwd_kernel, h), grid=(1,), out_shape=in_hbm(outs),...  29.9 us
    pallas_call x2, Pallas kernels, ffn_call(): pl.pallas_call(ffn_kernel, grid_spec=pltpu.PrefetchScalarGridSpec(num_sca...  26.5 us
    all_to_all x6, starting transfers between devices, exchange(): return lax.all_to_all(values, 'blk', 0, 0, tiled=True)  25 us
    ppermute x1, waiting for transfers between devices, gather_near(): four = jnp.concatenate([two, lax.ppermute(two, 'blk', Z_NEAR)])  24.6 us
    ppermute x1, waiting for transfers between devices, gather_near(): two = jnp.stack([piece, lax.ppermute(piece, 'blk', Z_FAR)])  18.1 us
  transfers between devices with their start and end apart: 36, of which 15 were waited for; matrix products, arithmetic and copies ran while one was open for 4% of the time, Pallas kernels for 34%

profile of v3, /device:TPU:0, one launch (start us, length us, event | category | flops | bytes accessed | tf_op | source)
XLA Modules:
  0.0 404.0 jit_solution(5348936873000633449)
XLA Ops:
  8.1 4.7 %fusion.hidden_ref = f32[256,1024]{1,0:T(8,128)} fusion(bf16[2048,1024]{1,0:T(8,128)(2,1)} %param.16, bf16[256,1024]{1,0:T(8,128)(2,1)} %refs_2_.1, bf16[256,1024]{1,0:T(8,128)(2,1)} %refs_0_.1), kind=kOutput, calls=%fused_computation.1 | convolution fusion | flops 1075838976 | bytes 6291456 | tf_op jit(solution)/shard_map/rc,cd->rd/dot_general | solution.py:45
  12.8 7.4 %qkv.1 = (f32[256,1024]{1,0:T(8,128)}, f32[256,1]{1,0:T(8,128)}, bf16[256,1024]{1,0:T(8,128)(2,1)}, bf16[8,128,384]{2,1,0:T(8,128)(2,1)}, bf16[8,128,384]{2,1,0:T(8,128)(2,1)}) custom-call(s32[2]{0:T(128)S(1)} %pad_add_fusion.1.ids_ref, f32[256,1024]{1,0:T(8,128)} %fusion.hidden_ref, f32[1,1024]{1,0:T(1,128)} %bitcast.78, bf16[1024,1024]{1,0:T(8,128)(2,1)} %wq_ref.3, ...), custom_call_target="tpu_custom_call" | custom-call | flops 6899999744 | tf_op jit(solution)/shard_map/qkv/pallas_call | solution.py:407
  20.3 6.3 %all-to-all-start = ((bf16[8,128,384]{2,1,0:T(8,128)(2,1)}), bf16[8,128,384]{2,1,0:T(8,128)(2,1)S(1)}, u32[]{:S(2)}, u32[]{:S(2)}) async-start(bf16[8,128,384]{2,1,0:T(8,128)(2,1)} %get-tuple-element.95), calls=%async_computation | async-start | bytes 1572864 | tf_op jit(solution)/shard_map/all_to_all | solution.py:1087
  27.7 4.8 %attn_tables.1 = (bf16[2,2,2048,128]{3,2,1,0:T(8,128)(2,1)}, bf16[2048,128]{1,0:T(8,128)(2,1)}) custom-call(s32[3,4]{1,0:T(4,128)S(1)} %pad_add_fusion.seg_ref, f32[2,7]{1,0:T(2,128)S(1)} %stack.114.slope_ref.coef_ref), custom_call_target="tpu_custom_call" | custom-call | tf_op jit(solution)/shard_map/attn_tables/pallas_call | solution.py:349
  32.4 15.2 %all-to-all-done.qkv_ref = bf16[8,128,384]{2,1,0:T(8,128)(2,1)S(1)} async-done(((bf16[8,128,384]{2,1,0:T(8,128)(2,1)}), bf16[8,128,384]{2,1,0:T(8,128)(2,1)S(1)}, u32[]{:S(2)}, u32[]{:S(2)}) %all-to-all-start) | async-done | bytes 786464 | tf_op jit(solution)/shard_map/all_to_all | solution.py:1087
  47.6 3.5 all-to-all-start.1
  51.2 14.9 %attn_fwd.2 = (f32[2048,64]{1,0:T(8,128)}, bf16[8,128,128]{2,1,0:T(8,128)(2,1)}, bf16[2,2048,128]{2,1,0:T(8,128)(2,1)}, bf16[2048,128]{1,0:T(8,128)(2,1)}, bf16[2048,128]{1,0:T(8,128)(2,1)}) custom-call(f32[2,7]{1,0:T(2,128)S(1)} %stack.114.slope_ref.coef_ref, bf16[8,128,384]{2,1,0:T(8,128)(2,1)} %copy-done.9, ...), custom_call_target="tpu_custom_call" | custom-call | flops 16099999744 | tf_op jit(solution)/shard_map/attn_fwd/pallas_call | solution.py:503
  66.1 6.0 %all-to-all-done.1.qkv_ref = bf16[8,128,384]{2,1,0:T(8,128)(2,1)S(1)} async-done(((bf16[8,128,384]{2,1,0:T(8,128)(2,1)}), bf16[8,128,384]{2,1,0:T(8,128)(2,1)S(1)}, u32[]{:S(2)}, u32[]{:S(2)}) %all-to-all-start.1) | async-done | bytes 786464 | tf_op jit(solution)/shard_map/all_to_all | solution.py:1087
  72.1 3.4 all-to-all-start.2
  75.5 15.0 %attn_fwd.3 = (f32[2048,64]{1,0:T(8,128)}, bf16[8,128,128]{2,1,0:T(8,128)(2,1)}, bf16[2,2048,128]{2,1,0:T(8,128)(2,1)}, bf16[2048,128]{1,0:T(8,128)(2,1)}, bf16[2048,128]{1,0:T(8,128)(2,1)}) custom-call(f32[2,7]{1,0:T(2,128)S(1)} %stack.114.slope_ref.coef_ref, bf16[8,128,384]{2,1,0:T(8,128)(2,1)} %copy-done.10, ...), custom_call_target="tpu_custom_call" | custom-call | flops 16099999744 | tf_op jit(solution)/shard_map/attn_fwd/pallas_call | solution.py:503
  90.5 14.8 %all_to_all.35.second_ref = bf16[8,128,128]{2,1,0:T(8,128)(2,1)} all-to-all(bf16[8,128,128]{2,1,0:T(8,128)(2,1)} %get-tuple-element.104), channel_id=1, replica_groups=mesh['dp'=4,'blk'=8] {'blk'}, dimensions={0} | all-to-all | bytes 524288 | tf_op jit(solution)/shard_map/all_to_all | solution.py:1087
  105.7 4.9 %attn_rows.1 = (bf16[256,1024]{1,0:T(8,128)(2,1)}, f32[256,1024]{1,0:T(8,128)}, f32[256,1]{1,0:T(8,128)}, bf16[256,1024]{1,0:T(8,128)(2,1)}, f32[256,1024]{1,0:T(8,128)}) custom-call(s32[2]{0:T(128)S(1)} %pad_add_fusion.1.ids_ref, bf16[8,128,128]{2,1,0:T(8,128)(2,1)} %copy-done.16, bf16[8,128,128]{2,1,0:T(8,128)(2,1)} %all_to_all.35.second_ref, ...), custom_call_target="tpu_custom_call" | custom-call | flops 5750000128 | tf_op jit(solution)/shard_map/attn_rows/pallas_call | solution.py:698
  111.1 1.7 collective-permute-done.nf_b
  112.8 0.8 copy-done.32
  113.6 13.2 %ffn.2 = (f32[256,1024]{1,0:T(8,128)}, f32[256,1024]{1,0:T(8,128)}, f32[256,1024]{1,0:T(8,128)}, f32[256,1024]{1,0:T(8,128)}, bf16[4,4,512,256]{3,2,1,0:T(8,128)(2,1)}) custom-call(s32[2]{0:T(128)S(1)} %pad_add_fusion.1.ids_ref, bf16[256,1024]{1,0:T(8,128)(2,1)} %get-tuple-element.106.nf_a, bf16[256,1024]{1,0:T(8,128)(2,1)} %copy-done.32, ...), custom_call_target="tpu_custom_call" | custom-call | flops 14949999616 | tf_op jit(solution)/shard_map/ffn/pallas_call | solution.py:761
  127.0 13.3 %ffn.3 = (f32[256,1024]{1,0:T(8,128)}, f32[256,1024]{1,0:T(8,128)}, f32[256,1024]{1,0:T(8,128)}, f32[256,1024]{1,0:T(8,128)}, bf16[4,4,512,256]{3,2,1,0:T(8,128)(2,1)}) custom-call(s32[2]{0:T(128)S(1)} %pad_add_fusion.1.ids_ref, bf16[256,1024]{1,0:T(8,128)(2,1)} %get-tuple-element.106.nf_a, bf16[256,1024]{1,0:T(8,128)(2,1)} %copy-done.32, ...), custom_call_target="tpu_custom_call" | custom-call | flops 14949999616 | tf_op jit(solution)/shard_map/ffn/pallas_call | solution.py:761
  140.2 1.2 copy-done.21
  142.3 1.8 collective-permute-done.3.came_b
  144.1 1.7 collective-permute-done.2.came_a
  145.8 1.0 copy-done.23
  146.8 6.0 %branch.1 = (f32[256,1024]{1,0:T(8,128)}, bf16[256,1024]{1,0:T(8,128)(2,1)}, bf16[8,256,128]{2,1,0:T(8,128)(2,1)}, f32[1,1024]{1,0:T(1,128)}) custom-call(s32[2]{0:T(128)S(1)} %pad_add_fusion.1.ids_ref, f32[256,1024]{1,0:T(8,128)} %get-tuple-element.110.gnf_a, f32[256,1024]{1,0:T(8,128)} %copy-done.23, f32[256,1024]{1,0:T(8,128)} %get-tuple-element.112.gnf_b, ...), custom_call_target="tpu_custom_call" | custom-call | flops 6899999744 | tf_op jit(solution)/shard_map/branch/pallas_call | solution.py:805
  152.8 3.5 all-to-all-start.4
  156.3 1.1 pad_maximum_fusion
  157.9 13.7 %all-to-all-done.4 = bf16[8,256,128]{2,1,0:T(8,128)(2,1)S(1)} async-done(((bf16[8,256,128]{2,1,0:T(8,128)(2,1)}), bf16[8,256,128]{2,1,0:T(8,128)(2,1)S(1)}, u32[]{:S(2)}, u32[]{:S(2)}) %all-to-all-start.4) | async-done | bytes 524320 | tf_op jit(solution)/shard_map/all_to_all | solution.py:1087
  172.4 15.9 %attn_bwd.2.first_ref = bf16[8,128,384]{2,1,0:T(8,128)(2,1)} custom-call(f32[2,7]{1,0:T(2,128)S(1)} %stack.114.slope_ref.coef_ref, bf16[2048,128]{1,0:T(8,128)(2,1)} %bitcast.67, f32[2048,64]{1,0:T(8,128)} %get-tuple-element.123.o_ref, bf16[2,2048,128]{2,1,0:T(8,128)(2,1)} %get-tuple-element.124.qb_ref, bf16[2048,128]{1,0:T(8,128)(2,1)} %get-tuple-element.125.ka_ref, ...), custom_call_target="tpu_custom_call" | custom-call | flops 18400000000 | tf_op jit(solution)/shard_map/attn_bwd/pallas_call | solution.py:597
  188.3 1.2 constant_dynamic-slice_fusion.15
  189.6 3.8 all-to-all-start.5
  193.4 16.7 %attn_bwd.3.second_ref = bf16[8,128,384]{2,1,0:T(8,128)(2,1)} custom-call(f32[2,7]{1,0:T(2,128)S(1)} %stack.114.slope_ref.coef_ref, bf16[2048,128]{1,0:T(8,128)(2,1)} %bitcast.68, f32[2048,64]{1,0:T(8,128)} %get-tuple-element.132.o_ref, bf16[2,2048,128]{2,1,0:T(8,128)(2,1)} %get-tuple-element.133.qb_ref, bf16[2048,128]{1,0:T(8,128)(2,1)} %get-tuple-element.134.ka_ref, ...), custom_call_target="tpu_custom_call" | custom-call | flops 18400000000 | tf_op jit(solution)/shard_map/attn_bwd/pallas_call | solution.py:597
  210.1 2.9 collective-permute-done.6
  213.0 1.0 fusion.11
  214.1 8.9 %slab.1 = bf16[4,384,256]{2,1,0:T(8,128)(2,1)} custom-call(bf16[2048,1024]{1,0:T(8,128)(2,1)} %all-gather.6.cloned.1.call-done.left_ref, bf16[8,128,384]{2,1,0:T(8,128)(2,1)} %attn_bwd.2.first_ref, bf16[8,128,384]{2,1,0:T(8,128)(2,1)} %attn_bwd.3.second_ref), custom_call_target="tpu_custom_call" | custom-call | flops 10350000128 | tf_op jit(solution)/shard_map/slab/pallas_call | solution.py:636
  223.0 3.7 collective-permute-done.7
  226.7 1.7 fusion.7
  228.5 4.4 %all-to-all-start.6 = ((bf16[8,128,384]{2,1,0:T(8,128)(2,1)}), bf16[8,128,384]{2,1,0:T(8,128)(2,1)}, u32[]{:S(2)}, u32[]{:S(2)}) async-start(bf16[8,128,384]{2,1,0:T(8,128)(2,1)} %attn_bwd.3.second_ref), calls=%async_computation.6 | async-start | bytes 1572864 | tf_op jit(solution)/shard_map/all_to_all | solution.py:1087
  233.5 1.0 slice_bitcast_fusion
  234.5 7.4 %collective-permute-start.11 = (bf16[4,384,256]{2,1,0:T(8,128)(2,1)}, bf16[4,384,256]{2,1,0:T(8,128)(2,1)}, u32[]{:S(2)}, u32[]{:S(2)}) collective-permute-start(bf16[4,384,256]{2,1,0:T(8,128)(2,1)} %slab.1), channel_id=1, source_target_pairs={{0,0},{1,1},{2,10},{3,11},{4,20},{5,21},{6,30},{7,31},{8,8},{9,9},... | collective-permute-start | bytes 2359304 | tf_op jit(solution)/shard_map/ppermute | solution.py:1149
  241.9 4.6 %wgrad.2 = (bf16[4,128,256]{2,1,0:T(8,128)(2,1)}, bf16[4,128,256]{2,1,0:T(8,128)(2,1)}, bf16[4,128,256]{2,1,0:T(8,128)(2,1)}, bf16[4,128,256]{2,1,0:T(8,128)(2,1)}) custom-call(s32[2]{0:T(128)S(1)} %pad_add_fusion.1.ids_ref, bf16[256,1024]{1,0:T(8,128)(2,1)} %get-tuple-element.130.refs_0_, bf16[256,1024]{1,0:T(8,128)(2,1)} %get-tuple-element.189.refs_1_, ...), custom_call_target="tpu_custom_call" | custom-call | flops 6899999744 | tf_op jit(solution)/shard_map/wgrad/pallas_call | solution.py:853
  246.5 1.4 collective-permute-start.8
  247.9 1.2 collective-permute-start.9
  249.1 0.9 collective-permute-start.10
  250.2 3.8 all-to-all-done.6.second_ref
  254.0 7.8 %tail.1.refs_4_ = bf16[272,1024]{1,0:T(8,128)(2,1)} custom-call(s32[2]{0:T(128)S(1)} %pad_add_fusion.1.ids_ref, bf16[8,128,384]{2,1,0:T(8,128)(2,1)} %copy-done.8, bf16[8,128,384]{2,1,0:T(8,128)(2,1)} %all-to-all-done.6.second_ref, bf16[1024,1024]{1,0:T(8,128)(2,1)} %wq_ref.3, bf16[1024,1024]{1,0:T(8,128)(2,1)} %wk_ref.3, bf16[1024,1024]{1,0:T(8,128)(2,1)} %wv_ref.3, ...), custom_call_target="tpu_custom_call" | custom-call | flops 9200000000 | tf_op jit(solution)/shard_map/tail/pallas_call | solution.py:894
  262.4 1.3 constant_dynamic-slice_fusion.3
  264.0 7.9 %collective-permute-start.12 = (bf16[2,1024,256]{2,1,0:T(8,128)(2,1)S(1)}, bf16[2,1024,256]{2,1,0:T(8,128)(2,1)S(1)}, u32[]{:S(2)}, u32[]{:S(2)}) collective-permute-start(bf16[2,1024,256]{2,1,0:T(8,128)(2,1)S(1)} %maximum_maximum_fusion.1), channel_id=1, source_target_pairs={{0,2},{1,3},{2,0},{3,1},{4,6},{5,7},{6,4},{7,5},{8,10},{9,11},{10,... | collective-permute-start | bytes 3145736 | tf_op jit(solution)/shard_map/ppermute | solution.py:947
  273.6 6.0 %wgrad.3 = (bf16[4,272,256]{2,1,0:T(8,128)(2,1)}, bf16[4,272,256]{2,1,0:T(8,128)(2,1)}, bf16[4,272,256]{2,1,0:T(8,128)(2,1)}, bf16[4,272,256]{2,1,0:T(8,128)(2,1)}) custom-call(s32[2]{0:T(128)S(1)} %pad_add_fusion.1.ids_ref, bf16[256,1024]{1,0:T(8,128)(2,1)} %refs_0_.1, bf16[256,1024]{1,0:T(8,128)(2,1)} %collective-permute-done.13.refs_1_, ...), custom_call_target="tpu_custom_call" | custom-call | flops 6899999744 | tf_op jit(solution)/shard_map/wgrad/pallas_call | solution.py:853
  279.5 1.1 collective-permute-start.16
  280.6 0.9 collective-permute-start.17
  281.5 1.5 collective-permute-start.18
  283.0 14.6 %collective-permute-done.12 = bf16[2,1024,256]{2,1,0:T(8,128)(2,1)S(1)} collective-permute-done((bf16[2,1024,256]{2,1,0:T(8,128)(2,1)S(1)}, bf16[2,1024,256]{2,1,0:T(8,128)(2,1)S(1)}, u32[]{:S(2)}, u32[]{:S(2)}) %collective-permute-start.12) | collective-permute-done | bytes 1048608 | tf_op jit(solution)/shard_map/ppermute | solution.py:947
  297.7 2.5 collective-permute-start.21
  300.2 2.3 fusion.8
  302.5 3.8 collective-permute-done.17
  307.0 17.4 %collective-permute-done.19 = bf16[2,272,256]{2,1,0:T(8,128)(2,1)S(1)} collective-permute-done((bf16[2,272,256]{2,1,0:T(8,128)(2,1)S(1)}, bf16[2,272,256]{2,1,0:T(8,128)(2,1)S(1)}, u32[]{:S(2)}, u32[]{:S(2)}) %collective-permute-start.19) | collective-permute-done | bytes 278560 | tf_op jit(solution)/shard_map/ppermute | solution.py:947
  324.5 1.0 fusion.4
  325.8 0.9 collective-permute-start.20
  326.7 9.1 %collective-permute-done.20 = bf16[272,256]{1,0:T(8,128)(2,1)S(1)} collective-permute-done((bf16[272,256]{1,0:T(8,128)(2,1)S(1)}, bf16[272,256]{1,0:T(8,128)(2,1)S(1)}, u32[]{:S(2)}, u32[]{:S(2)}) %collective-permute-start.20) | collective-permute-done | bytes 139296 | tf_op jit(solution)/shard_map/ppermute | solution.py:952
  335.9 18.1 %collective-permute-done.22 = bf16[272,256]{1,0:T(8,128)(2,1)S(1)} collective-permute-done((bf16[272,256]{1,0:T(8,128)(2,1)S(1)}, bf16[272,256]{1,0:T(8,128)(2,1)S(1)}, u32[]{:S(2)}, u32[]{:S(2)}) %collective-permute-start.22) | collective-permute-done | bytes 139296 | tf_op jit(solution)/shard_map/ppermute | solution.py:956
  354.2 24.6 %collective-permute-done.23 = bf16[2,272,256]{2,1,0:T(8,128)(2,1)S(1)} collective-permute-done((bf16[2,272,256]{2,1,0:T(8,128)(2,1)S(1)}, bf16[2,272,256]{2,1,0:T(8,128)(2,1)S(1)}, u32[]{:S(2)}, u32[]{:S(2)}) %collective-permute-start.23) | collective-permute-done | bytes 278560 | tf_op jit(solution)/shard_map/ppermute | solution.py:957
  379.0 1.2 add_convert_fusion.3
  380.3 1.0 fusion.18
  381.3 0.8 copy-done.26
  382.1 4.2 %skip.1 = (f32[2,4,2,128,256]{4,3,2,1,0:T(8,128)}, f32[16,256]{1,0:T(8,128)}) custom-call(s32[2]{0:T(128)S(1)} %pad_add_fusion.2.at_ref, bf16[4,272,256]{2,1,0:T(8,128)(2,1)} %copy-done.12, bf16[4,272,256]{2,1,0:T(8,128)(2,1)} %copy-done.26), custom_call_target="tpu_custom_call" | custom-call | flops 4600000000 | tf_op jit(solution)/shard_map/skip/pallas_call | solution.py:1036
  386.4 1.3 fusion.19
  387.7 9.2 %assemble.1 = (f32[4,2,2,256,256]{4,3,2,1,0:T(8,128)}, f32[1024,1024]{1,0:T(8,128)}, f32[1024,256]{1,0:T(8,128)}, f32[1024,256]{1,0:T(8,128)}, f32[1024,256]{1,0:T(8,128)}, /*index=5*/f32[1024,256]{1,0:T(8,128)}) custom-call(bf16[8,512,256]{2,1,0:T(8,128)(2,1)} %bitcast.75, bf16[8,1024,256]{2,1,0:T(8,128)(2,1)} %bitcast.74), custom_call_target="tpu_custom_call" | custom-call | flops 10350000128 | tf_op jit(solution)/shard_map/assemble/pallas_call | solution.py:989
  (139 shorter events, 9.3 us)
Async XLA Ops:
  12.8 14.5 %copy-start.18 = (s32[1,4]{1,0:T(1,128)S(1)}, s32[1,4]{1,0:T(1,128)}, u32[]{:S(2)}) copy-start(s32[1,4]{1,0:T(1,128)} %param.27) | copy-start | bytes 52
  12.8 14.8 %copy-start.17 = (s32[1,4]{1,0:T(1,128)S(1)}, s32[1,4]{1,0:T(1,128)}, u32[]{:S(2)}) copy-start(s32[1,4]{1,0:T(1,128)} %param.26) | copy-start | bytes 52
  20.3 27.3 %all-to-all-start = ((bf16[8,128,384]{2,1,0:T(8,128)(2,1)}), bf16[8,128,384]{2,1,0:T(8,128)(2,1)S(1)}, u32[]{:S(2)}, u32[]{:S(2)}) async-start(bf16[8,128,384]{2,1,0:T(8,128)(2,1)} %get-tuple-element.95), calls=%async_computation | async-start | bytes 1572864 | tf_op jit(solution)/shard_map/all_to_all | solution.py:1087
  47.6 3.6 copy-start.9
  47.6 24.5 %all-to-all-start.1 = ((bf16[8,128,384]{2,1,0:T(8,128)(2,1)}), bf16[8,128,384]{2,1,0:T(8,128)(2,1)S(1)}, u32[]{:S(2)}, u32[]{:S(2)}) async-start(bf16[8,128,384]{2,1,0:T(8,128)(2,1)} %get-tuple-element.100), calls=%async_computation.1 | async-start | bytes 1572864 | tf_op jit(solution)/shard_map/all_to_all | solution.py:1087
  72.1 3.5 copy-start.10
  72.1 18.5 %all-to-all-start.2 = ((bf16[8,128,128]{2,1,0:T(8,128)(2,1)}), bf16[8,128,128]{2,1,0:T(8,128)(2,1)S(1)}, u32[]{:S(2)}, u32[]{:S(2)}) async-start(bf16[8,128,128]{2,1,0:T(8,128)(2,1)} %get-tuple-element.102), calls=%async_computation.2 | async-start | bytes 524288 | tf_op jit(solution)/shard_map/all_to_all | solution.py:1087
  75.5 30.1 %copy-start.27 = (bf16[256,1024]{1,0:T(8,128)(2,1)S(1)}, bf16[256,1024]{1,0:T(8,128)(2,1)}, u32[]{:S(2)}) copy-start(bf16[256,1024]{1,0:T(8,128)(2,1)} %cot_ref.1) | copy-start | bytes 1572868
  75.5 77.3 %all-gather.6.cloned.1.call-start = ((), (), s32[]{:S(2)}) async-start(), calls=%async_computation.9 | async-start | bytes 4718592 | tf_op jit(solution)/shard_map/all_gather | solution.py:1102
  90.5 15.2 %copy-start.16 = (bf16[8,128,128]{2,1,0:T(8,128)(2,1)}, bf16[8,128,128]{2,1,0:T(8,128)(2,1)S(1)}, u32[]{:S(2)}) copy-start(bf16[8,128,128]{2,1,0:T(8,128)(2,1)S(1)} %all-to-all-done.2.first_ref) | copy-start | bytes 786436
  105.4 82.9 %reduce-scatter.7.cloned.1.call-start = ((), (), s32[]{:S(2)}) async-start(), calls=%async_computation.12 | async-start | bytes 5242880
  105.6 5.5 %collective-permute-start.1 = (bf16[256,1024]{1,0:T(8,128)(2,1)S(1)}, bf16[256,1024]{1,0:T(8,128)(2,1)S(1)}, u32[]{:S(2)}, u32[]{:S(2)}) collective-permute-start(bf16[256,1024]{1,0:T(8,128)(2,1)S(1)} %copy-done.27), channel_id=1, source_target_pairs={{0,1},{1,0},{2,3},{3,2},{4,5},{5,4},{6,7},{7,6},{8,9},{9,8},{10,11... | collective-permute-start | bytes 1572872 | tf_op jit(solution)/shard_map/ppermute | solution.py:927
  110.6 2.2 collective-permute-start
  111.1 1.7 copy-start.31
  126.9 115.0 %reduce-scatter.9.cloned.1.call-start = ((), (), s32[]{:S(2)}) async-start(), calls=%async_computation.13 | async-start | bytes 5242880
  140.2 1.2 copy-start.21
  140.2 1.6 copy-start.20
  141.4 2.7 collective-permute-start.3
  141.8 4.0 collective-permute-start.2
  144.1 1.7 copy-start.22
  145.8 1.0 copy-start.23
  146.8 9.5 %copy-start.14 = (bf16[256,1024]{1,0:T(8,128)(2,1)S(1)}, bf16[256,1024]{1,0:T(8,128)(2,1)}, u32[]{:S(2)}) copy-start(bf16[256,1024]{1,0:T(8,128)(2,1)} %get-tuple-element.130.refs_0_) | copy-start | bytes 1572868
  152.8 18.8 %all-to-all-start.4 = ((bf16[8,256,128]{2,1,0:T(8,128)(2,1)}), bf16[8,256,128]{2,1,0:T(8,128)(2,1)S(1)}, u32[]{:S(2)}, u32[]{:S(2)}) async-start(bf16[8,256,128]{2,1,0:T(8,128)(2,1)} %get-tuple-element.122), calls=%async_computation.4 | async-start | bytes 1048576 | tf_op jit(solution)/shard_map/all_to_all | solution.py:1087
  157.5 76.0 %collective-permute-start.5 = (bf16[2,256,1024]{2,1,0:T(8,128)(2,1)S(1)}, bf16[2,256,1024]{2,1,0:T(8,128)(2,1)S(1)}, u32[]{:S(2)}, u32[]{:S(2)}) collective-permute-start(bf16[2,256,1024]{2,1,0:T(8,128)(2,1)S(1)} %pad_maximum_fusion), channel_id=1, source_target_pairs={{0,1},{1,0},{2,3},{3,2},{4,5},{5,4},{6,7},{7,6},{8,9},{9,8},{10,11... | collective-permute-start | bytes 3145736 | tf_op jit(solution)/shard_map/ppermute | solution.py:927
  189.5 23.5 %collective-permute-start.6 = (bf16[2,512,256]{2,1,0:T(8,128)(2,1)S(1)}, bf16[2,512,256]{2,1,0:T(8,128)(2,1)}, u32[]{:S(2)}, u32[]{:S(2)}) collective-permute-start(bf16[2,512,256]{2,1,0:T(8,128)(2,1)S(1)} %pad_maximum_fusion.2), channel_id=1, source_target_pairs={{0,2},{1,3},{2,0},{3,1},{4,6},{5,7},{6,4},{7,5},{8,10},{9,11},{10,... | collective-permute-start | bytes 1572872 | tf_op jit(solution)/shard_map/ppermute | solution.py:947
  189.6 38.9 %all-to-all-start.5 = ((bf16[8,128,384]{2,1,0:T(8,128)(2,1)}), bf16[8,128,384]{2,1,0:T(8,128)(2,1)S(1)}, u32[]{:S(2)}, u32[]{:S(2)}) async-start(bf16[8,128,384]{2,1,0:T(8,128)(2,1)} %attn_bwd.2.first_ref), calls=%async_computation.5 | async-start | bytes 1572864 | tf_op jit(solution)/shard_map/all_to_all | solution.py:1087
  193.4 19.6 %copy-start.4 = (bf16[1,4,512,256]{3,2,1,0:T(8,128)(2,1)S(1)}, bf16[1,4,512,256]{3,2,1,0:T(8,128)(2,1)}, u32[]{:S(2)}) copy-start(bf16[1,4,512,256]{3,2,1,0:T(8,128)(2,1)} %reduce-scatter.7.cloned.1.call-done) | copy-start | bytes 3145732
  214.0 12.7 %collective-permute-start.7 = (bf16[512,256]{1,0:T(8,128)(2,1)S(1)}, bf16[512,256]{1,0:T(8,128)(2,1)S(1)}, u32[]{:S(2)}, u32[]{:S(2)}) collective-permute-start(bf16[512,256]{1,0:T(8,128)(2,1)S(1)} %fusion.11), channel_id=1, source_target_pairs={{0,4},{1,5},{2,6},{3,7},{4,0},{5,1},{6,2},{7,3},{8,12},{9,13},{10,... | collective-permute-start | bytes 786440 | tf_op jit(solution)/shard_map/ppermute | solution.py:952
  223.0 9.9 %copy-start.29 = (bf16[256,1024]{1,0:T(8,128)(2,1)S(1)}, bf16[256,1024]{1,0:T(8,128)(2,1)}, u32[]{:S(2)}) copy-start(bf16[256,1024]{1,0:T(8,128)(2,1)} %refs_0_.1) | copy-start | bytes 1572868
  228.5 18.1 %copy-start.8 = (bf16[8,128,384]{2,1,0:T(8,128)(2,1)}, bf16[8,128,384]{2,1,0:T(8,128)(2,1)S(1)}, u32[]{:S(2)}) copy-start(bf16[8,128,384]{2,1,0:T(8,128)(2,1)S(1)} %all-to-all-done.5.first_ref) | copy-start | bytes 2359300
  228.5 25.5 %all-to-all-start.6 = ((bf16[8,128,384]{2,1,0:T(8,128)(2,1)}), bf16[8,128,384]{2,1,0:T(8,128)(2,1)}, u32[]{:S(2)}, u32[]{:S(2)}) async-start(bf16[8,128,384]{2,1,0:T(8,128)(2,1)} %attn_bwd.3.second_ref), calls=%async_computation.6 | async-start | bytes 1572864 | tf_op jit(solution)/shard_map/all_to_all | solution.py:1087
  232.9 154.8 %all-gather.8.cloned.1.call-start = ((), (), s32[]{:S(2)}) async-start(), calls=%async_computation.10 | async-start | bytes 2359296 | tf_op jit(solution)/shard_map/all_gather | solution.py:1147
  232.9 39.0 %collective-permute-start.13 = (bf16[256,1024]{1,0:T(8,128)(2,1)S(1)}, bf16[256,1024]{1,0:T(8,128)(2,1)}, u32[]{:S(2)}, u32[]{:S(2)}) collective-permute-start(bf16[256,1024]{1,0:T(8,128)(2,1)S(1)} %copy-done.29), channel_id=1, source_target_pairs={{0,1},{1,0},{2,3},{3,2},{4,5},{5,4},{6,7},{7,6},{8,9},{9,8},{10,11... | collective-permute-start | bytes 1572872 | tf_op jit(solution)/shard_map/ppermute | solution.py:927
  234.5 27.9 %collective-permute-start.11 = (bf16[4,384,256]{2,1,0:T(8,128)(2,1)}, bf16[4,384,256]{2,1,0:T(8,128)(2,1)}, u32[]{:S(2)}, u32[]{:S(2)}) collective-permute-start(bf16[4,384,256]{2,1,0:T(8,128)(2,1)} %slab.1), channel_id=1, source_target_pairs={{0,0},{1,1},{2,10},{3,11},{4,20},{5,21},{6,30},{7,31},{8,8},{9,9},... | collective-permute-start | bytes 2359304 | tf_op jit(solution)/shard_map/ppermute | solution.py:1149
  241.9 8.1 %copy-start.2 = (bf16[1,4,512,256]{3,2,1,0:T(8,128)(2,1)S(1)}, bf16[1,4,512,256]{3,2,1,0:T(8,128)(2,1)}, u32[]{:S(2)}) copy-start(bf16[1,4,512,256]{3,2,1,0:T(8,128)(2,1)} %reduce-scatter.9.cloned.1.call-done) | copy-start | bytes 3145732
  246.5 15.3 %collective-permute-start.8 = (bf16[4,128,256]{2,1,0:T(8,128)(2,1)}, bf16[4,128,256]{2,1,0:T(8,128)(2,1)S(1)}, u32[]{:S(2)}, u32[]{:S(2)}) collective-permute-start(bf16[4,128,256]{2,1,0:T(8,128)(2,1)} %get-tuple-element.140), channel_id=1, source_target_pairs={{0,8},{8,0},{16,24},{24,16},{1,9},{9,1},{17,25},{25,17},{2,10},{10... | collective-permute-start | bytes 786440 | tf_op jit(solution)/shard_map/ppermute | solution.py:931
  247.9 14.0 %collective-permute-start.9 = (bf16[4,128,256]{2,1,0:T(8,128)(2,1)}, bf16[4,128,256]{2,1,0:T(8,128)(2,1)S(1)}, u32[]{:S(2)}, u32[]{:S(2)}) collective-permute-start(bf16[4,128,256]{2,1,0:T(8,128)(2,1)} %get-tuple-element.141), channel_id=1, source_target_pairs={{0,16},{8,24},{16,0},{24,8},{1,17},{9,25},{17,1},{25,9},{2,18},{10... | collective-permute-start | bytes 786440 | tf_op jit(solution)/shard_map/ppermute | solution.py:931
  249.1 13.3 %collective-permute-start.10 = (bf16[4,128,256]{2,1,0:T(8,128)(2,1)}, bf16[4,128,256]{2,1,0:T(8,128)(2,1)S(1)}, u32[]{:S(2)}, u32[]{:S(2)}) collective-permute-start(bf16[4,128,256]{2,1,0:T(8,128)(2,1)} %get-tuple-element.142), channel_id=1, source_target_pairs={{0,24},{8,16},{16,8},{24,0},{1,25},{9,17},{17,9},{25,1},{2,26},{10... | collective-permute-start | bytes 786440 | tf_op jit(solution)/shard_map/ppermute | solution.py:931
  250.1 137.6 %all-gather.10.cloned.1.call-start = ((), (), s32[]{:S(2)}) async-start(), calls=%async_computation.11 | async-start | bytes 4718592 | tf_op jit(solution)/shard_map/all_gather | solution.py:1179
  254.0 7.8 %copy-start.28 = (bf16[256,1024]{1,0:T(8,128)(2,1)S(1)}, bf16[256,1024]{1,0:T(8,128)(2,1)}, u32[]{:S(2)}) copy-start(bf16[256,1024]{1,0:T(8,128)(2,1)} %refs_2_.1) | copy-start | bytes 1572868
  254.0 9.7 %copy-start.15 = (bf16[4,128,256]{2,1,0:T(8,128)(2,1)S(1)}, bf16[4,128,256]{2,1,0:T(8,128)(2,1)}, u32[]{:S(2)}) copy-start(bf16[4,128,256]{2,1,0:T(8,128)(2,1)} %get-tuple-element.139) | copy-start | bytes 786436
  261.8 10.1 %collective-permute-start.14 = (bf16[256,1024]{1,0:T(8,128)(2,1)S(1)}, bf16[256,1024]{1,0:T(8,128)(2,1)S(1)}, u32[]{:S(2)}, u32[]{:S(2)}) collective-permute-start(bf16[256,1024]{1,0:T(8,128)(2,1)S(1)} %copy-done.28), channel_id=1, source_target_pairs={{0,1},{1,0},{2,3},{3,2},{4,5},{5,4},{6,7},{7,6},{8,9},{9,8},{10,11... | collective-permute-start | bytes 1572872 | tf_op jit(solution)/shard_map/ppermute | solution.py:927
  261.9 10.1 %collective-permute-start.15 = (bf16[272,1024]{1,0:T(8,128)(2,1)}, bf16[272,1024]{1,0:T(8,128)(2,1)S(1)}, u32[]{:S(2)}, u32[]{:S(2)}) collective-permute-start(bf16[272,1024]{1,0:T(8,128)(2,1)} %tail.1.refs_4_), channel_id=1, source_target_pairs={{0,1},{1,0},{2,3},{3,2},{4,5},{5,4},{6,7},{7,6},{8,9},{9,8},{10,11... | collective-permute-start | bytes 1671176 | tf_op jit(solution)/shard_map/ppermute | solution.py:927
  264.0 33.6 %collective-permute-start.12 = (bf16[2,1024,256]{2,1,0:T(8,128)(2,1)S(1)}, bf16[2,1024,256]{2,1,0:T(8,128)(2,1)S(1)}, u32[]{:S(2)}, u32[]{:S(2)}) collective-permute-start(bf16[2,1024,256]{2,1,0:T(8,128)(2,1)S(1)} %maximum_maximum_fusion.1), channel_id=1, source_target_pairs={{0,2},{1,3},{2,0},{3,1},{4,6},{5,7},{6,4},{7,5},{8,10},{9,11},{10,... | collective-permute-start | bytes 3145736 | tf_op jit(solution)/shard_map/ppermute | solution.py:947
  271.9 28.3 %copy-start.19 = (bf16[2048,1024]{1,0:T(8,128)(2,1)S(1)}, bf16[2048,1024]{1,0:T(8,128)(2,1)}, u32[]{:S(2)}) copy-start(bf16[2048,1024]{1,0:T(8,128)(2,1)} %param.16) | copy-start | bytes 12582916
  271.9 28.3 %copy-start.24 = (bf16[272,1024]{1,0:T(8,128)(2,1)S(1)}, bf16[272,1024]{1,0:T(8,128)(2,1)}, u32[]{:S(2)}) copy-start(bf16[272,1024]{1,0:T(8,128)(2,1)} %tail.1.refs_4_) | copy-start | bytes 1671172
  279.5 22.9 %collective-permute-start.16 = (bf16[4,272,256]{2,1,0:T(8,128)(2,1)}, bf16[4,272,256]{2,1,0:T(8,128)(2,1)S(1)}, u32[]{:S(2)}, u32[]{:S(2)}) collective-permute-start(bf16[4,272,256]{2,1,0:T(8,128)(2,1)} %get-tuple-element.159), channel_id=1, source_target_pairs={{0,8},{8,0},{16,24},{24,16},{1,9},{9,1},{17,25},{25,17},{2,10},{10... | collective-permute-start | bytes 1671176 | tf_op jit(solution)/shard_map/ppermute | solution.py:931
  280.6 25.7 %collective-permute-start.17 = (bf16[4,272,256]{2,1,0:T(8,128)(2,1)}, bf16[4,272,256]{2,1,0:T(8,128)(2,1)S(1)}, u32[]{:S(2)}, u32[]{:S(2)}) collective-permute-start(bf16[4,272,256]{2,1,0:T(8,128)(2,1)} %get-tuple-element.160), channel_id=1, source_target_pairs={{0,16},{8,24},{16,0},{24,8},{1,17},{9,25},{17,1},{25,9},{2,18},{10... | collective-permute-start | bytes 1671176 | tf_op jit(solution)/shard_map/ppermute | solution.py:931
  281.5 24.8 %collective-permute-start.18 = (bf16[4,272,256]{2,1,0:T(8,128)(2,1)}, bf16[4,272,256]{2,1,0:T(8,128)(2,1)S(1)}, u32[]{:S(2)}, u32[]{:S(2)}) collective-permute-start(bf16[4,272,256]{2,1,0:T(8,128)(2,1)} %get-tuple-element.161), channel_id=1, source_target_pairs={{0,24},{8,16},{16,8},{24,0},{1,25},{9,17},{17,9},{25,1},{2,26},{10... | collective-permute-start | bytes 1671176 | tf_op jit(solution)/shard_map/ppermute | solution.py:931
  297.7 8.6 %copy-start.11 = (bf16[4,272,256]{2,1,0:T(8,128)(2,1)S(1)}, bf16[4,272,256]{2,1,0:T(8,128)(2,1)}, u32[]{:S(2)}) copy-start(bf16[4,272,256]{2,1,0:T(8,128)(2,1)} %get-tuple-element.158) | copy-start | bytes 1671172
  297.7 26.8 %collective-permute-start.21 = (bf16[1024,256]{1,0:T(8,128)(2,1)S(1)}, bf16[1024,256]{1,0:T(8,128)(2,1)S(1)}, u32[]{:S(2)}, u32[]{:S(2)}) collective-permute-start(bf16[1024,256]{1,0:T(8,128)(2,1)S(1)} %fusion.5), channel_id=1, source_target_pairs={{0,4},{1,5},{2,6},{3,7},{4,0},{5,1},{6,2},{7,3},{8,12},{9,13},{10,... | collective-permute-start | bytes 1572872 | tf_op jit(solution)/shard_map/ppermute | solution.py:952
  306.6 18.9 %copy-start = (f32[256,1024]{1,0:T(8,128)S(1)}, f32[256,1024]{1,0:T(8,128)}, u32[]{:S(2)}) copy-start(f32[256,1024]{1,0:T(8,128)} %get-tuple-element.117) | copy-start | bytes 3145732
  306.6 18.9 %copy-start.1 = (f32[256,1024]{1,0:T(8,128)S(1)}, f32[256,1024]{1,0:T(8,128)}, u32[]{:S(2)}) copy-start(f32[256,1024]{1,0:T(8,128)} %get-tuple-element.118) | copy-start | bytes 3145732
  306.7 17.7 %collective-permute-start.19 = (bf16[2,272,256]{2,1,0:T(8,128)(2,1)S(1)}, bf16[2,272,256]{2,1,0:T(8,128)(2,1)S(1)}, u32[]{:S(2)}, u32[]{:S(2)}) collective-permute-start(bf16[2,272,256]{2,1,0:T(8,128)(2,1)S(1)} %pad_maximum_fusion.3), channel_id=1, source_target_pairs={{0,2},{1,3},{2,0},{3,1},{4,6},{5,7},{6,4},{7,5},{8,10},{9,11},{10,... | collective-permute-start | bytes 835592 | tf_op jit(solution)/shard_map/ppermute | solution.py:947
  325.5 53.4 %copy-start.5 = (f32[256,1024]{1,0:T(8,128)S(1)}, f32[256,1024]{1,0:T(8,128)}, u32[]{:S(2)}) copy-start(f32[256,1024]{1,0:T(8,128)} %get-tuple-element.105) | copy-start | bytes 3145732
  325.5 53.4 %copy-start.6 = (f32[256,1024]{1,0:T(8,128)S(1)}, f32[256,1024]{1,0:T(8,128)}, u32[]{:S(2)}) copy-start(f32[256,1024]{1,0:T(8,128)} %get-tuple-element.107) | copy-start | bytes 3145732
  325.5 53.4 %copy-start.7 = (f32[256,1024]{1,0:T(8,128)S(1)}, f32[256,1024]{1,0:T(8,128)}, u32[]{:S(2)}) copy-start(f32[256,1024]{1,0:T(8,128)} %get-tuple-element.108) | copy-start | bytes 3145732
  325.7 53.2 %collective-permute-start.4 = (f32[256,1024]{1,0:T(8,128)S(1)}, f32[256,1024]{1,0:T(8,128)S(1)}, u32[]{:S(2)}, u32[]{:S(2)}) collective-permute-start(f32[256,1024]{1,0:T(8,128)S(1)} %add.125), channel_id=1, source_target_pairs={{0,1},{1,0},{2,3},{3,2},{4,5},{5,4},{6,7},{7,6},{8,9},{9,8},{10,11... | collective-permute-start | bytes 3145736 | tf_op jit(solution)/shard_map/ppermute | solution.py:927
  325.8 10.0 %collective-permute-start.20 = (bf16[272,256]{1,0:T(8,128)(2,1)S(1)}, bf16[272,256]{1,0:T(8,128)(2,1)S(1)}, u32[]{:S(2)}, u32[]{:S(2)}) collective-permute-start(bf16[272,256]{1,0:T(8,128)(2,1)S(1)} %fusion.14), channel_id=1, source_target_pairs={{0,4},{1,5},{2,6},{3,7},{4,0},{5,1},{6,2},{7,3},{8,12},{9,13},{10,... | collective-permute-start | bytes 417800 | tf_op jit(solution)/shard_map/ppermute | solution.py:952
  335.9 18.1 %collective-permute-start.22 = (bf16[272,256]{1,0:T(8,128)(2,1)S(1)}, bf16[272,256]{1,0:T(8,128)(2,1)S(1)}, u32[]{:S(2)}, u32[]{:S(2)}) collective-permute-start(bf16[272,256]{1,0:T(8,128)(2,1)S(1)} %fusion.10), channel_id=1, source_target_pairs={{0,4},{1,5},{2,6},{3,7},{4,0},{5,1},{6,2},{7,3},{8,12},{9,13},{10,... | collective-permute-start | bytes 417800 | tf_op jit(solution)/shard_map/ppermute | solution.py:956
  354.0 24.7 %collective-permute-start.23 = (bf16[2,272,256]{2,1,0:T(8,128)(2,1)S(1)}, bf16[2,272,256]{2,1,0:T(8,128)(2,1)S(1)}, u32[]{:S(2)}, u32[]{:S(2)}) collective-permute-start(bf16[2,272,256]{2,1,0:T(8,128)(2,1)S(1)} %pad_maximum_fusion.4), channel_id=1, source_target_pairs={{0,2},{1,3},{2,0},{3,1},{4,6},{5,7},{6,4},{7,5},{8,10},{9,11},{10,... | collective-permute-start | bytes 835592 | tf_op jit(solution)/shard_map/ppermute | solution.py:957
  378.8 1.3 copy-start.12
  378.8 2.5 collective-permute-start.24
  378.9 1.3 copy-start.3
  (5 other events, 4.0 us)
Sparse Core Ops, SparseCore 0:
  105.5 46.0 all-gather.5
  250.2 27.5 all-gather.7
  325.6 53.8 all-gather.9
Sparse Core Ops, SparseCore 1:
  127.0 51.8 reduce-scatter.6
  182.5 52.5 reduce-scatter.8
